TPU v7x, 128 devices: a whole 4x4x4 slice. The times are simulated.
128 devices in a mesh: ctx: 8 (over y_lo, z), comp: 8 (over y_hi, x), grp: 2 (over core).
Axes of the slice: x: 4, y: 4 (y_hi: 2, y_lo: 2; y = y_hi * 2 + y_lo), z: 4, core: 2. Of those that a mesh axis runs over, the one named last changes fastest.
Arguments:
- prompt_query: bfloat16 [2, 4096, 1024], P('grp', 'ctx', 'comp'), may hold values from -64 to 64
- prompt_cache: bfloat16 [2, 4096, 256], P('grp', 'ctx'), may hold values from -6 to 6
- prompt_cotangent: bfloat16 [2, 4096, 1024], P('grp', 'ctx', 'comp'), may hold values from -3 to 3
- reply_query: bfloat16 [16384, 1024], P(('comp', 'grp'), 'ctx'), may hold values from -64 to 64
- reply_cache: bfloat16 [16384, 256], P(('comp', 'grp')), may hold values from -6 to 6
- reply_cotangent: bfloat16 [16384, 1024], P(('comp', 'grp'), 'ctx'), may hold values from -3 to 3
- reply_lengths: int32 [16, 4], P(('comp', 'grp')), may hold values from 0 to 512, as said below
- reply_owner: int32 [16, 4], P(('comp', 'grp')), may hold values from 0 to 1
Outputs:
- prompt_output: bfloat16 [2, 4096, 1024], P('grp', 'ctx', 'comp')
- prompt_query_grad: bfloat16 [2, 4096, 1024], P('grp', 'ctx', 'comp')
- prompt_cache_grad: bfloat16 [2, 4096, 256], P(None, ('ctx', 'comp', 'grp'))
- reply_output: bfloat16 [16384, 1024], P(('comp', 'grp'), 'ctx')
- reply_query_grad: bfloat16 [16384, 1024], P(('comp', 'grp'), 'ctx')
- reply_cache_grad: bfloat16 [16384, 256], P(('comp', 'grp'))
Inputs may be any that keep to these rules, and one draw needn't show every extreme that they name: `reply_lengths`: each row sums to at most 1024; some row sums to exactly 1024 and holds a completion of exactly 512 tokens; zeros mark unused slots.
All inputs are finite; a program needn't handle non-finite values.
Results may differ from a plain program's by a relative error of at most 0.03.
Values may be sent and summed in bfloat16 or wider, within the bound.
No kernel may reach another device: no remote copies, remote signals or barrier semaphores. Data moves between devices by JAX's collectives and lax.ppermute only.
A program may use at most 128 MiB of HBM per device.

v0:
```python
import jax
import jax.numpy as jnp
from jax import lax
from jax.sharding import PartitionSpec as P

MASKED = -1e30


def head_scores(query_heads, key_rows, allowed, scaling):
    scores = (
        jnp.einsum("rhd,kd->hrk", query_heads, key_rows, preferred_element_type=jnp.float32)
        * scaling
    )
    return jnp.where(allowed[None, :, :], scores, MASKED)


def backward_core(query_heads, grad_heads, key_rows, value_rows, weights, attended, scaling):
    rounded = weights.astype(jnp.bfloat16)
    row_dot = jnp.einsum(
        "rhd,rhd->hr", grad_heads.astype(jnp.float32), attended.astype(jnp.float32)
    )
    weight_grad = jnp.einsum(
        "rhd,kd->hrk", grad_heads, value_rows, preferred_element_type=jnp.float32
    )
    score_grad = (weights * (weight_grad - row_dot[:, :, None])).astype(jnp.bfloat16)
    query_grad = (
        jnp.einsum("hrk,kd->rhd", score_grad, key_rows, preferred_element_type=jnp.float32)
        * scaling
    ).astype(jnp.bfloat16)
    key_grad = (
        jnp.einsum("hrk,rhd->kd", score_grad, query_heads, preferred_element_type=jnp.float32)
        * scaling
    )
    value_grad = jnp.einsum("hrk,rhd->kd", rounded, grad_heads, preferred_element_type=jnp.float32)
    return (query_grad, jnp.concatenate([key_grad, value_grad], axis=1))


def full_pass(query_heads, grad_heads, key_rows, value_rows, allowed, usable, scaling):
    scores = head_scores(query_heads, key_rows, allowed, scaling)
    highest = jnp.max(scores, axis=2, keepdims=True)
    log_total = highest + jnp.log(jnp.sum(jnp.exp(scores - highest), axis=2, keepdims=True))
    weights = jnp.exp(scores - log_total)
    result = jnp.einsum(
        "hrk,kd->rhd", weights.astype(jnp.bfloat16), value_rows, preferred_element_type=jnp.float32
    )
    attended = jnp.where(usable[:, None, None], result, 0.0).astype(jnp.bfloat16)
    query_grad, stacked_grad = backward_core(
        query_heads, grad_heads, key_rows, value_rows, weights, attended, scaling
    )
    return (attended, query_grad, stacked_grad)


def per_device(
    prompt_query,
    prompt_cache,
    prompt_cotangent,
    reply_query,
    reply_cache,
    reply_cotangent,
    reply_lengths,
    reply_owner,
):
    head_size = prompt_cache.shape[2] // 2
    scaling = head_size ** (-0.5)
    row_count = prompt_query.shape[1]
    ctx_count = lax.axis_size("ctx")
    group_count = lax.axis_size("grp")
    ctx_place = lax.axis_index("ctx")
    group_place = lax.axis_index("grp")
    full_length = row_count * ctx_count
    query_heads = prompt_query[0].reshape(row_count, -1, head_size)
    grad_heads = prompt_cotangent[0].reshape(row_count, -1, head_size)
    query_places = ctx_place * row_count + jnp.arange(row_count, dtype=jnp.int32)
    key_places = jnp.arange(full_length, dtype=jnp.int32)
    causal = key_places[None, :] <= query_places[:, None]
    head_count = query_heads.shape[1]
    shard_rows = lax.all_gather(prompt_cache[0], "ctx", axis=0, tiled=True)
    highest = jnp.full((head_count, row_count), MASKED, jnp.float32)
    piece_places = jnp.arange(shard_rows.shape[0], dtype=jnp.int32)
    allowed = piece_places[None, :] <= query_places[:, None]
    scores = head_scores(query_heads, shard_rows[:, :head_size], allowed, scaling)
    new_high = jnp.maximum(highest, jnp.max(scores, axis=2))
    weights = jnp.exp(scores - new_high[:, :, None])
    running_sum = jnp.sum(weights, axis=2)
    accumulated = jnp.einsum(
        "hrk,kd->hrd",
        weights.astype(jnp.bfloat16),
        shard_rows[:, head_size:],
        preferred_element_type=jnp.float32,
    )
    highest, running_sum, accumulated = (new_high, running_sum, accumulated)
    log_total = highest + jnp.log(running_sum)
    prompt_out = jnp.transpose(accumulated / running_sum[:, :, None], (1, 0, 2)).astype(
        jnp.bfloat16
    )
    own_full = lax.all_gather(prompt_cache[0], "ctx", axis=0, tiled=True)
    scores = head_scores(query_heads, own_full[:, :head_size], causal, scaling)
    weights = jnp.exp(scores - log_total[:, :, None])
    prompt_dq, prompt_terms = backward_core(
        query_heads,
        grad_heads,
        own_full[:, :head_size],
        own_full[:, head_size:],
        weights,
        prompt_out,
        scaling,
    )
    pieces = lax.all_gather(prompt_cache, ("ctx", "grp"), axis=0, tiled=True)
    both_prompts = jnp.transpose(
        pieces.reshape(ctx_count, group_count, row_count, 2 * head_size), (1, 0, 2, 3)
    ).reshape(group_count * full_length, 2 * head_size)
    capacity = reply_query.shape[0]
    lengths = reply_lengths[0]
    owners = reply_owner[0]
    slot_count = lengths.shape[0]
    bounds = jnp.cumsum(lengths)
    places = jnp.arange(capacity, dtype=jnp.int32)
    slot_of = jnp.sum((places[:, None] >= bounds[None, :]).astype(jnp.int32), axis=1)
    picks = slot_of[:, None] == jnp.arange(slot_count, dtype=jnp.int32)[None, :]
    owner_of = jnp.sum(jnp.where(picks, owners[None, :], 0), axis=1)
    usable = places < bounds[-1]
    filled = bounds[-1]
    prompt_keys = both_prompts.shape[0]
    all_keys = jnp.concatenate([both_prompts, reply_cache], axis=0)
    key_rows = all_keys[:, :head_size]
    value_rows = all_keys[:, head_size:]
    key_owner = jnp.arange(prompt_keys, dtype=jnp.int32) // full_length
    reply_heads = reply_query.reshape(capacity, -1, head_size)
    reply_used = jnp.where(
        usable[:, None], reply_cotangent, jnp.zeros_like(reply_cotangent)
    ).reshape(capacity, -1, head_size)
    block_rows = min(512, capacity)
    block_count = capacity // block_rows

    def one_block(running, block_index):
        block_start = block_index * block_rows

        def work(unused):
            query_block = lax.dynamic_slice_in_dim(reply_heads, block_start, block_rows, 0)
            grad_block = lax.dynamic_slice_in_dim(reply_used, block_start, block_rows, 0)
            block_places = block_start + jnp.arange(block_rows, dtype=jnp.int32)
            block_slots = lax.dynamic_slice_in_dim(slot_of, block_start, block_rows, 0)
            block_owner = lax.dynamic_slice_in_dim(owner_of, block_start, block_rows, 0)
            block_usable = lax.dynamic_slice_in_dim(usable, block_start, block_rows, 0)
            allowed = jnp.concatenate(
                [
                    block_owner[:, None] == key_owner[None, :],
                    (block_slots[:, None] == slot_of[None, :])
                    & (places[None, :] <= block_places[:, None]),
                ],
                axis=1,
            )
            attended, query_grad, stacked_grad = full_pass(
                query_block, grad_block, key_rows, value_rows, allowed, block_usable, scaling
            )
            return (running + stacked_grad, attended, query_grad)

        def skip(unused):
            empty = jnp.zeros((block_rows, reply_heads.shape[1], head_size), jnp.bfloat16)
            return (running, empty, empty)

        running, attended, query_grad = lax.cond(block_start < filled, work, skip, 0)
        return (running, (attended, query_grad))

    initial_sum = jnp.zeros((all_keys.shape[0], 2 * head_size), jnp.float32)
    summed, (reply_out, reply_dq) = lax.scan(
        one_block, initial_sum, jnp.arange(block_count, dtype=jnp.int32)
    )
    own_prompt = (jnp.arange(group_count, dtype=jnp.int32) == group_place).astype(jnp.float32)
    prompt_total = (
        summed[:prompt_keys].reshape(group_count, full_length, 2 * head_size)
        + own_prompt[:, None, None] * prompt_terms[None, :, :]
    )
    prompt_grad = lax.psum_scatter(
        prompt_total, ("ctx", "comp", "grp"), scatter_dimension=1, tiled=True
    ).astype(jnp.bfloat16)
    reply_grad = lax.psum(summed[prompt_keys:], "ctx").astype(jnp.bfloat16)
    return (
        prompt_out.reshape(1, row_count, -1),
        prompt_dq.reshape(1, row_count, -1),
        prompt_grad,
        reply_out.reshape(capacity, -1),
        reply_dq.reshape(capacity, -1),
        reply_grad,
    )


def solution(mesh):
    return jax.shard_map(
        per_device,
        mesh=mesh,
        in_specs=(
            P("grp", "ctx", "comp"),
            P("grp", "ctx", None),
            P("grp", "ctx", "comp"),
            P(("comp", "grp"), "ctx"),
            P(("comp", "grp"), None),
            P(("comp", "grp"), "ctx"),
            P(("comp", "grp"), None),
            P(("comp", "grp"), None),
        ),
        out_specs=(
            P("grp", "ctx", "comp"),
            P("grp", "ctx", "comp"),
            P(None, ("ctx", "comp", "grp"), None),
            P(("comp", "grp"), "ctx"),
            P(("comp", "grp"), "ctx"),
            P(("comp", "grp"), None),
        ),
        check_vma=False,
    )
```

profile of v0, /device:TPU:4, one launch (start us, length us, event | category | flops | bytes accessed | tf_op | source)
XLA Modules:
  0.0 903.6 jit_solution(15549731170097055454)
XLA Ops:
  13.3 40.6 %all-gather.6.cloned.1.call-done = bf16[1,4096,256]{2,1,0:T(8,128)(2,1)} async-done(((bf16[1,512,256]{2,1,0:T(8,128)(2,1)}), bf16[1,4096,256]{2,1,0:T(8,128)(2,1)}) %all-gather.6.cloned.1.call-update) | async-done | bytes 2097168 | tf_op jit(solution)/shard_map/all_gather | solution.py:77
  53.9 2.6 fusion.63
  67.4 5.7 copy.28
  73.1 18.9 %all-gather.4.cloned.1.call-done = bf16[16,512,256]{2,1,0:T(8,128)(2,1)} async-done(((bf16[1,512,256]{2,1,0:T(8,128)(2,1)}), bf16[16,512,256]{2,1,0:T(8,128)(2,1)}) %all-gather.4.cloned.1.call-update) | async-done | bytes 4194320 | tf_op jit(solution)/shard_map/all_gather | solution.py:108
  94.5 6.6 pad_maximum_fusion.1
  101.1 4.8 broadcast_in_dim.97
  105.9 127.6 %while.19 = (s32[]{:T(128)}, f32[9216,256]{0,1:T(8,128)}, bf16[2,512,1,128]{3,1,2,0:T(8,128)(2,1)S(1)}, bf16[2,512,1,128]{3,1,2,0:T(8,128)(2,1)S(1)}, s32[2]{0:T...) while((s32[]{:T(128)}, f32[9216,256]{0,1:T(8,128)}, ...), condition=%wide.region_10.11_spmd.clone.clone, body=%wide.region_5.10_spmd.clone.clone.sunk | while | flops 7316636160 | bytes 204659664 | solution.py:166
  107.9 61.7 %conditional.4 = (f32[9216,256]{0,1:T(8,128)}, bf16[1,512,1,128]{3,1,2,0:T(8,128)(2,1)S(1)}, bf16[1,512,1,128]{3,1,2,0:T(8,128)(2,1)S(1)}) conditional(s32[]{:T(128)} %convert_element_type.132, f32[9216,256]{0,1:T(8,128)} %get-tuple-element.390, (s32[]{:T(128)}, s32[1024]{0:T(1024)S(1)}, s32[8192]{0:T(1024)S(1)}, s32[1024]{0:T(1024)S(1)}, ...), branch_computations={%region_6.6_spmd, %region_7.9_spmd.clone} | conditional | flops 7316627968 | bytes 204065408 | solution.py:162
  111.6 10.5 %fusion.62 = (f32[512]{0:T(512)S(1)}, f32[1,512,9216]{2,1,0:T(8,128)}) fusion(bf16[9216,128]{1,0:T(8,128)(2,1)} %get-tuple-element.221, bf16[1024,1,128]{2,0,1:T(8,128)(2,1)S(1)} %get-tuple-element.220, s32[]{:T(128)S(6)} %select_n.44, pred[512,1024]{1,0:T(32,128)(4,1)S(1)} %compare_and_fusion, pred[512,8192]{1,0:T(32,128)(4,1)S(1)} %broadcast_compare_fusion), kind=kOutput, calls=%fused_computation.98 | convolution fusion | flops 1226833408 | bytes 26085380 | tf_op jit(solution)/shard_map/while/body/eval_jaxpr/cond/branch_1_fun/rhd,kd->hrk/dot_general | solution.py:11
  122.1 9.0 exponential_reduce_fusion
  131.1 8.3 fusion.11
  139.4 4.3 fusion.16
  143.7 3.6 fusion.17
  147.3 9.2 %fusion.10 = bf16[512,9216]{1,0:T(8,128)(2,1)S(1)} fusion(bf16[9216,128]{1,0:T(8,128)(2,1)} %get-tuple-element.223, f32[1,512,9216]{2,1,0:T(8,128)} %get-tuple-element.274, f32[512]{0:T(512)S(1)} %get-tuple-element.275, f32[512]{0:T(512)S(1)} %log_add_fusion, bf16[1024,1,128]{2,0,1:T(8,128)(2,1)S(1)} %get-tuple-element.222, s32[]{:T(128)S(6)} %select_n.44), kind=kOutput, calls=%fused_computation.12 | convolution fusion | flops 1226833920 | bytes 30806020 | tf_op jit(solution)/shard_map/while/body/eval_jaxpr/cond/branch_1_fun/rhd,kd->hrk/dot_general | solution.py:22
  156.6 4.4 fusion.15
  162.8 6.8 maximum_add_fusion
  171.6 61.7 %conditional.4 = (f32[9216,256]{0,1:T(8,128)}, bf16[1,512,1,128]{3,1,2,0:T(8,128)(2,1)S(1)}, bf16[1,512,1,128]{3,1,2,0:T(8,128)(2,1)S(1)}) conditional(s32[]{:T(128)} %convert_element_type.132, f32[9216,256]{0,1:T(8,128)} %get-tuple-element.390, (s32[]{:T(128)}, s32[1024]{0:T(1024)S(1)}, s32[8192]{0:T(1024)S(1)}, s32[1024]{0:T(1024)S(1)}, ...), branch_computations={%region_6.6_spmd, %region_7.9_spmd.clone} | conditional | flops 7316627968 | bytes 204065408 | solution.py:162
  175.3 10.5 %fusion.62 = (f32[512]{0:T(512)S(1)}, f32[1,512,9216]{2,1,0:T(8,128)}) fusion(bf16[9216,128]{1,0:T(8,128)(2,1)} %get-tuple-element.221, bf16[1024,1,128]{2,0,1:T(8,128)(2,1)S(1)} %get-tuple-element.220, s32[]{:T(128)S(6)} %select_n.44, pred[512,1024]{1,0:T(32,128)(4,1)S(1)} %compare_and_fusion, pred[512,8192]{1,0:T(32,128)(4,1)S(1)} %broadcast_compare_fusion), kind=kOutput, calls=%fused_computation.98 | convolution fusion | flops 1226833408 | bytes 26085380 | tf_op jit(solution)/shard_map/while/body/eval_jaxpr/cond/branch_1_fun/rhd,kd->hrk/dot_general | solution.py:11
  185.8 9.0 exponential_reduce_fusion
  194.8 8.3 fusion.11
  203.1 4.3 fusion.16
  207.4 3.6 fusion.17
  211.0 9.2 %fusion.10 = bf16[512,9216]{1,0:T(8,128)(2,1)S(1)} fusion(bf16[9216,128]{1,0:T(8,128)(2,1)} %get-tuple-element.223, f32[1,512,9216]{2,1,0:T(8,128)} %get-tuple-element.274, f32[512]{0:T(512)S(1)} %get-tuple-element.275, f32[512]{0:T(512)S(1)} %log_add_fusion, bf16[1024,1,128]{2,0,1:T(8,128)(2,1)S(1)} %get-tuple-element.222, s32[]{:T(128)S(6)} %select_n.44), kind=kOutput, calls=%fused_computation.12 | convolution fusion | flops 1226833920 | bytes 30806020 | tf_op jit(solution)/shard_map/while/body/eval_jaxpr/cond/branch_1_fun/rhd,kd->hrk/dot_general | solution.py:22
  220.3 4.4 fusion.15
  226.5 6.8 maximum_add_fusion
  233.6 7.7 slice.31
  241.3 9.0 copy.27
  250.3 8.8 multiply_add_fusion
  260.6 4.2 fusion.52
  264.8 9.6 %copy.29 = f32[9216,256]{1,0:T(8,128)} copy(f32[9216,256]{0,1:T(8,128)} %get-tuple-element.124) | data formatting | bytes 18874368 | tf_op jit(solution)/shard_map/while | solution.py:166
  275.7 66.4 %all-reduce.1 = bf16[1024,256]{1,0:T(8,128)(2,1)} all-reduce(f32[1024,256]{1,0:T(8,128)S(1)} %slice.37), channel_id=1, replica_groups=mesh['ctx'=8,'comp'=8,'grp'=2] {'ctx'}, use_global_device_ids=true, to_apply=%region_12.13 | all-reduce | flops 262144 | bytes 1572864 | tf_op jit(solution)/shard_map/psum | solution.py:177
  342.2 553.4 %reduce-scatter.2.cloned.1.call-done = f32[2,32,256]{2,1,0:T(8,128)} async-done(((f32[2,4096,256]{2,1,0:T(8,128)}), f32[2,32,256]{2,1,0:T(8,128)}) %reduce-scatter.2.cloned.1.call-update) | async-done | bytes 65552 | tf_op jit(solution)/shard_map/reduce_scatter | solution.py:174
  (90 shorter events, 35.8 us)
Async XLA Ops:
  7.2 46.8 %copy-start = (bf16[1,512,128]{2,1,0:T(8,128)(2,1)S(1)}, bf16[1,512,128]{2,1,0:T(8,128)(2,1)}, u32[]{:S(2)}) copy-start(bf16[1,512,128]{2,1,0:T(8,128)(2,1)} %param.12) | copy-start | bytes 393220
  7.2 46.8 %all-gather.6.cloned.1.call-start = ((), (), s32[]{:S(2)}) async-start(), calls=%async_computation.3 | async-start | bytes 2359296 | tf_op jit(solution)/shard_map/all_gather | solution.py:77
  7.9 84.1 %all-gather.4.cloned.1.call-start = ((), (), s32[]{:S(2)}) async-start(), calls=%async_computation.1 | async-start | bytes 4456448 | tf_op jit(solution)/shard_map/all_gather | solution.py:108
  8.7 886.9 %reduce-scatter.2.cloned.1.call-start = ((), (), s32[]{:S(2)}) async-start(), calls=%async_computation.2 | async-start | bytes 8454144 | tf_op jit(solution)/shard_map/reduce_scatter | solution.py:174
  56.6 1.6 copy-start.3
  56.6 1.6 copy-start.6
  62.1 3.0 copy-start.2
  67.4 27.1 %copy-start.7 = (bf16[1024,256]{1,0:T(8,128)(2,1)S(1)}, bf16[1024,256]{1,0:T(8,128)(2,1)}, u32[]{:S(2)}) copy-start(bf16[1024,256]{1,0:T(8,128)(2,1)} %param.16) | copy-start | bytes 1572868
  94.5 11.4 %copy-start.5 = (bf16[1024,128]{1,0:T(8,128)(2,1)S(1)}, bf16[1024,128]{1,0:T(8,128)(2,1)}, u32[]{:S(2)}) copy-start(bf16[1024,128]{1,0:T(8,128)(2,1)} %param.15) | copy-start | bytes 786436
  156.6 6.2 slice-start
  161.0 1.7 slice-start.1
  220.3 6.2 slice-start
  224.7 1.7 slice-start.1
  233.5 7.7 copy-start.9
  233.6 7.7 copy-start.10
  241.3 9.0 copy-start.8
  259.0 1.6 copy-start.4
  260.6 636.4 %copy-start.1 = (bf16[1,512,128]{2,1,0:T(8,128)(2,1)S(1)}, bf16[1,512,128]{2,1,0:T(8,128)(2,1)}, u32[]{:S(2)}) copy-start(bf16[1,512,128]{2,1,0:T(8,128)(2,1)} %param.12) | copy-start | bytes 393220
Sparse Core Ops, SparseCore 0:
  9.7 44.2 all-gather.5
  55.6 36.3 all-gather.3
  259.2 636.3 reduce-scatter.1
where the time goes:
time: 919 us; the launch traced here: 904 us
  waiting for transfers between devices  614 us (67%)
  matrix products  81.3 us (9%)
  other arithmetic  79.4 us (9%)
  blocking collectives  66.4 us (7%)
  local copies, waits for them, and re-layouts  44.9 us (5%)
  between operations  13.9 us (2%)
    reduce_scatter x1, waiting for transfers between devices, per_device(): lax.psum_scatter(prompt_total, ('ctx', 'comp', 'grp'), scatter_dimension=...  553 us
    psum x1, blocking collectives, per_device(): reply_grad = lax.psum(summed[prompt_keys:], 'ctx').astype(jnp.bfloat16)  66.4 us
    all_gather x1, waiting for transfers between devices, per_device(): shard_rows = lax.all_gather(prompt_cache[0], 'ctx', axis=0, tiled=True)  40.6 us
    dot_general x3, matrix products, head_scores(): jnp.einsum('rhd,kd->hrk', query_heads, key_rows, preferred_element_type=j...  23.5 us
    dot_general x3, matrix products, backward_core(): jnp.einsum('rhd,kd->hrk', grad_heads, value_rows, preferred_element_type=...  20.3 us
    all_gather x1, waiting for transfers between devices, per_device(): pieces = lax.all_gather(prompt_cache, ('ctx', 'grp'), axis=0, tiled=True)  18.9 us
  transfers between devices with their start and end apart: 3, of which 3 were waited for; matrix products, arithmetic and copies ran while one was open for 4% of the time, Pallas kernels for 0%

commit v1 on v0

v1 whole, which is shorter than its diff:
```python
import functools
import jax
import jax.numpy as jnp
from jax import lax
from jax.experimental import pallas as pl
from jax.experimental.pallas import tpu as pltpu
from jax.sharding import PartitionSpec as P

ROWS = 256
CHUNK = 512
LOCAL = 256
LOG2E = 1.4426950408889634
MASKED = -1e30
F32 = jnp.float32
BF16 = jnp.bfloat16


def dot(a, b, ca, cb):
    return lax.dot_general(a, b, (((ca,), (cb,)), ((), ())), preferred_element_type=F32)


def run_block(q_t, do_t, scaling, parts, score_ref, weight_ref):
    head, rows = q_t.shape
    steep = scaling * LOG2E

    highest = jnp.full((8, rows), MASKED, F32)
    for cache, _, offset, size, first, last, mask in parts:

        def scores_of(c, highest, cache=cache, offset=offset, size=size, mask=mask):
            at = pl.multiple_of(c * size, size)
            scores = dot(cache[pl.ds(at, size), :head], q_t, 1, 0)
            if mask is not None:
                scores = mask(scores, at)
            score_ref[pl.ds(offset + at, size), :] = scores
            return jnp.maximum(highest, jnp.max(scores.reshape(size // 8, 8, rows), axis=0))

        highest = lax.fori_loop(first, last, scores_of, highest)
    highest = jnp.max(highest, axis=0, keepdims=True) * steep

    carry = (jnp.zeros((8, rows), F32), jnp.zeros((head, rows), F32))
    for cache, _, offset, size, first, last, _ in parts:

        def weights_of(c, carry, cache=cache, offset=offset, size=size):
            total, out = carry
            at = pl.multiple_of(c * size, size)
            weights = jnp.exp2(score_ref[pl.ds(offset + at, size), :] * steep - highest)
            total = total + jnp.sum(weights.reshape(size // 8, 8, rows), axis=0)
            rounded = weights.astype(BF16)
            weight_ref[pl.ds(offset + at, size), :] = rounded
            out = out + dot(cache[pl.ds(at, size), head:], rounded, 0, 0)
            return total, out

        carry = lax.fori_loop(first, last, weights_of, carry)
    total, out = carry
    inverse = 1.0 / jnp.sum(total, axis=0, keepdims=True)
    out = (out * inverse).astype(BF16)
    row_dot = jnp.sum(out.astype(F32) * do_t.astype(F32), axis=0, keepdims=True)
    q_scaled = (q_t.astype(F32) * (inverse * scaling)).astype(BF16)
    do_scaled = (do_t.astype(F32) * inverse).astype(BF16)

    query_grad = jnp.zeros((head, rows), F32)
    for cache, grad, offset, size, first, last, _ in parts:

        def grads_of(c, query_grad, cache=cache, grad=grad, offset=offset, size=size):
            at = pl.multiple_of(c * size, size)
            rounded = weight_ref[pl.ds(offset + at, size), :]
            weight_grad = dot(cache[pl.ds(at, size), head:], do_t, 1, 0)
            score_grad = (rounded.astype(F32) * (weight_grad - row_dot)).astype(BF16)
            grad[pl.ds(at, size), :head] += dot(score_grad, q_scaled, 1, 1)
            grad[pl.ds(at, size), head:] += dot(rounded, do_scaled, 1, 1)
            return query_grad + dot(cache[pl.ds(at, size), :head], score_grad, 0, 0)

        query_grad = lax.fori_loop(first, last, grads_of, query_grad)
    return out, (query_grad * (inverse * scaling)).astype(BF16)


def prompt_kernel(scaling, place_ref, q_ref, do_ref, cache_ref, carried_ref, arrived_ref, out_ref, dq_ref, sum_ref, grad, score_ref, weight_ref):
    length, rows_here = cache_ref.shape[0], q_ref.shape[0]
    shards = length // rows_here
    me = place_ref[0]
    grad[...] = carried_ref[...].astype(F32) + arrived_ref[...].astype(F32)

    def block(b, unused):
        here = pl.multiple_of(b * ROWS, ROWS)
        q_t = q_ref[pl.ds(here, ROWS), :].astype(F32).T.astype(BF16)
        do_t = do_ref[pl.ds(here, ROWS), :].astype(F32).T.astype(BF16)

        def causal(scores, at):
            keys = at + lax.broadcasted_iota(jnp.int32, scores.shape, 0)
            rows = here + lax.broadcasted_iota(jnp.int32, scores.shape, 1)
            return jnp.where(keys <= rows, scores, MASKED)

        whole = rows_here // CHUNK
        parts = [
            (cache_ref, grad, 0, ROWS, 0, b + 1, causal),
            (cache_ref, grad, 0, CHUNK, whole, whole * (me + 1), None),
        ]
        out, query_grad = run_block(q_t, do_t, scaling, parts, score_ref, weight_ref)
        out_ref[pl.ds(here, ROWS), :] = out.astype(F32).T.astype(BF16)
        dq_ref[pl.ds(here, ROWS), :] = query_grad.astype(F32).T.astype(BF16)
        return unused

    lax.fori_loop(0, q_ref.shape[0] // ROWS, block, 0)
    for k in range(shards):
        at = pl.multiple_of(lax.rem(me + (shards - k), shards) * rows_here, rows_here)
        sum_ref[pl.ds(at, rows_here), :] = grad[k * rows_here : (k + 1) * rows_here, :].astype(BF16)


def prompt_pass(place, q, do, cache, carried, arrived, scaling):
    rows, head = q.shape
    length = cache.shape[0]
    return pl.pallas_call(
        functools.partial(prompt_kernel, scaling),
        out_shape=[
            jax.ShapeDtypeStruct((rows, head), BF16),
            jax.ShapeDtypeStruct((rows, head), BF16),
            jax.ShapeDtypeStruct((length, 2 * head), BF16),
        ],
        in_specs=[pl.BlockSpec(memory_space=pltpu.SMEM)] + [pl.BlockSpec(memory_space=pltpu.VMEM)] * 5,
        out_specs=[pl.BlockSpec(memory_space=pltpu.VMEM)] * 3,
        scratch_shapes=[
            pltpu.VMEM((length, 2 * head), F32),
            pltpu.VMEM((length, ROWS), F32),
            pltpu.VMEM((length, ROWS), BF16),
        ],
        compiler_params=pltpu.CompilerParams(vmem_limit_bytes=48 * 1024 * 1024),
        name="prompt_pass",
    )(place, q, do, cache, carried, arrived)


def reply_kernel(scaling, which_ref, lengths_ref, owners_ref, q_ref, do_ref, cache_ref, own_ref, *refs):
    out_ref, dq_ref, sum_ref, own_sum_ref, q_t_ref, do_t_ref, out_t, dq_t, grad, own_grad, score_ref, weight_ref = refs[-12:]
    before = refs[:-12]
    capacity, head = q_ref.shape
    length = cache_ref.shape[0]
    slots = lengths_ref.shape[0]
    starts, ranks, counts = [], [], []
    at, rank = jnp.int32(0), jnp.int32(0)
    for s in range(slots):
        count = jnp.where(owners_ref[s] == which_ref[0], lengths_ref[s], 0)
        starts.append(at)
        ranks.append(rank)
        counts.append(count)
        at = at + lengths_ref[s]
        rank = rank + count
    blocks = (rank + ROWS - 1) // ROWS

    q_t_ref[...] = q_ref[...].astype(F32).T.astype(BF16)
    do_t_ref[...] = do_ref[...].astype(F32).T.astype(BF16)
    out_t[...] = jnp.zeros_like(out_t)
    dq_t[...] = jnp.zeros_like(dq_t)
    grad[...] = jnp.zeros_like(grad)
    if before:
        own_grad[...] = before[2][...]
    else:
        own_grad[...] = jnp.zeros_like(own_grad)

    def block(b, unused):
        first_rank = b * ROWS
        place_of = first_rank + lax.broadcasted_iota(jnp.int32, (1, ROWS), 1)
        place = jnp.full((1, ROWS), -1, jnp.int32)
        start = jnp.zeros((1, ROWS), jnp.int32)
        low, high = jnp.int32(capacity), jnp.int32(0)
        for s in range(slots):
            inside = (place_of >= ranks[s]) & (place_of < ranks[s] + counts[s])
            place = jnp.where(inside, place_of + (starts[s] - ranks[s]), place)
            start = jnp.where(inside, starts[s], start)
            begin = jnp.maximum(ranks[s], first_rank)
            end = jnp.minimum(ranks[s] + counts[s], first_rank + ROWS)
            some = begin < end
            low = jnp.where(some, jnp.minimum(low, starts[s]), low)
            high = jnp.where(some, jnp.maximum(high, end + (starts[s] - ranks[s])), high)
        picks = jnp.where(
            lax.broadcasted_iota(jnp.int32, (capacity, ROWS), 0) == place, 1.0, 0.0
        ).astype(BF16)
        q_t = dot(q_t_ref[...], picks, 1, 0).astype(BF16)
        do_t = dot(do_t_ref[...], picks, 1, 0).astype(BF16)

        def packed(scores, at):
            keys = at + lax.broadcasted_iota(jnp.int32, scores.shape, 0)
            return jnp.where((keys >= start) & (keys <= place), scores, MASKED)

        parts = [
            (cache_ref, grad, 0, CHUNK, 0, length // CHUNK, None),
            (own_ref, own_grad, length, LOCAL, low // LOCAL, (high + LOCAL - 1) // LOCAL, packed),
        ]
        out, query_grad = run_block(q_t, do_t, scaling, parts, score_ref, weight_ref)
        out_t[...] += dot(out, picks, 1, 1)
        dq_t[...] += dot(query_grad, picks, 1, 1)
        return unused

    lax.fori_loop(0, blocks, block, 0)
    out = out_t[...].T
    query_grad = dq_t[...].T
    if before:
        out = out + before[0][...].astype(F32)
        query_grad = query_grad + before[1][...].astype(F32)
    out_ref[...] = out.astype(BF16)
    dq_ref[...] = query_grad.astype(BF16)
    sum_ref[...] = grad[...].astype(BF16)
    own_sum_ref[...] = own_grad[...].astype(own_sum_ref.dtype)


def reply_pass(which, lengths, owners, q, do, cache, own, before, own_type, scaling):
    capacity, head = q.shape
    length = cache.shape[0]
    return pl.pallas_call(
        functools.partial(reply_kernel, scaling),
        out_shape=[
            jax.ShapeDtypeStruct((capacity, head), BF16),
            jax.ShapeDtypeStruct((capacity, head), BF16),
            jax.ShapeDtypeStruct((length, 2 * head), BF16),
            jax.ShapeDtypeStruct((capacity, 2 * head), own_type),
        ],
        in_specs=[pl.BlockSpec(memory_space=pltpu.SMEM)] * 3
        + [pl.BlockSpec(memory_space=pltpu.VMEM)] * (4 + len(before)),
        out_specs=[pl.BlockSpec(memory_space=pltpu.VMEM)] * 4,
        scratch_shapes=[
            pltpu.VMEM((head, capacity), BF16),
            pltpu.VMEM((head, capacity), BF16),
            pltpu.VMEM((head, capacity), F32),
            pltpu.VMEM((head, capacity), F32),
            pltpu.VMEM((length, 2 * head), F32),
            pltpu.VMEM((capacity, 2 * head), F32),
            pltpu.VMEM((length + capacity, ROWS), F32),
            pltpu.VMEM((length + capacity, ROWS), BF16),
        ],
        compiler_params=pltpu.CompilerParams(vmem_limit_bytes=48 * 1024 * 1024),
        name="reply_pass",
    )(which, lengths, owners, q, do, cache, own, *before)


def per_device(
    prompt_query,
    prompt_cache,
    prompt_cotangent,
    reply_query,
    reply_cache,
    reply_cotangent,
    reply_lengths,
    reply_owner,
):
    width = prompt_cache.shape[2]
    scaling = (width // 2) ** (-0.5)
    row_count = prompt_query.shape[1]
    capacity = reply_query.shape[0]
    ctx_count, comp_count, group_count = (lax.axis_size(name) for name in ("ctx", "comp", "grp"))
    place = lax.axis_index("ctx").astype(jnp.int32).reshape(1)
    group = lax.axis_index("grp").astype(jnp.int32).reshape(1)
    swap = [(0, 1), (1, 0)]

    with jax.named_scope("gather_keys"):
        own = prompt_cache[0]
        shards = [own] + [
            lax.ppermute(own, "ctx", [(i, (i + k) % ctx_count) for i in range(ctx_count)])
            for k in range(1, ctx_count)
        ]
        mine = jnp.concatenate(shards, axis=0)
        other = lax.ppermute(mine, "grp", swap)

    lengths, owners = reply_lengths[0], reply_owner[0]
    with jax.named_scope("reply_other"):
        out1, dq1, sum1, own1 = reply_pass(
            1 - group, lengths, owners, reply_query, reply_cotangent, other, reply_cache, [], F32, scaling
        )
    arrived = lax.ppermute(sum1, "grp", swap)
    with jax.named_scope("reply_own"):
        reply_out, reply_dq, sum2, own2 = reply_pass(
            group, lengths, owners, reply_query, reply_cotangent, mine, reply_cache, [out1, dq1, own1], BF16, scaling
        )
    with jax.named_scope("prompt_rows"):
        prompt_out, prompt_dq, total = prompt_pass(
            place, prompt_query[0], prompt_cotangent[0], mine, sum2, arrived, scaling
        )

    with jax.named_scope("reply_cache_sum"):
        terms = lax.all_to_all(own2.reshape(ctx_count, -1, width), "ctx", 0, 0, tiled=True)
        part = jnp.sum(terms.astype(F32), axis=0).astype(BF16)
        reply_grad = lax.all_to_all(
            jnp.broadcast_to(part[None], (ctx_count,) + part.shape), "ctx", 0, 0, tiled=True
        ).reshape(capacity, width)

    with jax.named_scope("prompt_cache_sum"):
        count = ctx_count * comp_count
        terms = lax.all_to_all(total.reshape(count, -1, width), ("ctx", "comp"), 0, 0, tiled=True)
        part = jnp.sum(terms.astype(F32), axis=0).astype(BF16)
        prompt_grad = lax.all_to_all(part.reshape(group_count, -1, width), "grp", 0, 0, tiled=True)
    return (
        prompt_out[None],
        prompt_dq[None],
        prompt_grad,
        reply_out,
        reply_dq,
        reply_grad,
    )


def solution(mesh):
    return jax.shard_map(
        per_device,
        mesh=mesh,
        in_specs=(
            P("grp", "ctx", "comp"),
            P("grp", "ctx", None),
            P("grp", "ctx", "comp"),
            P(("comp", "grp"), "ctx"),
            P(("comp", "grp"), None),
            P(("comp", "grp"), "ctx"),
            P(("comp", "grp"), None),
            P(("comp", "grp"), None),
        ),
        out_specs=(
            P("grp", "ctx", "comp"),
            P("grp", "ctx", "comp"),
            P(None, ("ctx", "comp", "grp"), None),
            P(("comp", "grp"), "ctx"),
            P(("comp", "grp"), "ctx"),
            P(("comp", "grp"), None),
        ),
        check_vma=False,
    )
```

time: 919 us -> 189 us (0.21)
  the two profiles are of different devices: /device:TPU:4 before, /device:TPU:1 now
where the time goes in v1:
time: 189 us; the launch traced here: 186 us
  starting transfers between devices  57.5 us (30%)
  Pallas kernels  53.8 us (28%)
  waiting for transfers between devices  42.1 us (22%)
  blocking collectives  25.4 us (13%)
  local copies, waits for them, and re-layouts  6.08 us (3%)
    pallas_call x2, Pallas kernels, reply_pass(): pl.pallas_call(functools.partial(reply_kernel, scaling), out_shape=[jax.S...  47.5 us
    all_to_all x1, starting transfers between devices, per_device(): lax.all_to_all(total.reshape(count, -1, width), ('ctx', 'comp'), 0, 0, ti...  35.1 us
    all_to_all x1, waiting for transfers between devices, per_device(): lax.all_to_all(total.reshape(count, -1, width), ('ctx', 'comp'), 0, 0, ti...  19.7 us
    ppermute x7, waiting for transfers between devices, per_device(): lax.ppermute(own, 'ctx', [(i, (i + k) % ctx_count) for i in range(ctx_cou...  18.5 us
    ppermute x7, starting transfers between devices, per_device(): lax.ppermute(own, 'ctx', [(i, (i + k) % ctx_count) for i in range(ctx_cou...  16.5 us
    all_to_all x1, blocking collectives, per_device(): lax.all_to_all(part.reshape(group_count, -1, width), 'grp', 0, 0, tiled=T...  13.4 us
    all_to_all x1, blocking collectives, per_device(): lax.all_to_all(own2.reshape(ctx_count, -1, width), 'ctx', 0, 0, tiled=True)  12 us
    pallas_call x1, Pallas kernels, prompt_pass(): pl.pallas_call(functools.partial(prompt_kernel, scaling), out_shape=[jax....  6.27 us
  transfers between devices with their start and end apart: 11, of which 5 were waited for; matrix products, arithmetic and copies ran while one was open for 1% of the time, Pallas kernels for 16%

profile of v1, /device:TPU:1, one launch (start us, length us, event | category | flops | bytes accessed | tf_op | source)
XLA Modules:
  0.0 186.1 jit_solution(13740088124416221750)
XLA Ops:
  0.7 2.5 %collective-permute-start = (bf16[512,256]{1,0:T(8,128)(2,1)}, bf16[512,256]{1,0:T(8,128)(2,1)S(1)}, u32[]{:S(2)}, u32[]{:S(2)}) collective-permute-start(bf16[512,256]{1,0:T(8,128)(2,1)} %bitcast.23), channel_id=1, source_target_pairs={{0,16},{16,32},{32,48},{48,64},{64,80},{80,96},{96,112},{112,0},{1... | collective-permute-start | bytes 786440 | tf_op jit(solution)/shard_map/gather_keys/ppermute | solution.py:255
  3.2 3.2 %collective-permute-start.6 = (bf16[512,256]{1,0:T(8,128)(2,1)}, bf16[512,256]{1,0:T(8,128)(2,1)S(1)}, u32[]{:S(2)}, u32[]{:S(2)}) collective-permute-start(bf16[512,256]{1,0:T(8,128)(2,1)} %bitcast.24), channel_id=1, source_target_pairs={{0,112},{16,0},{32,16},{48,32},{64,48},{80,64},{96,80},{112,96},{1... | collective-permute-start | bytes 786440 | tf_op jit(solution)/shard_map/gather_keys/ppermute | solution.py:255
  6.4 1.2 collective-permute-start.5
  7.7 2.4 %collective-permute-start.1 = (bf16[512,256]{1,0:T(8,128)(2,1)}, bf16[512,256]{1,0:T(8,128)(2,1)S(1)}, u32[]{:S(2)}, u32[]{:S(2)}) collective-permute-start(bf16[512,256]{1,0:T(8,128)(2,1)} %bitcast.27), channel_id=1, source_target_pairs={{0,32},{16,48},{32,64},{48,80},{64,96},{80,112},{96,0},{112,16},{1... | collective-permute-start | bytes 786440 | tf_op jit(solution)/shard_map/gather_keys/ppermute | solution.py:255
  10.1 1.0 constant_dynamic-update-slice_fusion.7
  11.1 1.5 collective-permute-done
  12.6 9.9 %collective-permute-done.1 = bf16[512,256]{1,0:T(8,128)(2,1)S(1)} collective-permute-done((bf16[512,256]{1,0:T(8,128)(2,1)}, bf16[512,256]{1,0:T(8,128)(2,1)S(1)}, u32[]{:S(2)}, u32[]{:S(2)}) %collective-permute-start.1) | collective-permute-done | bytes 262176 | tf_op jit(solution)/shard_map/gather_keys/ppermute | solution.py:255
  22.5 7.1 %collective-permute-start.4 = (bf16[512,256]{1,0:T(8,128)(2,1)}, bf16[512,256]{1,0:T(8,128)(2,1)S(1)}, u32[]{:S(2)}, u32[]{:S(2)}) collective-permute-start(bf16[512,256]{1,0:T(8,128)(2,1)} %bitcast.29), channel_id=1, source_target_pairs={{0,80},{16,96},{32,112},{48,0},{64,16},{80,32},{96,48},{112,64},{1... | collective-permute-start | bytes 786440 | tf_op jit(solution)/shard_map/gather_keys/ppermute | solution.py:255
  29.6 0.0 collective-permute-done.2
  29.7 0.0 collective-permute-done.3
  29.7 7.1 %collective-permute-done.4 = bf16[512,256]{1,0:T(8,128)(2,1)S(1)} collective-permute-done((bf16[512,256]{1,0:T(8,128)(2,1)}, bf16[512,256]{1,0:T(8,128)(2,1)S(1)}, u32[]{:S(2)}, u32[]{:S(2)}) %collective-permute-start.4) | collective-permute-done | bytes 262176 | tf_op jit(solution)/shard_map/gather_keys/ppermute | solution.py:255
  36.8 0.0 collective-permute-done.5
  36.9 2.4 %collective-permute-start.7 = (bf16[4096,256]{1,0:T(8,128)(2,1)S(1)}, bf16[4096,256]{1,0:T(8,128)(2,1)}, u32[]{:S(2)}, u32[]{:S(2)}) collective-permute-start(bf16[4096,256]{1,0:T(8,128)(2,1)S(1)} %constant_dynamic-update-slice_fusion.cache_ref), channel_id=1, source_target_pairs={{0,1},{1,0},{2,3},{3,2},{4,5},{5,4},{6,7},{7,6},{8,9},{9,8},{10,11... | collective-permute-start | bytes 6291464 | tf_op jit(solution)/shard_map/gather_keys/ppermute | solution.py:259
  39.3 3.9 %collective-permute-done.7.cache_ref = bf16[4096,256]{1,0:T(8,128)(2,1)} collective-permute-done((bf16[4096,256]{1,0:T(8,128)(2,1)S(1)}, bf16[4096,256]{1,0:T(8,128)(2,1)}, u32[]{:S(2)}, u32[]{:S(2)}) %collective-permute-start.7) | collective-permute-done | bytes 2097184 | tf_op jit(solution)/shard_map/gather_keys/ppermute | solution.py:259
  43.2 24.8 %reply_pass.2 = (bf16[1024,128]{1,0:T(8,128)(2,1)S(1)}, bf16[1024,128]{1,0:T(8,128)(2,1)S(1)}, bf16[4096,256]{1,0:T(8,128)(2,1)}, f32[1024,256]{1,0:T(8,128)S(1)}) custom-call(s32[1]{0:T(128)S(6)} %sub.3.which_ref, s32[4]{0:T(128)S(1)} %bitcast.18, s32[4]{0:T(128)S(1)} %bitcast.20, bf16[1024,128]{1,0:T(8,128)(2,1)S(1)} %copy-done.5, ...), custom_call_target="tpu_custom_call" | custom-call | tf_op jit(solution)/shard_map/reply_other/reply_pass/pallas_call | solution.py:207
  68.0 0.0 collective-permute-start.8
  68.0 22.7 %reply_pass.3 = (bf16[1024,128]{1,0:T(8,128)(2,1)}, bf16[1024,128]{1,0:T(8,128)(2,1)}, bf16[4096,256]{1,0:T(8,128)(2,1)S(1)}, bf16[1024,256]{1,0:T(8,128)(2,1)S(1)}) custom-call(s32[1]{0:T(128)} %bitcast.4.which_ref, s32[4]{0:T(128)S(1)} %bitcast.19, s32[4]{0:T(128)S(1)} %bitcast.21, bf16[1024,128]{1,0:T(8,128)(2,1)S(1)} %copy-done.5, ...), custom_call_target="tpu_custom_call" | custom-call | tf_op jit(solution)/shard_map/reply_own/reply_pass/pallas_call | solution.py:207
  90.8 1.3 copy-done.2
  92.1 12.0 %all_to_all.20 = bf16[8,128,256]{2,1,0:T(8,128)(2,1)S(1)} all-to-all(bf16[8,128,256]{2,1,0:T(8,128)(2,1)S(1)} %bitcast.15), channel_id=1, replica_groups=mesh['ctx'=8,'comp'=8,'grp'=2] {'ctx'}, dimensions={0} | all-to-all | bytes 1048576 | tf_op jit(solution)/shard_map/reply_cache_sum/all_to_all | solution.py:277
  104.1 0.1 reduce_sum.25
  104.2 0.8 broadcast_in_dim.14
  105.0 3.5 %all-to-all-start.3 = ((bf16[8,128,256]{2,1,0:T(8,128)(2,1)}), bf16[8,128,256]{2,1,0:T(8,128)(2,1)S(1)}, u32[]{:S(2)}, u32[]{:S(2)}) async-start(bf16[8,128,256]{2,1,0:T(8,128)(2,1)} %broadcast_in_dim.14), calls=%async_computation.3 | async-start | bytes 1048576 | tf_op jit(solution)/shard_map/reply_cache_sum/all_to_all | solution.py:279
  108.6 0.0 collective-permute-done.8.arrived_ref
  108.6 6.3 %prompt_pass.1 = (bf16[512,128]{1,0:T(8,128)(2,1)}, bf16[512,128]{1,0:T(8,128)(2,1)}, bf16[4096,256]{1,0:T(8,128)(2,1)S(1)}) custom-call(s32[1]{0:T(128)} %bitcast.place_ref, bf16[512,128]{1,0:T(8,128)(2,1)S(1)} %bitcast.16, bf16[512,128]{1,0:T(8,128)(2,1)S(1)} %bitcast.17, bf16[4096,256]{1,0:T(8,128)(2,1)S(1)} %copy-done.1, bf16[4096,256]{1,0:T(8,128)(2,1)} %copy-done.2, ...), custom_call_target="tpu_custom_call" | custom-call | tf_op jit(solution)/shard_map/prompt_rows/prompt_pass/pallas_call | solution.py:112
  114.9 1.3 copy-done.3
  116.2 0.0 all-to-all-done.3
  116.2 35.1 %all-to-all-start = ((bf16[64,64,256]{2,1,0:T(8,128)(2,1)}), bf16[64,64,256]{2,1,0:T(8,128)(2,1)S(1)}, u32[]{:S(2)}, u32[]{:S(2)}) async-start(bf16[64,64,256]{2,1,0:T(8,128)(2,1)} %bitcast.14), calls=%async_computation | async-start | bytes 4194304 | tf_op jit(solution)/shard_map/prompt_cache_sum/all_to_all | solution.py:285
  151.3 19.7 %all-to-all-done = bf16[64,64,256]{2,1,0:T(8,128)(2,1)S(1)} async-done(((bf16[64,64,256]{2,1,0:T(8,128)(2,1)}), bf16[64,64,256]{2,1,0:T(8,128)(2,1)S(1)}, u32[]{:S(2)}, u32[]{:S(2)}) %all-to-all-start) | async-done | bytes 2097184 | tf_op jit(solution)/shard_map/prompt_cache_sum/all_to_all | solution.py:285
  171.0 0.3 reduce_sum.24
  171.3 13.4 %all_to_all.21 = bf16[2,32,256]{2,1,0:T(8,128)(2,1)S(1)} all-to-all(bf16[2,32,256]{2,1,0:T(8,128)(2,1)S(1)} %bitcast.30), channel_id=1, replica_groups=mesh['ctx'=8,'comp'=8,'grp'=2] {'grp'}, dimensions={0} | all-to-all | bytes 65536 | tf_op jit(solution)/shard_map/prompt_cache_sum/all_to_all | solution.py:287
  184.7 0.6 copy.23
  185.3 0.8 copy.24
  (30 shorter events, 0.2 us)
Async XLA Ops:
  0.6 42.6 %copy-start.4 = (bf16[1024,256]{1,0:T(8,128)(2,1)S(1)}, bf16[1024,256]{1,0:T(8,128)(2,1)}, u32[]{:S(2)}) copy-start(bf16[1024,256]{1,0:T(8,128)(2,1)} %own_ref.3) | copy-start | bytes 1572868
  0.6 42.6 %copy-start.5 = (bf16[1024,128]{1,0:T(8,128)(2,1)S(1)}, bf16[1024,128]{1,0:T(8,128)(2,1)}, u32[]{:S(2)}) copy-start(bf16[1024,128]{1,0:T(8,128)(2,1)} %q_ref.3) | copy-start | bytes 786436
  0.7 42.6 %copy-start.6 = (bf16[1024,128]{1,0:T(8,128)(2,1)S(1)}, bf16[1024,128]{1,0:T(8,128)(2,1)}, u32[]{:S(2)}) copy-start(bf16[1024,128]{1,0:T(8,128)(2,1)} %do_ref.3) | copy-start | bytes 786436
  0.7 42.5 %copy-start.9 = (s32[1,4]{1,0:T(1,128)S(1)}, s32[1,4]{1,0:T(1,128)}, u32[]{:S(2)}) copy-start(s32[1,4]{1,0:T(1,128)} %param.14) | copy-start | bytes 52
  0.7 42.5 %copy-start.10 = (s32[1,4]{1,0:T(1,128)S(1)}, s32[1,4]{1,0:T(1,128)}, u32[]{:S(2)}) copy-start(s32[1,4]{1,0:T(1,128)} %param.15) | copy-start | bytes 52
  0.7 11.9 %collective-permute-start = (bf16[512,256]{1,0:T(8,128)(2,1)}, bf16[512,256]{1,0:T(8,128)(2,1)S(1)}, u32[]{:S(2)}, u32[]{:S(2)}) collective-permute-start(bf16[512,256]{1,0:T(8,128)(2,1)} %bitcast.23), channel_id=1, source_target_pairs={{0,16},{16,32},{32,48},{48,64},{64,80},{80,96},{96,112},{112,0},{1... | collective-permute-start | bytes 786440 | tf_op jit(solution)/shard_map/gather_keys/ppermute | solution.py:255
  3.2 33.6 %collective-permute-start.6 = (bf16[512,256]{1,0:T(8,128)(2,1)}, bf16[512,256]{1,0:T(8,128)(2,1)S(1)}, u32[]{:S(2)}, u32[]{:S(2)}) collective-permute-start(bf16[512,256]{1,0:T(8,128)(2,1)} %bitcast.24), channel_id=1, source_target_pairs={{0,112},{16,0},{32,16},{48,32},{64,48},{80,64},{96,80},{112,96},{1... | collective-permute-start | bytes 786440 | tf_op jit(solution)/shard_map/gather_keys/ppermute | solution.py:255
  6.4 30.4 %collective-permute-start.5 = (bf16[512,256]{1,0:T(8,128)(2,1)}, bf16[512,256]{1,0:T(8,128)(2,1)S(1)}, u32[]{:S(2)}, u32[]{:S(2)}) collective-permute-start(bf16[512,256]{1,0:T(8,128)(2,1)} %bitcast.25), channel_id=1, source_target_pairs={{0,96},{16,112},{32,0},{48,16},{64,32},{80,48},{96,64},{112,80},{1... | collective-permute-start | bytes 786440 | tf_op jit(solution)/shard_map/gather_keys/ppermute | solution.py:255
  7.7 22.0 %collective-permute-start.2 = (bf16[512,256]{1,0:T(8,128)(2,1)}, bf16[512,256]{1,0:T(8,128)(2,1)S(1)}, u32[]{:S(2)}, u32[]{:S(2)}) collective-permute-start(bf16[512,256]{1,0:T(8,128)(2,1)} %bitcast.26), channel_id=1, source_target_pairs={{0,48},{16,64},{32,80},{48,96},{64,112},{80,0},{96,16},{112,32},{1... | collective-permute-start | bytes 786440 | tf_op jit(solution)/shard_map/gather_keys/ppermute | solution.py:255
  7.7 14.8 %collective-permute-start.1 = (bf16[512,256]{1,0:T(8,128)(2,1)}, bf16[512,256]{1,0:T(8,128)(2,1)S(1)}, u32[]{:S(2)}, u32[]{:S(2)}) collective-permute-start(bf16[512,256]{1,0:T(8,128)(2,1)} %bitcast.27), channel_id=1, source_target_pairs={{0,32},{16,48},{32,64},{48,80},{64,96},{80,112},{96,0},{112,16},{1... | collective-permute-start | bytes 786440 | tf_op jit(solution)/shard_map/gather_keys/ppermute | solution.py:255
  12.6 17.1 %collective-permute-start.3 = (bf16[512,256]{1,0:T(8,128)(2,1)}, bf16[512,256]{1,0:T(8,128)(2,1)S(1)}, u32[]{:S(2)}, u32[]{:S(2)}) collective-permute-start(bf16[512,256]{1,0:T(8,128)(2,1)} %bitcast.28), channel_id=1, source_target_pairs={{0,64},{16,80},{32,96},{48,112},{64,0},{80,16},{96,32},{112,48},{1... | collective-permute-start | bytes 786440 | tf_op jit(solution)/shard_map/gather_keys/ppermute | solution.py:255
  22.5 14.3 %collective-permute-start.4 = (bf16[512,256]{1,0:T(8,128)(2,1)}, bf16[512,256]{1,0:T(8,128)(2,1)S(1)}, u32[]{:S(2)}, u32[]{:S(2)}) collective-permute-start(bf16[512,256]{1,0:T(8,128)(2,1)} %bitcast.29), channel_id=1, source_target_pairs={{0,80},{16,96},{32,112},{48,0},{64,16},{80,32},{96,48},{112,64},{1... | collective-permute-start | bytes 786440 | tf_op jit(solution)/shard_map/gather_keys/ppermute | solution.py:255
  36.9 31.2 %copy-start = (bf16[4096,256]{1,0:T(8,128)(2,1)}, bf16[4096,256]{1,0:T(8,128)(2,1)S(1)}, u32[]{:S(2)}) copy-start(bf16[4096,256]{1,0:T(8,128)(2,1)S(1)} %constant_dynamic-update-slice_fusion.cache_ref) | copy-start | bytes 6291460
  36.9 6.3 %collective-permute-start.7 = (bf16[4096,256]{1,0:T(8,128)(2,1)S(1)}, bf16[4096,256]{1,0:T(8,128)(2,1)}, u32[]{:S(2)}, u32[]{:S(2)}) collective-permute-start(bf16[4096,256]{1,0:T(8,128)(2,1)S(1)} %constant_dynamic-update-slice_fusion.cache_ref), channel_id=1, source_target_pairs={{0,1},{1,0},{2,3},{3,2},{4,5},{5,4},{6,7},{7,6},{8,9},{9,8},{10,11... | collective-permute-start | bytes 6291464 | tf_op jit(solution)/shard_map/gather_keys/ppermute | solution.py:259
  68.0 40.5 %collective-permute-start.8 = (bf16[4096,256]{1,0:T(8,128)(2,1)}, bf16[4096,256]{1,0:T(8,128)(2,1)}, u32[]{:S(2)}, u32[]{:S(2)}) collective-permute-start(bf16[4096,256]{1,0:T(8,128)(2,1)} %get-tuple-element.21), channel_id=1, source_target_pairs={{0,1},{1,0},{2,3},{3,2},{4,5},{5,4},{6,7},{7,6},{8,9},{9,8},{10,11... | collective-permute-start | bytes 6291464 | tf_op jit(solution)/shard_map/ppermute | solution.py:266
  90.7 1.3 copy-start.2
  92.1 16.5 %copy-start.1 = (bf16[4096,256]{1,0:T(8,128)(2,1)S(1)}, bf16[4096,256]{1,0:T(8,128)(2,1)}, u32[]{:S(2)}) copy-start(bf16[4096,256]{1,0:T(8,128)(2,1)} %copy-done) | copy-start | bytes 6291460
  92.1 16.5 %copy-start.7 = (bf16[1,512,128]{2,1,0:T(8,128)(2,1)S(1)}, bf16[1,512,128]{2,1,0:T(8,128)(2,1)}, u32[]{:S(2)}) copy-start(bf16[1,512,128]{2,1,0:T(8,128)(2,1)} %param.8) | copy-start | bytes 393220
  92.1 16.5 %copy-start.8 = (bf16[1,512,128]{2,1,0:T(8,128)(2,1)S(1)}, bf16[1,512,128]{2,1,0:T(8,128)(2,1)}, u32[]{:S(2)}) copy-start(bf16[1,512,128]{2,1,0:T(8,128)(2,1)} %param.10) | copy-start | bytes 393220
  105.0 11.2 %all-to-all-start.3 = ((bf16[8,128,256]{2,1,0:T(8,128)(2,1)}), bf16[8,128,256]{2,1,0:T(8,128)(2,1)S(1)}, u32[]{:S(2)}, u32[]{:S(2)}) async-start(bf16[8,128,256]{2,1,0:T(8,128)(2,1)} %broadcast_in_dim.14), calls=%async_computation.3 | async-start | bytes 1048576 | tf_op jit(solution)/shard_map/reply_cache_sum/all_to_all | solution.py:279
  114.9 1.3 copy-start.3
  116.2 54.8 %all-to-all-start = ((bf16[64,64,256]{2,1,0:T(8,128)(2,1)}), bf16[64,64,256]{2,1,0:T(8,128)(2,1)S(1)}, u32[]{:S(2)}, u32[]{:S(2)}) async-start(bf16[64,64,256]{2,1,0:T(8,128)(2,1)} %bitcast.14), calls=%async_computation | async-start | bytes 4194304 | tf_op jit(solution)/shard_map/prompt_cache_sum/all_to_all | solution.py:285

commit v2 on v1

v2 whole, which is shorter than its diff:
```python
import functools
import jax
import jax.numpy as jnp
from jax import lax
from jax.experimental import pallas as pl
from jax.experimental.pallas import tpu as pltpu
from jax.sharding import PartitionSpec as P

ROWS = 256
CHUNK = 512
LOG2E = 1.4426950408889634
MASKED = -1e30
F32 = jnp.float32
BF16 = jnp.bfloat16


def dot(a, b, ca, cb):
    return lax.dot_general(a, b, (((ca,), (cb,)), ((), ())), preferred_element_type=F32)


def turned(x):
    return x.astype(F32).T.astype(BF16)


def run_block(q_t, do_t, scaling, pieces, extra, score_ref, weight_ref, slope_ref=None):
    head, rows = q_t.shape
    steep = scaling * LOG2E

    def each(step, carry):
        for piece in pieces:
            carry = step(piece, carry)
        if extra is not None:
            carry = lax.fori_loop(1, extra[0], lambda w, c: step(extra[1](w), c), carry)
        return carry

    def scores_of(piece, highest):
        cache, at, _, _, row, size, mask = piece
        scores = dot(cache[pl.ds(at, size), :head], q_t, 1, 0)
        if mask is not None:
            scores = mask(scores)
        score_ref[pl.ds(row, size), :] = scores
        return jnp.maximum(highest, jnp.max(scores.reshape(size // 8, 8, rows), axis=0))

    highest = each(scores_of, jnp.full((8, rows), MASKED, F32))
    highest = jnp.max(highest, axis=0, keepdims=True) * steep

    def weights_of(piece, carry):
        cache, at, _, _, row, size, _ = piece
        total, out = carry
        weights = jnp.exp2(score_ref[pl.ds(row, size), :] * steep - highest)
        total = total + jnp.sum(weights.reshape(size // 8, 8, rows), axis=0)
        rounded = weights.astype(BF16)
        weight_ref[pl.ds(row, size), :] = rounded
        if slope_ref is not None:
            slope_ref[pl.ds(row, size), :] = dot(cache[pl.ds(at, size), head:], do_t, 1, 0)
        return total, out + dot(cache[pl.ds(at, size), head:], rounded, 0, 0)

    total, out = each(weights_of, (jnp.zeros((8, rows), F32), jnp.zeros((head, rows), F32)))
    inverse = 1.0 / jnp.sum(total, axis=0, keepdims=True)
    out = (out * inverse).astype(BF16)
    row_dot = jnp.sum(out.astype(F32) * do_t.astype(F32), axis=0, keepdims=True)
    q_scaled = turned(q_t.astype(F32) * (inverse * scaling))
    do_scaled = turned(do_t.astype(F32) * inverse)

    def grads_of(piece, query_grad):
        cache, at, grad, to, row, size, _ = piece
        rounded = weight_ref[pl.ds(row, size), :]
        if slope_ref is not None:
            weight_grad = slope_ref[pl.ds(row, size), :]
        else:
            weight_grad = dot(cache[pl.ds(at, size), head:], do_t, 1, 0)
        score_grad = (rounded.astype(F32) * (weight_grad - row_dot)).astype(BF16)
        grad[pl.ds(to, size), :head] += dot(score_grad, q_scaled, 1, 0)
        grad[pl.ds(to, size), head:] += dot(rounded, do_scaled, 1, 0)
        return query_grad + dot(cache[pl.ds(at, size), :head], score_grad, 0, 0)

    query_grad = each(grads_of, jnp.zeros((head, rows), F32))
    return out, (query_grad * (inverse * scaling)).astype(BF16)


def leave_in_order(me, inner, rows_here, grad, sum_ref):
    for k in range(grad.shape[0] // rows_here):
        outer = lax.div(me, inner) if k < inner else 1 - lax.div(me, inner)
        place = outer * inner + lax.rem(lax.rem(me, inner) + (2 * inner - k), inner)
        at = pl.multiple_of(place * rows_here, rows_here)
        sum_ref[pl.ds(at, rows_here), :] = grad[k * rows_here : (k + 1) * rows_here, :].astype(BF16)


def prompt_kernel(scaling, inner, place_ref, q_ref, do_ref, *refs):
    caches, (carried_ref, out_ref, dq_ref, sum_ref, grad, score_ref, weight_ref) = refs[:-7], refs[-7:]
    length, rows_here = grad.shape[0], q_ref.shape[0]
    half = length // 2
    me_outer, me_inner = lax.div(place_ref[0], inner), lax.rem(place_ref[0], inner)
    grad[...] = carried_ref[...].astype(F32)

    def block(b, unused):
        here = pl.multiple_of(b * ROWS, ROWS)

        def causal(scores):
            keys = lax.broadcasted_iota(jnp.int32, scores.shape, 0)
            rows = here + lax.broadcasted_iota(jnp.int32, scores.shape, 1)
            return jnp.where(keys <= rows, scores, MASKED)

        def earlier(at, scores):
            keys = at + lax.broadcasted_iota(jnp.int32, scores.shape, 0)
            limit = rows_here * (me_inner + 1) if at < half else length * me_outer
            return jnp.where(keys < limit, scores, MASKED)

        pieces, at = [], 0
        for cache_ref in caches:
            begin = 0
            while begin < cache_ref.shape[0]:
                size = rows_here if at == 0 else min(CHUNK, cache_ref.shape[0] - begin)
                mask = causal if at == 0 else functools.partial(earlier, at)
                pieces.append((cache_ref, begin, grad, at, at, size, mask))
                at, begin = at + size, begin + size
        out, query_grad = run_block(
            turned(q_ref[pl.ds(here, ROWS), :]), turned(do_ref[pl.ds(here, ROWS), :]), scaling, pieces, None, score_ref, weight_ref
        )
        out_ref[pl.ds(here, ROWS), :] = turned(out)
        dq_ref[pl.ds(here, ROWS), :] = turned(query_grad)
        return unused

    lax.fori_loop(0, rows_here // ROWS, block, 0)
    leave_in_order(place_ref[0], inner, rows_here, grad, sum_ref)


def prompt_pass(place, inner, q, do, caches, carried, scaling):
    rows, head = q.shape
    length = carried.shape[0]
    return pl.pallas_call(
        functools.partial(prompt_kernel, scaling, inner),
        out_shape=[
            jax.ShapeDtypeStruct((rows, head), BF16),
            jax.ShapeDtypeStruct((rows, head), BF16),
            jax.ShapeDtypeStruct((length, 2 * head), BF16),
        ],
        in_specs=[pl.BlockSpec(memory_space=pltpu.SMEM)] + [pl.BlockSpec(memory_space=pltpu.VMEM)] * (3 + len(caches)),
        out_specs=[pl.BlockSpec(memory_space=pltpu.VMEM)] * 3,
        scratch_shapes=[
            pltpu.VMEM((length, 2 * head), F32),
            pltpu.VMEM((length, ROWS), F32),
            pltpu.VMEM((length, ROWS), BF16),
        ],
        compiler_params=pltpu.CompilerParams(vmem_limit_bytes=24 * 1024 * 1024),
        cost_estimate=pl.CostEstimate(flops=24 * rows * length * head, bytes_accessed=8 * length * head, transcendentals=0),
        name="prompt_pass",
    )(place, q, do, *caches, carried)


def reply_kernel(
    scaling, inner, other_count, scalars_ref, lengths_ref, owners_ref, q_ref, do_ref, own_ref, *refs
):
    (
        out_ref, dq_ref, other_sum_ref, mine_sum_ref, own_keep_ref, own_send_ref,
        picks_ref, q_t_ref, do_t_ref, results, grad, own_grad, score_ref, weight_ref, slope_ref,
    ) = refs[-15:]
    caches = refs[:-15]
    others, mines = caches[:other_count], caches[other_count:]
    capacity, head = q_ref.shape
    length = grad.shape[0]
    slots = lengths_ref.shape[0]
    window = capacity // 2

    starts, ranks, counts = [], [], []
    total = jnp.int32(0)
    edges = [total]
    for of_mine in (False, True):
        place_now = jnp.int32(0)
        for s in range(slots):
            taken = (owners_ref[s] == scalars_ref[1]) == of_mine
            count = jnp.where(taken, lengths_ref[s], 0)
            starts.append(place_now)
            ranks.append(total)
            counts.append(count)
            place_now = place_now + lengths_ref[s]
            total = total + count
        total = (total + ROWS - 1) // ROWS * ROWS
        edges.append(total)

    def located(rank_of):
        place = jnp.full(rank_of.shape, -1, jnp.int32)
        start = jnp.zeros(rank_of.shape, jnp.int32)
        for s in range(2 * slots):
            inside = (rank_of >= ranks[s]) & (rank_of < ranks[s] + counts[s])
            place = jnp.where(inside, rank_of + (starts[s] - ranks[s]), place)
            start = jnp.where(inside, starts[s], start)
        return place, start

    spread = q_t_ref.shape[1]
    place_all, _ = located(lax.broadcasted_iota(jnp.int32, (1, spread), 1))
    picks_ref[...] = jnp.where(
        lax.broadcasted_iota(jnp.int32, (capacity, spread), 0) == place_all, 1.0, 0.0
    ).astype(BF16)
    q_t_ref[...] = dot(turned(q_ref[...]), picks_ref[...], 1, 0).astype(BF16)
    do_t_ref[...] = dot(turned(do_ref[...]), picks_ref[...], 1, 0).astype(BF16)
    results[...] = jnp.zeros_like(results)
    own_grad[...] = jnp.zeros_like(own_grad)

    for parts, sum_ref, edge in ((others, other_sum_ref, 0), (mines, mine_sum_ref, 1)):
        grad[...] = jnp.zeros_like(grad)

        def block(b, unused):
            first_rank = pl.multiple_of(b * ROWS, ROWS)
            here = pl.ds(first_rank, ROWS)
            low, high = jnp.int32(capacity), jnp.int32(0)
            for s in range(2 * slots):
                begin = jnp.maximum(ranks[s], first_rank)
                end = jnp.minimum(ranks[s] + counts[s], first_rank + ROWS)
                some = begin < end
                low = jnp.where(some, jnp.minimum(low, starts[s]), low)
                high = jnp.where(some, jnp.maximum(high, end + (starts[s] - ranks[s])), high)
            low = (low // 32) * 32
            place, start = located(first_rank + lax.broadcasted_iota(jnp.int32, (1, ROWS), 1))

            def own_piece(w):
                begin = low + w * window
                at = pl.multiple_of(jnp.minimum(begin, capacity - window), 32)

                def packed(scores):
                    keys = at + lax.broadcasted_iota(jnp.int32, scores.shape, 0)
                    return jnp.where((keys >= jnp.maximum(start, begin)) & (keys <= place), scores, MASKED)

                return own_ref, at, own_grad, at, length + w * window, window, packed

            pieces, at = [], 0
            for cache_ref in parts:
                for begin in range(0, cache_ref.shape[0], CHUNK):
                    size = min(CHUNK, cache_ref.shape[0] - begin)
                    pieces.append((cache_ref, begin, grad, at, at, size, None))
                    at += size
            pieces.append(own_piece(0))
            extra = ((high - low + window - 1) // window, own_piece)
            out, query_grad = run_block(
                q_t_ref[:, here], do_t_ref[:, here], scaling, pieces, extra, score_ref, weight_ref, slope_ref
            )
            results[here, :head] = turned(out)
            results[here, head:] = turned(query_grad)
            return unused

        lax.fori_loop(edges[edge] // ROWS, edges[edge + 1] // ROWS, block, 0)
        if edge == 0:
            leave_in_order(scalars_ref[0], inner, length // (2 * inner), grad, sum_ref)
        else:
            sum_ref[...] = grad[...].astype(BF16)

    placed = dot(picks_ref[...], results[...], 1, 0).astype(BF16)
    out_ref[...] = placed[:, :head]
    dq_ref[...] = placed[:, head:]
    share = capacity // (2 * inner)
    me_outer, me_inner = lax.div(scalars_ref[0], inner), lax.rem(scalars_ref[0], inner)
    for k in range(inner):
        there = lax.rem(me_inner + k, inner)
        for outer, ref in ((me_outer, own_keep_ref), (1 - me_outer, own_send_ref)):
            at = pl.multiple_of((outer * inner + there) * share, share)
            ref[k * share : (k + 1) * share, :] = own_grad[pl.ds(at, share), :].astype(BF16)


def reply_pass(scalars, inner, lengths, owners, q, do, own, others, mines, scaling):
    capacity, head = q.shape
    length = sum(part.shape[0] for part in mines)
    spread = capacity + ROWS
    return pl.pallas_call(
        functools.partial(reply_kernel, scaling, inner, len(others)),
        out_shape=[
            jax.ShapeDtypeStruct((capacity, head), BF16),
            jax.ShapeDtypeStruct((capacity, head), BF16),
            jax.ShapeDtypeStruct((length, 2 * head), BF16),
            jax.ShapeDtypeStruct((length, 2 * head), BF16),
            jax.ShapeDtypeStruct((capacity // 2, 2 * head), BF16),
            jax.ShapeDtypeStruct((capacity // 2, 2 * head), BF16),
        ],
        in_specs=[pl.BlockSpec(memory_space=pltpu.SMEM)] * 3 + [pl.BlockSpec(memory_space=pltpu.VMEM)] * (3 + len(others) + len(mines)),
        out_specs=[pl.BlockSpec(memory_space=pltpu.VMEM)] * 6,
        scratch_shapes=[
            pltpu.VMEM((capacity, spread), BF16),
            pltpu.VMEM((head, spread), BF16),
            pltpu.VMEM((head, spread), BF16),
            pltpu.VMEM((spread, 2 * head), BF16),
            pltpu.VMEM((length, 2 * head), F32),
            pltpu.VMEM((capacity, 2 * head), F32),
            pltpu.VMEM((length + capacity, ROWS), F32),
            pltpu.VMEM((length + capacity, ROWS), BF16),
            pltpu.VMEM((length + capacity, ROWS), F32),
        ],
        compiler_params=pltpu.CompilerParams(vmem_limit_bytes=36 * 1024 * 1024),
        cost_estimate=pl.CostEstimate(flops=24 * capacity * length * head, bytes_accessed=16 * length * head, transcendentals=0),
        name="reply_pass",
    )(scalars, lengths, owners, q, do, own, *others, *mines)


def place_kernel(inner, first, place_ref, *refs):
    out_ref, halves = refs[-1], (refs[:first], refs[first:-1])
    share = out_ref.shape[0] // (2 * inner)
    me_outer, me_inner = lax.div(place_ref[0], inner), lax.rem(place_ref[0], inner)
    for outer, pieces in zip((me_outer, 1 - me_outer), halves):
        at = 0
        for ref in pieces:
            for begin in range(0, ref.shape[0], share):
                there = outer * inner + lax.rem(me_inner + (inner - at), inner)
                out_ref[pl.ds(pl.multiple_of(there * share, share), share), :] = ref[begin : begin + share, :]
                at += 1


def placed_in_order(place, inner, mine, other):
    rows = sum(x.shape[0] for x in mine)
    operands = [*mine, *other]
    return pl.pallas_call(
        functools.partial(place_kernel, inner, len(mine)),
        out_shape=jax.ShapeDtypeStruct((2 * rows, mine[0].shape[1]), BF16),
        in_specs=[pl.BlockSpec(memory_space=pltpu.SMEM)] + [pl.BlockSpec(memory_space=pltpu.VMEM)] * len(operands),
        out_specs=pl.BlockSpec(memory_space=pltpu.VMEM),
        compiler_params=pltpu.CompilerParams(vmem_limit_bytes=8 * 1024 * 1024),
        name="placed_in_order",
    )(place, *operands)


def join_kernel(total_ref, arrived_ref, keep_ref, came_ref, shares_ref, *pieces):
    shares_ref[...] = (total_ref[...].astype(F32) + arrived_ref[...].astype(F32)).astype(BF16)
    rows = pieces[0].shape[0]
    for k, ref in enumerate(pieces):
        at = slice(k * rows, (k + 1) * rows)
        ref[...] = (keep_ref[at, :].astype(F32) + came_ref[at, :].astype(F32)).astype(BF16)


def join(total, arrived, keep, came, count):
    rows, width = keep.shape
    return pl.pallas_call(
        join_kernel,
        out_shape=[jax.ShapeDtypeStruct(total.shape, BF16)]
        + [jax.ShapeDtypeStruct((rows // count, width), BF16)] * count,
        in_specs=[pl.BlockSpec(memory_space=pltpu.VMEM)] * 4,
        out_specs=[pl.BlockSpec(memory_space=pltpu.VMEM)] * (1 + count),
        compiler_params=pltpu.CompilerParams(vmem_limit_bytes=16 * 1024 * 1024),
        name="join_sums",
    )(total, arrived, keep, came)


def per_device(
    prompt_query,
    prompt_cache,
    prompt_cotangent,
    reply_query,
    reply_cache,
    reply_cotangent,
    reply_lengths,
    reply_owner,
):
    width = prompt_cache.shape[2]
    scaling = (width // 2) ** (-0.5)
    capacity = reply_query.shape[0]
    ctx_count, comp_count, group_count = (lax.axis_size(name) for name in ("ctx", "comp", "grp"))
    inner, comp_inner = ctx_count // 2, comp_count // 2
    place = lax.axis_index("ctx").astype(jnp.int32).reshape(1)
    group = lax.axis_index("grp").astype(jnp.int32).reshape(1)

    def swap(x):
        return lax.ppermute(x, "grp", [(0, 1), (1, 0)])

    def along_z(x, k):
        pairs = [(i, i // inner * inner + (i + k) % inner) for i in range(ctx_count)]
        return lax.ppermute(x, "ctx", pairs)

    def outer_swap(x):
        return lax.ppermute(x, "ctx", [(i, (i + inner) % ctx_count) for i in range(ctx_count)])

    def along_y(x, k):
        pairs = []
        for ctx in range(ctx_count):
            for comp in range(comp_count):
                y = (2 * (comp // comp_inner) + ctx // inner + k) % 4
                to_ctx = y % 2 * inner + ctx % inner
                to_comp = y // 2 * comp_inner + comp % comp_inner
                pairs.append((ctx * comp_count + comp, to_ctx * comp_count + to_comp))
        return lax.ppermute(x, ("ctx", "comp"), pairs)

    with jax.named_scope("gather_keys"):
        own = prompt_cache[0]
        next_1, next_3, next_2 = along_z(own, 1), along_z(own, inner - 1), along_z(own, 2)
        y_0 = along_y(own, 1)
        y_1, y_3 = along_y(next_1, 1), along_y(next_3, -1)
        half = own.shape[0] // 2
        y_2a, y_2b = along_y(next_2[:half], 1), along_y(next_2[half:], -1)
        mines = [own, next_1, next_2, next_3, y_0, y_1, y_2a, y_2b, y_3]
        others = [swap(jnp.concatenate(part, axis=0)) for part in (mines[:inner], mines[inner:])]

    with jax.named_scope("reply_rows"):
        reply_out, reply_dq, other_sum, mine_sum, own_keep, own_send = reply_pass(
            jnp.concatenate([place, group]), inner, reply_lengths[0], reply_owner[0], reply_query, reply_cotangent, reply_cache,
            others, mines, scaling,
        )
    arrived = swap(other_sum)
    with jax.named_scope("prompt_rows"):
        prompt_out, prompt_dq, total = prompt_pass(
            place, inner, prompt_query[0], prompt_cotangent[0], mines, mine_sum, scaling
        )

    with jax.named_scope("prompt_cache_sum"):
        count = ctx_count * comp_count
        shares, *pieces = join(total, arrived, own_keep, outer_swap(own_send), inner)
        terms = lax.all_to_all(shares.reshape(count, -1, width), ("ctx", "comp"), 0, 0, tiled=True)
    with jax.named_scope("reply_cache_sum"):
        part = pieces[0].astype(F32)
        for k in range(1, inner):
            part = part + along_z(pieces[k], k).astype(F32)
        part = part.astype(BF16)
        mine_half = jnp.concatenate([part] + [along_z(part, k) for k in range(1, inner)], axis=0)
        reply_grad = placed_in_order(place, inner, [mine_half], [outer_swap(mine_half)])
    with jax.named_scope("prompt_cache_halves"):
        summed = jnp.sum(terms.astype(F32), axis=0).astype(BF16)
        rows = summed.shape[0] // group_count
        first, second = summed[:rows], summed[rows:]
        is_first = group[0] == 0
        kept = jnp.where(is_first, first, second)
        came = swap(jnp.where(is_first, second, first))
        prompt_grad = jnp.where(is_first, jnp.stack([kept, came]), jnp.stack([came, kept]))
    return (
        prompt_out[None],
        prompt_dq[None],
        prompt_grad,
        reply_out,
        reply_dq,
        reply_grad,
    )


def solution(mesh):
    return jax.shard_map(
        per_device,
        mesh=mesh,
        in_specs=(
            P("grp", "ctx", "comp"),
            P("grp", "ctx", None),
            P("grp", "ctx", "comp"),
            P(("comp", "grp"), "ctx"),
            P(("comp", "grp"), None),
            P(("comp", "grp"), "ctx"),
            P(("comp", "grp"), None),
            P(("comp", "grp"), None),
        ),
        out_specs=(
            P("grp", "ctx", "comp"),
            P("grp", "ctx", "comp"),
            P(None, ("ctx", "comp", "grp"), None),
            P(("comp", "grp"), "ctx"),
            P(("comp", "grp"), "ctx"),
            P(("comp", "grp"), None),
        ),
        check_vma=False,
    )
```

time: 189 us -> 130 us (0.69)
  the two profiles are of different devices: /device:TPU:1 before, /device:TPU:4 now
where the time goes in v2:
time: 130 us; the launch traced here: 129 us
  starting transfers between devices  45.6 us (35%)
  waiting for transfers between devices  43.4 us (33%)
  Pallas kernels  30.7 us (24%)
  local copies, waits for them, and re-layouts  5.54 us (4%)
  other arithmetic  3.06 us (2%)
    ppermute x9, waiting for transfers between devices, along_z(): return lax.ppermute(x, 'ctx', pairs)  31.5 us
    pallas_call x1, Pallas kernels, reply_pass(): pl.pallas_call(functools.partial(reply_kernel, scaling, inner, len(others...  17.2 us
    ppermute x9, starting transfers between devices, along_z(): return lax.ppermute(x, 'ctx', pairs)  16.1 us
    pallas_call x1, Pallas kernels, prompt_pass(): pl.pallas_call(functools.partial(prompt_kernel, scaling, inner), out_shap...  10.8 us
    all_to_all x1, starting transfers between devices, per_device(): lax.all_to_all(shares.reshape(count, -1, width), ('ctx', 'comp'), 0, 0, t...  9.02 us
    ppermute x4, starting transfers between devices, swap(): return lax.ppermute(x, 'grp', [(0, 1), (1, 0)])  9 us
    ppermute x5, starting transfers between devices, along_y(): return lax.ppermute(x, ('ctx', 'comp'), pairs)  8.52 us
    ppermute x2, waiting for transfers between devices, outer_swap(): lax.ppermute(x, 'ctx', [(i, (i + inner) % ctx_count) for i in range(ctx_c...  5.31 us
  transfers between devices with their start and end apart: 21, of which 10 were waited for; matrix products, arithmetic and copies ran while one was open for 5% of the time, Pallas kernels for 9%

profile of v2, /device:TPU:4, one launch (start us, length us, event | category | flops | bytes accessed | tf_op | source)
XLA Modules:
  0.0 129.1 jit_solution(3345641794546438633)
XLA Ops:
  0.6 4.0 %collective-permute-start.1 = (bf16[512,256]{1,0:T(8,128)(2,1)}, bf16[512,256]{1,0:T(8,128)(2,1)S(1)}, u32[]{:S(2)}, u32[]{:S(2)}) collective-permute-start(bf16[512,256]{1,0:T(8,128)(2,1)} %bitcast.13), channel_id=1, source_target_pairs={{0,32},{16,48},{32,0},{48,16},{64,96},{80,112},{96,64},{112,80},{1... | collective-permute-start | bytes 786440 | tf_op jit(solution)/shard_map/gather_keys/ppermute | solution.py:362
  4.6 1.0 collective-permute-start
  5.6 2.2 %collective-permute-start.2 = (bf16[512,256]{1,0:T(8,128)(2,1)}, bf16[512,256]{1,0:T(8,128)(2,1)S(1)}, u32[]{:S(2)}, u32[]{:S(2)}) collective-permute-start(bf16[512,256]{1,0:T(8,128)(2,1)} %bitcast.15), channel_id=1, source_target_pairs={{0,48},{16,0},{32,16},{48,32},{64,112},{80,64},{96,80},{112,96},{1... | collective-permute-start | bytes 786440 | tf_op jit(solution)/shard_map/gather_keys/ppermute | solution.py:362
  7.8 1.6 %collective-permute-start.3 = (bf16[512,256]{1,0:T(8,128)(2,1)}, bf16[512,256]{1,0:T(8,128)(2,1)S(1)}, u32[]{:S(2)}, u32[]{:S(2)}) collective-permute-start(bf16[512,256]{1,0:T(8,128)(2,1)} %bitcast.16), channel_id=1, source_target_pairs={{0,64},{2,66},{4,68},{6,70},{8,72},{10,74},{12,76},{14,78},{16,80}... | collective-permute-start | bytes 786440 | tf_op jit(solution)/shard_map/gather_keys/ppermute | solution.py:375
  9.4 2.6 %collective-permute-done.1.refs_4_.refs_2_ = bf16[512,256]{1,0:T(8,128)(2,1)S(1)} collective-permute-done((bf16[512,256]{1,0:T(8,128)(2,1)}, bf16[512,256]{1,0:T(8,128)(2,1)S(1)}, u32[]{:S(2)}, u32[]{:S(2)}) %collective-permute-start.1) | collective-permute-done | bytes 262176 | tf_op jit(solution)/shard_map/gather_keys/ppermute | solution.py:362
  12.0 3.1 %collective-permute-start.6 = (bf16[256,256]{1,0:T(8,128)(2,1)S(1)}, bf16[256,256]{1,0:T(8,128)(2,1)S(1)}, u32[]{:S(2)}, u32[]{:S(2)}) collective-permute-start(bf16[256,256]{1,0:T(8,128)(2,1)S(1)} %get-tuple-element.34), channel_id=1, source_target_pairs={{0,72},{2,74},{4,76},{6,78},{8,64},{10,66},{12,68},{14,70},{16,88}... | collective-permute-start | bytes 393224 | tf_op jit(solution)/shard_map/gather_keys/ppermute | solution.py:375
  15.2 1.5 %collective-permute-done.refs_3_.refs_1_ = bf16[512,256]{1,0:T(8,128)(2,1)S(1)} collective-permute-done((bf16[512,256]{1,0:T(8,128)(2,1)}, bf16[512,256]{1,0:T(8,128)(2,1)S(1)}, u32[]{:S(2)}, u32[]{:S(2)}) %collective-permute-start) | collective-permute-done | bytes 262176 | tf_op jit(solution)/shard_map/gather_keys/ppermute | solution.py:362
  16.7 1.6 %collective-permute-start.4 = (bf16[512,256]{1,0:T(8,128)(2,1)S(1)}, bf16[512,256]{1,0:T(8,128)(2,1)S(1)}, u32[]{:S(2)}, u32[]{:S(2)}) collective-permute-start(bf16[512,256]{1,0:T(8,128)(2,1)S(1)} %collective-permute-done.refs_3_.refs_1_), channel_id=1, source_target_pairs={{0,64},{2,66},{4,68},{6,70},{8,72},{10,74},{12,76},{14,78},{16,80}... | collective-permute-start | bytes 786440 | tf_op jit(solution)/shard_map/gather_keys/ppermute | solution.py:375
  18.3 2.0 %pad_maximum_fusion = bf16[2048,256]{1,0:T(8,128)(2,1)} fusion(bf16[512,256]{1,0:T(8,128)(2,1)S(1)} %collective-permute-done.2.refs_5_.refs_3_, bf16[512,256]{1,0:T(8,128)(2,1)S(1)} %collective-permute-done.1.refs_4_.refs_2_, bf16[512,256]{1,0:T(8,128)(2,1)S(1)} %collective-permute-done.refs_3_.refs_1_, bf16[512,256]{1,0:T(8,128)(2,1)} %bitcast.17), kind=kLoop, calls=%fused_computation | loop fusion | flops 4194304 | bytes 2097152 | tf_op jit(solution)/shard_map/gather_keys/concatenate | solution.py:385
  20.3 2.2 %collective-permute-start.7 = (bf16[512,256]{1,0:T(8,128)(2,1)S(1)}, bf16[512,256]{1,0:T(8,128)(2,1)S(1)}, u32[]{:S(2)}, u32[]{:S(2)}) collective-permute-start(bf16[512,256]{1,0:T(8,128)(2,1)S(1)} %collective-permute-done.2.refs_5_.refs_3_), channel_id=1, source_target_pairs={{0,72},{2,74},{4,76},{6,78},{8,64},{10,66},{12,68},{14,70},{16,88}... | collective-permute-start | bytes 786440 | tf_op jit(solution)/shard_map/gather_keys/ppermute | solution.py:375
  23.2 3.7 %collective-permute-done.4.refs_7_.refs_5_ = bf16[512,256]{1,0:T(8,128)(2,1)S(1)} collective-permute-done((bf16[512,256]{1,0:T(8,128)(2,1)S(1)}, bf16[512,256]{1,0:T(8,128)(2,1)S(1)}, u32[]{:S(2)}, u32[]{:S(2)}) %collective-permute-start.4) | collective-permute-done | bytes 262176 | tf_op jit(solution)/shard_map/gather_keys/ppermute | solution.py:375
  29.8 2.9 %collective-permute-done.9.refs_1_ = bf16[2048,256]{1,0:T(8,128)(2,1)} collective-permute-done((bf16[2048,256]{1,0:T(8,128)(2,1)}, bf16[2048,256]{1,0:T(8,128)(2,1)}, u32[]{:S(2)}, u32[]{:S(2)}) %collective-permute-start.9) | collective-permute-done | bytes 1048608 | tf_op jit(solution)/shard_map/gather_keys/ppermute | solution.py:358
  32.8 1.0 copy-done.1
  33.8 0.9 copy-done.3
  34.8 17.2 %reply_pass.1 = (bf16[1024,128]{1,0:T(8,128)(2,1)}, bf16[1024,128]{1,0:T(8,128)(2,1)}, bf16[4096,256]{1,0:T(8,128)(2,1)S(1)}, bf16[4096,256]{1,0:T(8,128)(2,1)S(...) custom-call(s32[2]{0:T(128)S(1)} %pad_add_fusion.scalars_ref, s32[4]{0:T(128)S(1)} %bitcast.22, ...), custom_call_target="tpu_custom_call" | custom-call | flops 12884901888 | bytes 8388608 | tf_op jit(solution)/shard_map/reply_rows/reply_pass/pallas_call | solution.py:263
  52.0 8.9 %collective-permute-start.10 = (bf16[4096,256]{1,0:T(8,128)(2,1)S(1)}, bf16[4096,256]{1,0:T(8,128)(2,1)S(1)}, u32[]{:S(2)}, u32[]{:S(2)}) collective-permute-start(bf16[4096,256]{1,0:T(8,128)(2,1)S(1)} %get-tuple-element.24), channel_id=1, source_target_pairs={{0,1},{1,0},{2,3},{3,2},{4,5},{5,4},{6,7},{7,6},{8,9},{9,8},{10,11... | collective-permute-start | bytes 6291464 | tf_op jit(solution)/shard_map/ppermute | solution.py:358
  60.9 1.6 %collective-permute-start.11 = (bf16[512,256]{1,0:T(8,128)(2,1)S(1)}, bf16[512,256]{1,0:T(8,128)(2,1)S(1)}, u32[]{:S(2)}, u32[]{:S(2)}) collective-permute-start(bf16[512,256]{1,0:T(8,128)(2,1)S(1)} %get-tuple-element.26), channel_id=1, source_target_pairs={{0,64},{16,80},{32,96},{48,112},{64,0},{80,16},{96,32},{112,48},{1... | collective-permute-start | bytes 786440 | tf_op jit(solution)/shard_map/prompt_cache_sum/ppermute | solution.py:365
  62.5 10.8 %prompt_pass.1 = (bf16[512,128]{1,0:T(8,128)(2,1)}, bf16[512,128]{1,0:T(8,128)(2,1)}, bf16[4096,256]{1,0:T(8,128)(2,1)S(1)}) custom-call(s32[1]{0:T(128)} %bitcast.place_ref, bf16[512,128]{1,0:T(8,128)(2,1)S(1)} %bitcast.20, bf16[512,128]{1,0:T(8,128)(2,1)S(1)} %bitcast.21, bf16[512,256]{1,0:T(8,128)(2,1)S(1)} %bitcast.19, ...), custom_call_target="tpu_custom_call" | custom-call | flops 6442450944 | bytes 4194304 | tf_op jit(solution)/shard_map/prompt_rows/prompt_pass/pallas_call | solution.py:131
  73.3 1.8 %join_sums.1 = (bf16[4096,256]{1,0:T(8,128)(2,1)}, bf16[128,256]{1,0:T(8,128)(2,1)S(1)}, bf16[128,256]{1,0:T(8,128)(2,1)S(1)}, bf16[128,256]{1,0:T(8,128)(2,1)S(1)}, bf16[128,256]{1,0:T(8,128)(2,1)S(1)}) custom-call(bf16[4096,256]{1,0:T(8,128)(2,1)S(1)} %get-tuple-element.23.total_ref, bf16[4096,256]{1,0:T(8,128)(2,1)S(1)} %collective-permute-done.10.arrived_ref, ...), custom_call_target="tpu_custom_call" | custom-call | tf_op jit(solution)/shard_map/prompt_cache_sum/join_sums/pallas_call | solution.py:328
  75.1 9.0 %all-to-all-start = ((bf16[64,64,256]{2,1,0:T(8,128)(2,1)}), bf16[64,64,256]{2,1,0:T(8,128)(2,1)S(1)}, u32[]{:S(2)}, u32[]{:S(2)}) async-start(bf16[64,64,256]{2,1,0:T(8,128)(2,1)} %bitcast.9), calls=%async_computation | async-start | bytes 4194304 | tf_op jit(solution)/shard_map/prompt_cache_sum/all_to_all | solution.py:401
  84.2 1.5 %collective-permute-start.13 = (bf16[128,256]{1,0:T(8,128)(2,1)S(1)}, bf16[128,256]{1,0:T(8,128)(2,1)S(1)}, u32[]{:S(2)}, u32[]{:S(2)}) collective-permute-start(bf16[128,256]{1,0:T(8,128)(2,1)S(1)} %get-tuple-element.31), channel_id=1, source_target_pairs={{0,16},{16,32},{32,48},{48,0},{64,80},{80,96},{96,112},{112,64},{1... | collective-permute-start | bytes 196616 | tf_op jit(solution)/shard_map/reply_cache_sum/ppermute | solution.py:362
  85.7 2.7 %collective-permute-start.14 = (bf16[128,256]{1,0:T(8,128)(2,1)S(1)}, bf16[128,256]{1,0:T(8,128)(2,1)S(1)}, u32[]{:S(2)}, u32[]{:S(2)}) collective-permute-start(bf16[128,256]{1,0:T(8,128)(2,1)S(1)} %get-tuple-element.32), channel_id=1, source_target_pairs={{0,32},{16,48},{32,0},{48,16},{64,96},{80,112},{96,64},{112,80},{1... | collective-permute-start | bytes 196616 | tf_op jit(solution)/shard_map/reply_cache_sum/ppermute | solution.py:362
  88.4 1.4 %collective-permute-start.15 = (bf16[128,256]{1,0:T(8,128)(2,1)S(1)}, bf16[128,256]{1,0:T(8,128)(2,1)S(1)}, u32[]{:S(2)}, u32[]{:S(2)}) collective-permute-start(bf16[128,256]{1,0:T(8,128)(2,1)S(1)} %get-tuple-element.33), channel_id=1, source_target_pairs={{0,48},{16,0},{32,16},{48,32},{64,112},{80,64},{96,80},{112,96},{1... | collective-permute-start | bytes 196616 | tf_op jit(solution)/shard_map/reply_cache_sum/ppermute | solution.py:362
  89.8 20.4 %collective-permute-done.13 = bf16[128,256]{1,0:T(8,128)(2,1)S(1)} collective-permute-done((bf16[128,256]{1,0:T(8,128)(2,1)S(1)}, bf16[128,256]{1,0:T(8,128)(2,1)S(1)}, u32[]{:S(2)}, u32[]{:S(2)}) %collective-permute-start.13) | collective-permute-done | bytes 65568 | tf_op jit(solution)/shard_map/reply_cache_sum/ppermute | solution.py:362
  110.3 2.4 %collective-permute-done.14 = bf16[128,256]{1,0:T(8,128)(2,1)S(1)} collective-permute-done((bf16[128,256]{1,0:T(8,128)(2,1)S(1)}, bf16[128,256]{1,0:T(8,128)(2,1)S(1)}, u32[]{:S(2)}, u32[]{:S(2)}) %collective-permute-start.14) | collective-permute-done | bytes 65568 | tf_op jit(solution)/shard_map/reply_cache_sum/ppermute | solution.py:362
  112.7 1.1 collective-permute-start.18
  113.8 1.1 collective-permute-start.17
  114.9 1.0 collective-permute-start.16
  115.9 1.7 %collective-permute-done.18 = bf16[128,256]{1,0:T(8,128)(2,1)S(1)} collective-permute-done((bf16[128,256]{1,0:T(8,128)(2,1)S(1)}, bf16[128,256]{1,0:T(8,128)(2,1)S(1)}, u32[]{:S(2)}, u32[]{:S(2)}) %collective-permute-start.18) | collective-permute-done | bytes 65568 | tf_op jit(solution)/shard_map/reply_cache_sum/ppermute | solution.py:362
  117.6 2.1 %collective-permute-done.17 = bf16[128,256]{1,0:T(8,128)(2,1)S(1)} collective-permute-done((bf16[128,256]{1,0:T(8,128)(2,1)S(1)}, bf16[128,256]{1,0:T(8,128)(2,1)S(1)}, u32[]{:S(2)}, u32[]{:S(2)}) %collective-permute-start.17) | collective-permute-done | bytes 65568 | tf_op jit(solution)/shard_map/reply_cache_sum/ppermute | solution.py:362
  120.5 1.4 %collective-permute-start.19 = (bf16[512,256]{1,0:T(8,128)(2,1)S(1)}, bf16[512,256]{1,0:T(8,128)(2,1)S(1)}, u32[]{:S(2)}, u32[]{:S(2)}) collective-permute-start(bf16[512,256]{1,0:T(8,128)(2,1)S(1)} %pad_maximum_fusion.1.refs_0_), channel_id=1, source_target_pairs={{0,64},{16,80},{32,96},{48,112},{64,0},{80,16},{96,32},{112,48},{1... | collective-permute-start | bytes 786440 | tf_op jit(solution)/shard_map/reply_cache_sum/ppermute | solution.py:365
  122.3 5.3 %collective-permute-done.19.refs_1_ = bf16[512,256]{1,0:T(8,128)(2,1)S(1)} collective-permute-done((bf16[512,256]{1,0:T(8,128)(2,1)S(1)}, bf16[512,256]{1,0:T(8,128)(2,1)S(1)}, u32[]{:S(2)}, u32[]{:S(2)}) %collective-permute-start.19) | collective-permute-done | bytes 262176 | tf_op jit(solution)/shard_map/reply_cache_sum/ppermute | solution.py:365
  (43 shorter events, 6.4 us)
Async XLA Ops:
  0.6 11.3 %collective-permute-start.1 = (bf16[512,256]{1,0:T(8,128)(2,1)}, bf16[512,256]{1,0:T(8,128)(2,1)S(1)}, u32[]{:S(2)}, u32[]{:S(2)}) collective-permute-start(bf16[512,256]{1,0:T(8,128)(2,1)} %bitcast.13), channel_id=1, source_target_pairs={{0,32},{16,48},{32,0},{48,16},{64,96},{80,112},{96,64},{112,80},{1... | collective-permute-start | bytes 786440 | tf_op jit(solution)/shard_map/gather_keys/ppermute | solution.py:362
  4.6 12.1 %collective-permute-start = (bf16[512,256]{1,0:T(8,128)(2,1)}, bf16[512,256]{1,0:T(8,128)(2,1)S(1)}, u32[]{:S(2)}, u32[]{:S(2)}) collective-permute-start(bf16[512,256]{1,0:T(8,128)(2,1)} %bitcast.14), channel_id=1, source_target_pairs={{0,16},{16,32},{32,48},{48,0},{64,80},{80,96},{96,112},{112,64},{1... | collective-permute-start | bytes 786440 | tf_op jit(solution)/shard_map/gather_keys/ppermute | solution.py:362
  5.6 12.7 %collective-permute-start.2 = (bf16[512,256]{1,0:T(8,128)(2,1)}, bf16[512,256]{1,0:T(8,128)(2,1)S(1)}, u32[]{:S(2)}, u32[]{:S(2)}) collective-permute-start(bf16[512,256]{1,0:T(8,128)(2,1)} %bitcast.15), channel_id=1, source_target_pairs={{0,48},{16,0},{32,16},{48,32},{64,112},{80,64},{96,80},{112,96},{1... | collective-permute-start | bytes 786440 | tf_op jit(solution)/shard_map/gather_keys/ppermute | solution.py:362
  7.8 12.5 %collective-permute-start.3 = (bf16[512,256]{1,0:T(8,128)(2,1)}, bf16[512,256]{1,0:T(8,128)(2,1)S(1)}, u32[]{:S(2)}, u32[]{:S(2)}) collective-permute-start(bf16[512,256]{1,0:T(8,128)(2,1)} %bitcast.16), channel_id=1, source_target_pairs={{0,64},{2,66},{4,68},{6,70},{8,72},{10,74},{12,76},{14,78},{16,80}... | collective-permute-start | bytes 786440 | tf_op jit(solution)/shard_map/gather_keys/ppermute | solution.py:375
  12.0 16.4 %collective-permute-start.6 = (bf16[256,256]{1,0:T(8,128)(2,1)S(1)}, bf16[256,256]{1,0:T(8,128)(2,1)S(1)}, u32[]{:S(2)}, u32[]{:S(2)}) collective-permute-start(bf16[256,256]{1,0:T(8,128)(2,1)S(1)} %get-tuple-element.34), channel_id=1, source_target_pairs={{0,72},{2,74},{4,76},{6,78},{8,64},{10,66},{12,68},{14,70},{16,88}... | collective-permute-start | bytes 393224 | tf_op jit(solution)/shard_map/gather_keys/ppermute | solution.py:375
  15.1 17.7 %copy-start = (bf16[1,512,256]{2,1,0:T(8,128)(2,1)S(1)}, bf16[1,512,256]{2,1,0:T(8,128)(2,1)}, u32[]{:S(2)}) copy-start(bf16[1,512,256]{2,1,0:T(8,128)(2,1)} %param.9) | copy-start | bytes 786436
  15.1 17.7 %copy-start.2 = (bf16[1024,128]{1,0:T(8,128)(2,1)S(1)}, bf16[1024,128]{1,0:T(8,128)(2,1)}, u32[]{:S(2)}) copy-start(bf16[1024,128]{1,0:T(8,128)(2,1)} %q_ref.1) | copy-start | bytes 786436
  15.1 17.7 %copy-start.6 = (s32[1,4]{1,0:T(1,128)S(1)}, s32[1,4]{1,0:T(1,128)}, u32[]{:S(2)}) copy-start(s32[1,4]{1,0:T(1,128)} %param.14) | copy-start | bytes 52
  15.1 17.7 %copy-start.7 = (s32[1,4]{1,0:T(1,128)S(1)}, s32[1,4]{1,0:T(1,128)}, u32[]{:S(2)}) copy-start(s32[1,4]{1,0:T(1,128)} %param.15) | copy-start | bytes 52
  15.1 12.6 %collective-permute-start.5 = (bf16[256,256]{1,0:T(8,128)(2,1)S(1)}, bf16[256,256]{1,0:T(8,128)(2,1)S(1)}, u32[]{:S(2)}, u32[]{:S(2)}) collective-permute-start(bf16[256,256]{1,0:T(8,128)(2,1)S(1)} %get-tuple-element.35), channel_id=1, source_target_pairs={{0,64},{2,66},{4,68},{6,70},{8,72},{10,74},{12,76},{14,78},{16,80}... | collective-permute-start | bytes 393224 | tf_op jit(solution)/shard_map/gather_keys/ppermute | solution.py:375
  16.7 10.2 %collective-permute-start.4 = (bf16[512,256]{1,0:T(8,128)(2,1)S(1)}, bf16[512,256]{1,0:T(8,128)(2,1)S(1)}, u32[]{:S(2)}, u32[]{:S(2)}) collective-permute-start(bf16[512,256]{1,0:T(8,128)(2,1)S(1)} %collective-permute-done.refs_3_.refs_1_), channel_id=1, source_target_pairs={{0,64},{2,66},{4,68},{6,70},{8,72},{10,74},{12,76},{14,78},{16,80}... | collective-permute-start | bytes 786440 | tf_op jit(solution)/shard_map/gather_keys/ppermute | solution.py:375
  20.3 9.5 %collective-permute-start.8 = (bf16[2048,256]{1,0:T(8,128)(2,1)}, bf16[2048,256]{1,0:T(8,128)(2,1)S(1)}, u32[]{:S(2)}, u32[]{:S(2)}) collective-permute-start(bf16[2048,256]{1,0:T(8,128)(2,1)} %pad_maximum_fusion), channel_id=1, source_target_pairs={{0,1},{1,0},{2,3},{3,2},{4,5},{5,4},{6,7},{7,6},{8,9},{9,8},{10,11... | collective-permute-start | bytes 3145736 | tf_op jit(solution)/shard_map/gather_keys/ppermute | solution.py:358
  20.3 8.7 %collective-permute-start.7 = (bf16[512,256]{1,0:T(8,128)(2,1)S(1)}, bf16[512,256]{1,0:T(8,128)(2,1)S(1)}, u32[]{:S(2)}, u32[]{:S(2)}) collective-permute-start(bf16[512,256]{1,0:T(8,128)(2,1)S(1)} %collective-permute-done.2.refs_5_.refs_3_), channel_id=1, source_target_pairs={{0,72},{2,74},{4,76},{6,78},{8,64},{10,66},{12,68},{14,70},{16,88}... | collective-permute-start | bytes 786440 | tf_op jit(solution)/shard_map/gather_keys/ppermute | solution.py:375
  29.8 3.0 %collective-permute-start.9 = (bf16[2048,256]{1,0:T(8,128)(2,1)}, bf16[2048,256]{1,0:T(8,128)(2,1)}, u32[]{:S(2)}, u32[]{:S(2)}) collective-permute-start(bf16[2048,256]{1,0:T(8,128)(2,1)} %constant_dynamic-update-slice_fusion), channel_id=1, source_target_pairs={{0,1},{1,0},{2,3},{3,2},{4,5},{5,4},{6,7},{7,6},{8,9},{9,8},{10,11... | collective-permute-start | bytes 3145736 | tf_op jit(solution)/shard_map/gather_keys/ppermute | solution.py:358
  32.8 1.0 copy-start.1
  33.8 0.9 copy-start.3
  34.8 27.7 %copy-start.4 = (bf16[1,512,128]{2,1,0:T(8,128)(2,1)S(1)}, bf16[1,512,128]{2,1,0:T(8,128)(2,1)}, u32[]{:S(2)}) copy-start(bf16[1,512,128]{2,1,0:T(8,128)(2,1)} %param.8) | copy-start | bytes 393220
  34.8 27.7 %copy-start.5 = (bf16[1,512,128]{2,1,0:T(8,128)(2,1)S(1)}, bf16[1,512,128]{2,1,0:T(8,128)(2,1)}, u32[]{:S(2)}) copy-start(bf16[1,512,128]{2,1,0:T(8,128)(2,1)} %param.10) | copy-start | bytes 393220
  52.0 21.3 %collective-permute-start.10 = (bf16[4096,256]{1,0:T(8,128)(2,1)S(1)}, bf16[4096,256]{1,0:T(8,128)(2,1)S(1)}, u32[]{:S(2)}, u32[]{:S(2)}) collective-permute-start(bf16[4096,256]{1,0:T(8,128)(2,1)S(1)} %get-tuple-element.24), channel_id=1, source_target_pairs={{0,1},{1,0},{2,3},{3,2},{4,5},{5,4},{6,7},{7,6},{8,9},{9,8},{10,11... | collective-permute-start | bytes 6291464 | tf_op jit(solution)/shard_map/ppermute | solution.py:358
  60.9 12.4 %collective-permute-start.11 = (bf16[512,256]{1,0:T(8,128)(2,1)S(1)}, bf16[512,256]{1,0:T(8,128)(2,1)S(1)}, u32[]{:S(2)}, u32[]{:S(2)}) collective-permute-start(bf16[512,256]{1,0:T(8,128)(2,1)S(1)} %get-tuple-element.26), channel_id=1, source_target_pairs={{0,64},{16,80},{32,96},{48,112},{64,0},{80,16},{96,32},{112,48},{1... | collective-permute-start | bytes 786440 | tf_op jit(solution)/shard_map/prompt_cache_sum/ppermute | solution.py:365
  75.1 46.8 %all-to-all-start = ((bf16[64,64,256]{2,1,0:T(8,128)(2,1)}), bf16[64,64,256]{2,1,0:T(8,128)(2,1)S(1)}, u32[]{:S(2)}, u32[]{:S(2)}) async-start(bf16[64,64,256]{2,1,0:T(8,128)(2,1)} %bitcast.9), calls=%async_computation | async-start | bytes 4194304 | tf_op jit(solution)/shard_map/prompt_cache_sum/all_to_all | solution.py:401
  84.2 26.1 %collective-permute-start.13 = (bf16[128,256]{1,0:T(8,128)(2,1)S(1)}, bf16[128,256]{1,0:T(8,128)(2,1)S(1)}, u32[]{:S(2)}, u32[]{:S(2)}) collective-permute-start(bf16[128,256]{1,0:T(8,128)(2,1)S(1)} %get-tuple-element.31), channel_id=1, source_target_pairs={{0,16},{16,32},{32,48},{48,0},{64,80},{80,96},{96,112},{112,64},{1... | collective-permute-start | bytes 196616 | tf_op jit(solution)/shard_map/reply_cache_sum/ppermute | solution.py:362
  85.7 27.0 %collective-permute-start.14 = (bf16[128,256]{1,0:T(8,128)(2,1)S(1)}, bf16[128,256]{1,0:T(8,128)(2,1)S(1)}, u32[]{:S(2)}, u32[]{:S(2)}) collective-permute-start(bf16[128,256]{1,0:T(8,128)(2,1)S(1)} %get-tuple-element.32), channel_id=1, source_target_pairs={{0,32},{16,48},{32,0},{48,16},{64,96},{80,112},{96,64},{112,80},{1... | collective-permute-start | bytes 196616 | tf_op jit(solution)/shard_map/reply_cache_sum/ppermute | solution.py:362
  88.4 24.3 %collective-permute-start.15 = (bf16[128,256]{1,0:T(8,128)(2,1)S(1)}, bf16[128,256]{1,0:T(8,128)(2,1)S(1)}, u32[]{:S(2)}, u32[]{:S(2)}) collective-permute-start(bf16[128,256]{1,0:T(8,128)(2,1)S(1)} %get-tuple-element.33), channel_id=1, source_target_pairs={{0,48},{16,0},{32,16},{48,32},{64,112},{80,64},{96,80},{112,96},{1... | collective-permute-start | bytes 196616 | tf_op jit(solution)/shard_map/reply_cache_sum/ppermute | solution.py:362
  112.7 4.9 %collective-permute-start.18 = (bf16[128,256]{1,0:T(8,128)(2,1)S(1)}, bf16[128,256]{1,0:T(8,128)(2,1)S(1)}, u32[]{:S(2)}, u32[]{:S(2)}) collective-permute-start(bf16[128,256]{1,0:T(8,128)(2,1)S(1)} %add_convert_fusion), channel_id=1, source_target_pairs={{0,48},{16,0},{32,16},{48,32},{64,112},{80,64},{96,80},{112,96},{1... | collective-permute-start | bytes 196616 | tf_op jit(solution)/shard_map/reply_cache_sum/ppermute | solution.py:362
  113.8 5.9 %collective-permute-start.17 = (bf16[128,256]{1,0:T(8,128)(2,1)S(1)}, bf16[128,256]{1,0:T(8,128)(2,1)S(1)}, u32[]{:S(2)}, u32[]{:S(2)}) collective-permute-start(bf16[128,256]{1,0:T(8,128)(2,1)S(1)} %add_convert_fusion), channel_id=1, source_target_pairs={{0,32},{16,48},{32,0},{48,16},{64,96},{80,112},{96,64},{112,80},{1... | collective-permute-start | bytes 196616 | tf_op jit(solution)/shard_map/reply_cache_sum/ppermute | solution.py:362
  114.9 5.5 %collective-permute-start.16 = (bf16[128,256]{1,0:T(8,128)(2,1)S(1)}, bf16[128,256]{1,0:T(8,128)(2,1)S(1)}, u32[]{:S(2)}, u32[]{:S(2)}) collective-permute-start(bf16[128,256]{1,0:T(8,128)(2,1)S(1)} %add_convert_fusion), channel_id=1, source_target_pairs={{0,16},{16,32},{32,48},{48,0},{64,80},{80,96},{96,112},{112,64},{1... | collective-permute-start | bytes 196616 | tf_op jit(solution)/shard_map/reply_cache_sum/ppermute | solution.py:362
  120.5 7.1 %collective-permute-start.19 = (bf16[512,256]{1,0:T(8,128)(2,1)S(1)}, bf16[512,256]{1,0:T(8,128)(2,1)S(1)}, u32[]{:S(2)}, u32[]{:S(2)}) collective-permute-start(bf16[512,256]{1,0:T(8,128)(2,1)S(1)} %pad_maximum_fusion.1.refs_0_), channel_id=1, source_target_pairs={{0,64},{16,80},{32,96},{48,112},{64,0},{80,16},{96,32},{112,48},{1... | collective-permute-start | bytes 786440 | tf_op jit(solution)/shard_map/reply_cache_sum/ppermute | solution.py:365
  122.2 6.2 %collective-permute-start.12 = (bf16[32,256]{1,0:T(8,128)(2,1)S(1)}, bf16[32,256]{1,0:T(8,128)(2,1)S(1)}, u32[]{:S(2)}, u32[]{:S(2)}) collective-permute-start(bf16[32,256]{1,0:T(8,128)(2,1)S(1)} %get-tuple-element.37), channel_id=1, source_target_pairs={{0,1},{1,0},{2,3},{3,2},{4,5},{5,4},{6,7},{7,6},{8,9},{9,8},{10,11... | collective-permute-start | bytes 49160 | tf_op jit(solution)/shard_map/prompt_cache_halves/ppermute | solution.py:358

commit v3 on v2

--- a/solution.py
+++ b/solution.py
@@ -7,6 +7,7 @@
 from jax.sharding import PartitionSpec as P
 
 ROWS = 256
+PROMPT_ROWS = 512
 CHUNK = 512
 LOG2E = 1.4426950408889634
 MASKED = -1e30
@@ -78,12 +79,12 @@
     return out, (query_grad * (inverse * scaling)).astype(BF16)
 
 
-def leave_in_order(me, inner, rows_here, grad, sum_ref):
-    for k in range(grad.shape[0] // rows_here):
+def leave_in_order(me, inner, rows_here, order, grad, sum_ref):
+    for i, k in enumerate(order):
         outer = lax.div(me, inner) if k < inner else 1 - lax.div(me, inner)
         place = outer * inner + lax.rem(lax.rem(me, inner) + (2 * inner - k), inner)
         at = pl.multiple_of(place * rows_here, rows_here)
-        sum_ref[pl.ds(at, rows_here), :] = grad[k * rows_here : (k + 1) * rows_here, :].astype(BF16)
+        sum_ref[pl.ds(at, rows_here), :] = grad[i * rows_here : (i + 1) * rows_here, :].astype(BF16)
 
 
 def prompt_kernel(scaling, inner, place_ref, q_ref, do_ref, *refs):
@@ -94,7 +95,7 @@
     grad[...] = carried_ref[...].astype(F32)
 
     def block(b, unused):
-        here = pl.multiple_of(b * ROWS, ROWS)
+        here = pl.multiple_of(b * PROMPT_ROWS, PROMPT_ROWS)
 
         def causal(scores):
             keys = lax.broadcasted_iota(jnp.int32, scores.shape, 0)
@@ -115,14 +116,14 @@
                 pieces.append((cache_ref, begin, grad, at, at, size, mask))
                 at, begin = at + size, begin + size
         out, query_grad = run_block(
-            turned(q_ref[pl.ds(here, ROWS), :]), turned(do_ref[pl.ds(here, ROWS), :]), scaling, pieces, None, score_ref, weight_ref
+            turned(q_ref[pl.ds(here, PROMPT_ROWS), :]), turned(do_ref[pl.ds(here, PROMPT_ROWS), :]), scaling, pieces, None, score_ref, weight_ref
         )
-        out_ref[pl.ds(here, ROWS), :] = turned(out)
-        dq_ref[pl.ds(here, ROWS), :] = turned(query_grad)
+        out_ref[pl.ds(here, PROMPT_ROWS), :] = turned(out)
+        dq_ref[pl.ds(here, PROMPT_ROWS), :] = turned(query_grad)
         return unused
 
-    lax.fori_loop(0, rows_here // ROWS, block, 0)
-    leave_in_order(place_ref[0], inner, rows_here, grad, sum_ref)
+    lax.fori_loop(0, rows_here // PROMPT_ROWS, block, 0)
+    leave_in_order(place_ref[0], inner, rows_here, range(2 * inner), grad, sum_ref)
 
 
 def prompt_pass(place, inner, q, do, caches, carried, scaling):
@@ -139,23 +140,22 @@
         out_specs=[pl.BlockSpec(memory_space=pltpu.VMEM)] * 3,
         scratch_shapes=[
             pltpu.VMEM((length, 2 * head), F32),
-            pltpu.VMEM((length, ROWS), F32),
-            pltpu.VMEM((length, ROWS), BF16),
+            pltpu.VMEM((length, PROMPT_ROWS), F32),
+            pltpu.VMEM((length, PROMPT_ROWS), BF16),
         ],
-        compiler_params=pltpu.CompilerParams(vmem_limit_bytes=24 * 1024 * 1024),
+        compiler_params=pltpu.CompilerParams(vmem_limit_bytes=28 * 1024 * 1024),
         cost_estimate=pl.CostEstimate(flops=24 * rows * length * head, bytes_accessed=8 * length * head, transcendentals=0),
         name="prompt_pass",
     )(place, q, do, *caches, carried)
 
 
 def reply_kernel(
-    scaling, inner, other_count, scalars_ref, lengths_ref, owners_ref, q_ref, do_ref, own_ref, *refs
+    scaling, inner, other_count, other_order, scalars_ref, lengths_ref, owners_ref, q_ref, do_ref, own_ref, *refs
 ):
-    (
-        out_ref, dq_ref, other_sum_ref, mine_sum_ref, own_keep_ref, own_send_ref,
-        picks_ref, q_t_ref, do_t_ref, results, grad, own_grad, score_ref, weight_ref, slope_ref,
-    ) = refs[-15:]
-    caches = refs[:-15]
+    caches, refs = refs[: -13 - inner], refs[-13 - inner :]
+    out_ref, dq_ref, other_sum_ref, mine_sum_ref = refs[:4]
+    own_pieces = refs[4 : 4 + inner]
+    picks_ref, q_t_ref, do_t_ref, results, grad, own_grad, score_ref, weight_ref, slope_ref = refs[4 + inner :]
     others, mines = caches[:other_count], caches[other_count:]
     capacity, head = q_ref.shape
     length = grad.shape[0]
@@ -240,7 +240,7 @@
 
         lax.fori_loop(edges[edge] // ROWS, edges[edge + 1] // ROWS, block, 0)
         if edge == 0:
-            leave_in_order(scalars_ref[0], inner, length // (2 * inner), grad, sum_ref)
+            leave_in_order(scalars_ref[0], inner, length // (2 * inner), other_order, grad, sum_ref)
         else:
             sum_ref[...] = grad[...].astype(BF16)
 
@@ -248,30 +248,28 @@
     out_ref[...] = placed[:, :head]
     dq_ref[...] = placed[:, head:]
     share = capacity // (2 * inner)
-    me_outer, me_inner = lax.div(scalars_ref[0], inner), lax.rem(scalars_ref[0], inner)
-    for k in range(inner):
-        there = lax.rem(me_inner + k, inner)
-        for outer, ref in ((me_outer, own_keep_ref), (1 - me_outer, own_send_ref)):
+    for k, ref in enumerate(own_pieces):
+        there = lax.rem(lax.rem(scalars_ref[0], inner) + k, inner)
+        for outer in range(2):
             at = pl.multiple_of((outer * inner + there) * share, share)
-            ref[k * share : (k + 1) * share, :] = own_grad[pl.ds(at, share), :].astype(BF16)
-
-
-def reply_pass(scalars, inner, lengths, owners, q, do, own, others, mines, scaling):
+            ref[outer * share : (outer + 1) * share, :] = own_grad[pl.ds(at, share), :].astype(BF16)
+
+
+def reply_pass(scalars, inner, lengths, owners, q, do, own, others, other_order, mines, scaling):
     capacity, head = q.shape
     length = sum(part.shape[0] for part in mines)
     spread = capacity + ROWS
     return pl.pallas_call(
-        functools.partial(reply_kernel, scaling, inner, len(others)),
+        functools.partial(reply_kernel, scaling, inner, len(others), other_order),
         out_shape=[
             jax.ShapeDtypeStruct((capacity, head), BF16),
             jax.ShapeDtypeStruct((capacity, head), BF16),
             jax.ShapeDtypeStruct((length, 2 * head), BF16),
             jax.ShapeDtypeStruct((length, 2 * head), BF16),
-            jax.ShapeDtypeStruct((capacity // 2, 2 * head), BF16),
-            jax.ShapeDtypeStruct((capacity // 2, 2 * head), BF16),
-        ],
+        ]
+        + [jax.ShapeDtypeStruct((capacity // inner, 2 * head), BF16)] * inner,
         in_specs=[pl.BlockSpec(memory_space=pltpu.SMEM)] * 3 + [pl.BlockSpec(memory_space=pltpu.VMEM)] * (3 + len(others) + len(mines)),
-        out_specs=[pl.BlockSpec(memory_space=pltpu.VMEM)] * 6,
+        out_specs=[pl.BlockSpec(memory_space=pltpu.VMEM)] * (4 + inner),
         scratch_shapes=[
             pltpu.VMEM((capacity, spread), BF16),
             pltpu.VMEM((head, spread), BF16),
@@ -289,51 +287,46 @@
     )(scalars, lengths, owners, q, do, own, *others, *mines)
 
 
-def place_kernel(inner, first, place_ref, *refs):
-    out_ref, halves = refs[-1], (refs[:first], refs[first:-1])
+def place_kernel(inner, place_ref, *refs):
+    out_ref = refs[-1]
     share = out_ref.shape[0] // (2 * inner)
-    me_outer, me_inner = lax.div(place_ref[0], inner), lax.rem(place_ref[0], inner)
-    for outer, pieces in zip((me_outer, 1 - me_outer), halves):
-        at = 0
-        for ref in pieces:
-            for begin in range(0, ref.shape[0], share):
-                there = outer * inner + lax.rem(me_inner + (inner - at), inner)
-                out_ref[pl.ds(pl.multiple_of(there * share, share), share), :] = ref[begin : begin + share, :]
-                at += 1
-
-
-def placed_in_order(place, inner, mine, other):
-    rows = sum(x.shape[0] for x in mine)
-    operands = [*mine, *other]
+    for k, ref in enumerate(refs[:-1]):
+        there = lax.rem(lax.rem(place_ref[0], inner) + (inner - k), inner)
+        for outer in range(2):
+            at = pl.multiple_of((outer * inner + there) * share, share)
+            out_ref[pl.ds(at, share), :] = ref[outer * share : (outer + 1) * share, :]
+
+
+def placed_in_order(place, pieces):
+    rows, width = pieces[0].shape
     return pl.pallas_call(
-        functools.partial(place_kernel, inner, len(mine)),
-        out_shape=jax.ShapeDtypeStruct((2 * rows, mine[0].shape[1]), BF16),
-        in_specs=[pl.BlockSpec(memory_space=pltpu.SMEM)] + [pl.BlockSpec(memory_space=pltpu.VMEM)] * len(operands),
+        functools.partial(place_kernel, len(pieces)),
+        out_shape=jax.ShapeDtypeStruct((len(pieces) * rows, width), BF16),
+        in_specs=[pl.BlockSpec(memory_space=pltpu.SMEM)] + [pl.BlockSpec(memory_space=pltpu.VMEM)] * len(pieces),
         out_specs=pl.BlockSpec(memory_space=pltpu.VMEM),
         compiler_params=pltpu.CompilerParams(vmem_limit_bytes=8 * 1024 * 1024),
         name="placed_in_order",
-    )(place, *operands)
-
-
-def join_kernel(total_ref, arrived_ref, keep_ref, came_ref, shares_ref, *pieces):
+    )(place, *pieces)
+
+
+def join_kernel(total_ref, arrived_ref, *refs):
+    *pieces, shares_ref, part_ref = refs
     shares_ref[...] = (total_ref[...].astype(F32) + arrived_ref[...].astype(F32)).astype(BF16)
-    rows = pieces[0].shape[0]
-    for k, ref in enumerate(pieces):
-        at = slice(k * rows, (k + 1) * rows)
-        ref[...] = (keep_ref[at, :].astype(F32) + came_ref[at, :].astype(F32)).astype(BF16)
-
-
-def join(total, arrived, keep, came, count):
-    rows, width = keep.shape
+    part = pieces[0][...].astype(F32)
+    for ref in pieces[1:]:
+        part = part + ref[...].astype(F32)
+    part_ref[...] = part.astype(BF16)
+
+
+def join(total, arrived, pieces):
     return pl.pallas_call(
         join_kernel,
-        out_shape=[jax.ShapeDtypeStruct(total.shape, BF16)]
-        + [jax.ShapeDtypeStruct((rows // count, width), BF16)] * count,
-        in_specs=[pl.BlockSpec(memory_space=pltpu.VMEM)] * 4,
-        out_specs=[pl.BlockSpec(memory_space=pltpu.VMEM)] * (1 + count),
+        out_shape=[jax.ShapeDtypeStruct(total.shape, BF16), jax.ShapeDtypeStruct(pieces[0].shape, BF16)],
+        in_specs=[pl.BlockSpec(memory_space=pltpu.VMEM)] * (2 + len(pieces)),
+        out_specs=[pl.BlockSpec(memory_space=pltpu.VMEM)] * 2,
         compiler_params=pltpu.CompilerParams(vmem_limit_bytes=16 * 1024 * 1024),
         name="join_sums",
-    )(total, arrived, keep, came)
+    )(total, arrived, *pieces)
 
 
 def per_device(
@@ -382,12 +375,14 @@
         half = own.shape[0] // 2
         y_2a, y_2b = along_y(next_2[:half], 1), along_y(next_2[half:], -1)
         mines = [own, next_1, next_2, next_3, y_0, y_1, y_2a, y_2b, y_3]
-        others = [swap(jnp.concatenate(part, axis=0)) for part in (mines[:inner], mines[inner:])]
+        early, late = [own, next_1, next_3], [next_2, y_0, y_1, y_2a, y_2b, y_3]
+        others = [swap(jnp.concatenate(part, axis=0)) for part in (early, late)]
+        other_order = (0, 1, 3, 2, 4, 5, 6, 7)
 
     with jax.named_scope("reply_rows"):
-        reply_out, reply_dq, other_sum, mine_sum, own_keep, own_send = reply_pass(
+        reply_out, reply_dq, other_sum, mine_sum, *own_pieces = reply_pass(
             jnp.concatenate([place, group]), inner, reply_lengths[0], reply_owner[0], reply_query, reply_cotangent, reply_cache,
-            others, mines, scaling,
+            others, other_order, mines, scaling,
         )
     arrived = swap(other_sum)
     with jax.named_scope("prompt_rows"):
@@ -397,15 +392,12 @@
 
     with jax.named_scope("prompt_cache_sum"):
         count = ctx_count * comp_count
-        shares, *pieces = join(total, arrived, own_keep, outer_swap(own_send), inner)
+        came = [along_z(own_pieces[k], k) for k in range(1, inner)]
+        shares, part = join(total, arrived, [own_pieces[0], *came])
         terms = lax.all_to_all(shares.reshape(count, -1, width), ("ctx", "comp"), 0, 0, tiled=True)
     with jax.named_scope("reply_cache_sum"):
-        part = pieces[0].astype(F32)
-        for k in range(1, inner):
-            part = part + along_z(pieces[k], k).astype(F32)
-        part = part.astype(BF16)
-        mine_half = jnp.concatenate([part] + [along_z(part, k) for k in range(1, inner)], axis=0)
-        reply_grad = placed_in_order(place, inner, [mine_half], [outer_swap(mine_half)])
+        part = (part.astype(F32) + outer_swap(part).astype(F32)).astype(BF16)
+        reply_grad = placed_in_order(place, [part] + [along_z(part, k) for k in range(1, inner)])
     with jax.named_scope("prompt_cache_halves"):
         summed = jnp.sum(terms.astype(F32), axis=0).astype(BF16)
         rows = summed.shape[0] // group_count

time: 130 us -> 127 us (0.977)
  starting transfers between devices: 45.6 us -> 39.4 us
  Pallas kernels: 30.7 us -> 32.9 us
  local copies, waits for them, and re-layouts: 5.54 us -> 7.19 us
    ppermute x2 -> x1, waiting for transfers between devices: 5.31 us -> 25.2 us  [outer_swap(): lax.ppermute(x, 'ctx', [(i, (i + inner) % ctx_count) for i in range(ctx_c...]
    ppermute x9, waiting for transfers between devices: 31.5 us -> 14.9 us  [along_z(): return lax.ppermute(x, 'ctx', pairs)]
    ppermute x4, starting transfers between devices: 9 us -> 0.6 us  [swap(): return lax.ppermute(x, 'grp', [(0, 1), (1, 0)])]
    pallas_call x1, Pallas kernels: 17.2 us -> 22 us  [reply_pass(): pl.pallas_call(functools.partial(reply_kernel, scaling, inner, len(others...]
    all_to_all x1, starting transfers between devices: 9.02 us -> 13 us  [per_device(): lax.all_to_all(shares.reshape(count, -1, width), ('ctx', 'comp'), 0, 0, t...]
    pallas_call x1, Pallas kernels: 10.8 us -> 8.31 us  [prompt_pass(): pl.pallas_call(functools.partial(prompt_kernel, scaling, inner), out_shap...]
    ppermute x5, waiting for transfers between devices: 3.72 us -> 1.35 us  [along_y(): return lax.ppermute(x, ('ctx', 'comp'), pairs)]
    unnamed x20 -> x21, local copies, waits for them, and re-layouts: 4.8 us -> 6.46 us
  transfers between devices with their start and end apart: 21 -> 20, of which waited for: 10 -> 9; matrix products, arithmetic and copies ran while one was open for 5% -> 4% of each run, Pallas kernels for 9% -> 7%
where the time goes in v3:
time: 127 us
  waiting for transfers between devices  44.4 us (35%)
  starting transfers between devices  39.4 us (31%)
  Pallas kernels  32.9 us (26%)
  local copies, waits for them, and re-layouts  7.19 us (6%)
  other arithmetic  1.98 us (2%)
    ppermute x1, waiting for transfers between devices, outer_swap(): lax.ppermute(x, 'ctx', [(i, (i + inner) % ctx_count) for i in range(ctx_c...  25.2 us
    pallas_call x1, Pallas kernels, reply_pass(): pl.pallas_call(functools.partial(reply_kernel, scaling, inner, len(others...  22 us
    ppermute x9, waiting for transfers between devices, along_z(): return lax.ppermute(x, 'ctx', pairs)  14.9 us
    ppermute x9, starting transfers between devices, along_z(): return lax.ppermute(x, 'ctx', pairs)  14.7 us
    all_to_all x1, starting transfers between devices, per_device(): lax.all_to_all(shares.reshape(count, -1, width), ('ctx', 'comp'), 0, 0, t...  13 us
    ppermute x5, starting transfers between devices, along_y(): return lax.ppermute(x, ('ctx', 'comp'), pairs)  9.47 us
    pallas_call x1, Pallas kernels, prompt_pass(): pl.pallas_call(functools.partial(prompt_kernel, scaling, inner), out_shap...  8.31 us
    unnamed x21, local copies, waits for them, and re-layouts  6.46 us
  transfers between devices with their start and end apart: 20, of which 9 were waited for; matrix products, arithmetic and copies ran while one was open for 4% of the time, Pallas kernels for 7%

profile of v3, /device:TPU:4, one launch (start us, length us, event | category | flops | bytes accessed | tf_op | source)
XLA Modules:
  0.0 126.7 jit_solution(3435268008991846309)
XLA Ops:
  0.6 2.0 %collective-permute-start = (bf16[512,256]{1,0:T(8,128)(2,1)}, bf16[512,256]{1,0:T(8,128)(2,1)S(1)}, u32[]{:S(2)}, u32[]{:S(2)}) collective-permute-start(bf16[512,256]{1,0:T(8,128)(2,1)} %bitcast.13), channel_id=1, source_target_pairs={{0,16},{16,32},{32,48},{48,0},{64,80},{80,96},{96,112},{112,64},{1... | collective-permute-start | bytes 786440 | tf_op jit(solution)/shard_map/gather_keys/ppermute | solution.py:355
  2.6 3.6 %collective-permute-start.1 = (bf16[512,256]{1,0:T(8,128)(2,1)}, bf16[512,256]{1,0:T(8,128)(2,1)S(1)}, u32[]{:S(2)}, u32[]{:S(2)}) collective-permute-start(bf16[512,256]{1,0:T(8,128)(2,1)} %bitcast.14), channel_id=1, source_target_pairs={{0,32},{16,48},{32,0},{48,16},{64,96},{80,112},{96,64},{112,80},{1... | collective-permute-start | bytes 786440 | tf_op jit(solution)/shard_map/gather_keys/ppermute | solution.py:355
  6.2 1.0 collective-permute-start.2
  7.2 1.6 %collective-permute-start.3 = (bf16[512,256]{1,0:T(8,128)(2,1)}, bf16[512,256]{1,0:T(8,128)(2,1)S(1)}, u32[]{:S(2)}, u32[]{:S(2)}) collective-permute-start(bf16[512,256]{1,0:T(8,128)(2,1)} %bitcast.16), channel_id=1, source_target_pairs={{0,64},{2,66},{4,68},{6,70},{8,72},{10,74},{12,76},{14,78},{16,80}... | collective-permute-start | bytes 786440 | tf_op jit(solution)/shard_map/gather_keys/ppermute | solution.py:368
  8.8 2.5 %collective-permute-done.refs_3_.refs_1_ = bf16[512,256]{1,0:T(8,128)(2,1)S(1)} collective-permute-done((bf16[512,256]{1,0:T(8,128)(2,1)}, bf16[512,256]{1,0:T(8,128)(2,1)S(1)}, u32[]{:S(2)}, u32[]{:S(2)}) %collective-permute-start) | collective-permute-done | bytes 262176 | tf_op jit(solution)/shard_map/gather_keys/ppermute | solution.py:355
  11.3 1.6 %collective-permute-start.4 = (bf16[512,256]{1,0:T(8,128)(2,1)S(1)}, bf16[512,256]{1,0:T(8,128)(2,1)S(1)}, u32[]{:S(2)}, u32[]{:S(2)}) collective-permute-start(bf16[512,256]{1,0:T(8,128)(2,1)S(1)} %collective-permute-done.refs_3_.refs_1_), channel_id=1, source_target_pairs={{0,64},{2,66},{4,68},{6,70},{8,72},{10,74},{12,76},{14,78},{16,80}... | collective-permute-start | bytes 786440 | tf_op jit(solution)/shard_map/gather_keys/ppermute | solution.py:368
  12.8 5.2 %collective-permute-done.1.refs_4_.refs_2_ = bf16[512,256]{1,0:T(8,128)(2,1)S(1)} collective-permute-done((bf16[512,256]{1,0:T(8,128)(2,1)}, bf16[512,256]{1,0:T(8,128)(2,1)S(1)}, u32[]{:S(2)}, u32[]{:S(2)}) %collective-permute-start.1) | collective-permute-done | bytes 262176 | tf_op jit(solution)/shard_map/gather_keys/ppermute | solution.py:355
  18.1 3.1 %collective-permute-start.6 = (bf16[256,256]{1,0:T(8,128)(2,1)S(1)}, bf16[256,256]{1,0:T(8,128)(2,1)S(1)}, u32[]{:S(2)}, u32[]{:S(2)}) collective-permute-start(bf16[256,256]{1,0:T(8,128)(2,1)S(1)} %get-tuple-element.32), channel_id=1, source_target_pairs={{0,72},{2,74},{4,76},{6,78},{8,64},{10,66},{12,68},{14,70},{16,88}... | collective-permute-start | bytes 393224 | tf_op jit(solution)/shard_map/gather_keys/ppermute | solution.py:368
  21.2 3.2 %collective-permute-start.7 = (bf16[512,256]{1,0:T(8,128)(2,1)S(1)}, bf16[512,256]{1,0:T(8,128)(2,1)S(1)}, u32[]{:S(2)}, u32[]{:S(2)}) collective-permute-start(bf16[512,256]{1,0:T(8,128)(2,1)S(1)} %collective-permute-done.2.refs_5_.refs_3_), channel_id=1, source_target_pairs={{0,72},{2,74},{4,76},{6,78},{8,64},{10,66},{12,68},{14,70},{16,88}... | collective-permute-start | bytes 786440 | tf_op jit(solution)/shard_map/gather_keys/ppermute | solution.py:368
  24.4 0.7 constant_dynamic-update-slice_fusion.5
  25.1 0.7 constant_dynamic-update-slice_fusion.4
  25.9 0.7 constant_dynamic-update-slice_fusion.3
  26.6 0.7 collective-permute-done.5.refs_8_.refs_6_
  30.0 0.9 pad_maximum_fusion
  31.5 3.0 %collective-permute-done.8.refs_0_ = bf16[1536,256]{1,0:T(8,128)(2,1)} collective-permute-done((bf16[1536,256]{1,0:T(8,128)(2,1)}, bf16[1536,256]{1,0:T(8,128)(2,1)}, u32[]{:S(2)}, u32[]{:S(2)}) %collective-permute-start.8) | collective-permute-done | bytes 786464 | tf_op jit(solution)/shard_map/gather_keys/ppermute | solution.py:351
  34.5 1.0 copy-done.1
  35.5 0.9 copy-done.2
  36.5 0.9 copy-done.3
  37.4 22.0 %reply_pass.1 = (bf16[1024,128]{1,0:T(8,128)(2,1)}, bf16[1024,128]{1,0:T(8,128)(2,1)}, bf16[4096,256]{1,0:T(8,128)(2,1)S(1)}, bf16[4096,256]{1,0:T(8,128)(2,1)S(...) custom-call(s32[2]{0:T(128)S(1)} %pad_add_fusion.scalars_ref, ...), custom_call_target="tpu_custom_call" | custom-call | flops 12884901888 | bytes 8388608 | tf_op jit(solution)/shard_map/reply_rows/reply_pass/pallas_call | solution.py:262
  59.4 1.2 collective-permute-start.12
  60.6 2.4 %collective-permute-start.13 = (bf16[256,256]{1,0:T(8,128)(2,1)S(1)}, bf16[256,256]{1,0:T(8,128)(2,1)S(1)}, u32[]{:S(2)}, u32[]{:S(2)}) collective-permute-start(bf16[256,256]{1,0:T(8,128)(2,1)S(1)} %get-tuple-element.27), channel_id=1, source_target_pairs={{0,48},{16,0},{32,16},{48,32},{64,112},{80,64},{96,80},{112,96},{1... | collective-permute-start | bytes 393224 | tf_op jit(solution)/shard_map/prompt_cache_sum/ppermute | solution.py:355
  63.0 8.3 %prompt_pass.1 = (bf16[512,128]{1,0:T(8,128)(2,1)}, bf16[512,128]{1,0:T(8,128)(2,1)}, bf16[4096,256]{1,0:T(8,128)(2,1)S(1)}) custom-call(s32[1]{0:T(128)} %bitcast.place_ref, bf16[512,128]{1,0:T(8,128)(2,1)S(1)} %bitcast.20, bf16[512,128]{1,0:T(8,128)(2,1)S(1)} %bitcast.21, bf16[512,256]{1,0:T(8,128)(2,1)S(1)} %bitcast.19, ...), custom_call_target="tpu_custom_call" | custom-call | flops 6442450944 | bytes 4194304 | tf_op jit(solution)/shard_map/prompt_rows/prompt_pass/pallas_call | solution.py:132
  71.3 1.8 %join_sums.1 = (bf16[4096,256]{1,0:T(8,128)(2,1)}, bf16[256,256]{1,0:T(8,128)(2,1)S(1)}) custom-call(bf16[4096,256]{1,0:T(8,128)(2,1)S(1)} %get-tuple-element.22.total_ref, bf16[4096,256]{1,0:T(8,128)(2,1)S(1)} %collective-permute-done.10.arrived_ref, bf16[256,256]{1,0:T(8,128)(2,1)S(1)} %get-tuple-element.24.refs_0_, ...), custom_call_target="tpu_custom_call" | custom-call | tf_op jit(solution)/shard_map/prompt_cache_sum/join_sums/pallas_call | solution.py:322
  73.1 13.0 %all-to-all-start = ((bf16[64,64,256]{2,1,0:T(8,128)(2,1)}), bf16[64,64,256]{2,1,0:T(8,128)(2,1)S(1)}, u32[]{:S(2)}, u32[]{:S(2)}) async-start(bf16[64,64,256]{2,1,0:T(8,128)(2,1)} %bitcast.9), calls=%async_computation | async-start | bytes 4194304 | tf_op jit(solution)/shard_map/prompt_cache_sum/all_to_all | solution.py:397
  86.1 1.7 %collective-permute-start.15 = (bf16[256,256]{1,0:T(8,128)(2,1)S(1)}, bf16[256,256]{1,0:T(8,128)(2,1)S(1)}, u32[]{:S(2)}, u32[]{:S(2)}) collective-permute-start(bf16[256,256]{1,0:T(8,128)(2,1)S(1)} %get-tuple-element.31), channel_id=1, source_target_pairs={{0,64},{16,80},{32,96},{48,112},{64,0},{80,16},{96,32},{112,48},{1... | collective-permute-start | bytes 393224 | tf_op jit(solution)/shard_map/reply_cache_sum/ppermute | solution.py:358
  87.8 25.2 %collective-permute-done.15 = bf16[256,256]{1,0:T(8,128)(2,1)S(1)} collective-permute-done((bf16[256,256]{1,0:T(8,128)(2,1)S(1)}, bf16[256,256]{1,0:T(8,128)(2,1)S(1)}, u32[]{:S(2)}, u32[]{:S(2)}) %collective-permute-start.15) | collective-permute-done | bytes 131104 | tf_op jit(solution)/shard_map/reply_cache_sum/ppermute | solution.py:358
  113.0 3.1 %collective-permute-start.18 = (bf16[256,256]{1,0:T(8,128)(2,1)S(1)}, bf16[256,256]{1,0:T(8,128)(2,1)S(1)}, u32[]{:S(2)}, u32[]{:S(2)}) collective-permute-start(bf16[256,256]{1,0:T(8,128)(2,1)S(1)} %add_convert_fusion.refs_0_), channel_id=1, source_target_pairs={{0,48},{16,0},{32,16},{48,32},{64,112},{80,64},{96,80},{112,96},{1... | collective-permute-start | bytes 393224 | tf_op jit(solution)/shard_map/reply_cache_sum/ppermute | solution.py:355
  116.5 1.1 collective-permute-start.16
  118.0 3.8 %collective-permute-done.18.refs_3_ = bf16[256,256]{1,0:T(8,128)(2,1)S(1)} collective-permute-done((bf16[256,256]{1,0:T(8,128)(2,1)S(1)}, bf16[256,256]{1,0:T(8,128)(2,1)S(1)}, u32[]{:S(2)}, u32[]{:S(2)}) %collective-permute-start.18) | collective-permute-done | bytes 131104 | tf_op jit(solution)/shard_map/reply_cache_sum/ppermute | solution.py:355
  121.8 2.3 %collective-permute-done.17.refs_2_ = bf16[256,256]{1,0:T(8,128)(2,1)S(1)} collective-permute-done((bf16[256,256]{1,0:T(8,128)(2,1)S(1)}, bf16[256,256]{1,0:T(8,128)(2,1)S(1)}, u32[]{:S(2)}, u32[]{:S(2)}) %collective-permute-start.17) | collective-permute-done | bytes 131104 | tf_op jit(solution)/shard_map/reply_cache_sum/ppermute | solution.py:355
  124.1 1.2 collective-permute-done.16.refs_1_
  125.2 0.8 placed_in_order.1
  (41 shorter events, 4.7 us)
Async XLA Ops:
  0.6 10.6 %collective-permute-start = (bf16[512,256]{1,0:T(8,128)(2,1)}, bf16[512,256]{1,0:T(8,128)(2,1)S(1)}, u32[]{:S(2)}, u32[]{:S(2)}) collective-permute-start(bf16[512,256]{1,0:T(8,128)(2,1)} %bitcast.13), channel_id=1, source_target_pairs={{0,16},{16,32},{32,48},{48,0},{64,80},{80,96},{96,112},{112,64},{1... | collective-permute-start | bytes 786440 | tf_op jit(solution)/shard_map/gather_keys/ppermute | solution.py:355
  2.6 15.4 %collective-permute-start.1 = (bf16[512,256]{1,0:T(8,128)(2,1)}, bf16[512,256]{1,0:T(8,128)(2,1)S(1)}, u32[]{:S(2)}, u32[]{:S(2)}) collective-permute-start(bf16[512,256]{1,0:T(8,128)(2,1)} %bitcast.14), channel_id=1, source_target_pairs={{0,32},{16,48},{32,0},{48,16},{64,96},{80,112},{96,64},{112,80},{1... | collective-permute-start | bytes 786440 | tf_op jit(solution)/shard_map/gather_keys/ppermute | solution.py:355
  6.2 15.0 %collective-permute-start.2 = (bf16[512,256]{1,0:T(8,128)(2,1)}, bf16[512,256]{1,0:T(8,128)(2,1)S(1)}, u32[]{:S(2)}, u32[]{:S(2)}) collective-permute-start(bf16[512,256]{1,0:T(8,128)(2,1)} %bitcast.15), channel_id=1, source_target_pairs={{0,48},{16,0},{32,16},{48,32},{64,112},{80,64},{96,80},{112,96},{1... | collective-permute-start | bytes 786440 | tf_op jit(solution)/shard_map/gather_keys/ppermute | solution.py:355
  7.2 17.9 %collective-permute-start.3 = (bf16[512,256]{1,0:T(8,128)(2,1)}, bf16[512,256]{1,0:T(8,128)(2,1)S(1)}, u32[]{:S(2)}, u32[]{:S(2)}) collective-permute-start(bf16[512,256]{1,0:T(8,128)(2,1)} %bitcast.16), channel_id=1, source_target_pairs={{0,64},{2,66},{4,68},{6,70},{8,72},{10,74},{12,76},{14,78},{16,80}... | collective-permute-start | bytes 786440 | tf_op jit(solution)/shard_map/gather_keys/ppermute | solution.py:368
  11.3 14.6 %collective-permute-start.4 = (bf16[512,256]{1,0:T(8,128)(2,1)S(1)}, bf16[512,256]{1,0:T(8,128)(2,1)S(1)}, u32[]{:S(2)}, u32[]{:S(2)}) collective-permute-start(bf16[512,256]{1,0:T(8,128)(2,1)S(1)} %collective-permute-done.refs_3_.refs_1_), channel_id=1, source_target_pairs={{0,64},{2,66},{4,68},{6,70},{8,72},{10,74},{12,76},{14,78},{16,80}... | collective-permute-start | bytes 786440 | tf_op jit(solution)/shard_map/gather_keys/ppermute | solution.py:368
  18.1 9.9 %collective-permute-start.6 = (bf16[256,256]{1,0:T(8,128)(2,1)S(1)}, bf16[256,256]{1,0:T(8,128)(2,1)S(1)}, u32[]{:S(2)}, u32[]{:S(2)}) collective-permute-start(bf16[256,256]{1,0:T(8,128)(2,1)S(1)} %get-tuple-element.32), channel_id=1, source_target_pairs={{0,72},{2,74},{4,76},{6,78},{8,64},{10,66},{12,68},{14,70},{16,88}... | collective-permute-start | bytes 393224 | tf_op jit(solution)/shard_map/gather_keys/ppermute | solution.py:368
  21.2 8.8 %copy-start = (bf16[1,512,256]{2,1,0:T(8,128)(2,1)S(1)}, bf16[1,512,256]{2,1,0:T(8,128)(2,1)}, u32[]{:S(2)}) copy-start(bf16[1,512,256]{2,1,0:T(8,128)(2,1)} %param.9) | copy-start | bytes 786436
  21.2 6.2 %collective-permute-start.5 = (bf16[256,256]{1,0:T(8,128)(2,1)S(1)}, bf16[256,256]{1,0:T(8,128)(2,1)S(1)}, u32[]{:S(2)}, u32[]{:S(2)}) collective-permute-start(bf16[256,256]{1,0:T(8,128)(2,1)S(1)} %get-tuple-element.33), channel_id=1, source_target_pairs={{0,64},{2,66},{4,68},{6,70},{8,72},{10,74},{12,76},{14,78},{16,80}... | collective-permute-start | bytes 393224 | tf_op jit(solution)/shard_map/gather_keys/ppermute | solution.py:368
  21.2 8.1 %collective-permute-start.7 = (bf16[512,256]{1,0:T(8,128)(2,1)S(1)}, bf16[512,256]{1,0:T(8,128)(2,1)S(1)}, u32[]{:S(2)}, u32[]{:S(2)}) collective-permute-start(bf16[512,256]{1,0:T(8,128)(2,1)S(1)} %collective-permute-done.2.refs_5_.refs_3_), channel_id=1, source_target_pairs={{0,72},{2,74},{4,76},{6,78},{8,64},{10,66},{12,68},{14,70},{16,88}... | collective-permute-start | bytes 786440 | tf_op jit(solution)/shard_map/gather_keys/ppermute | solution.py:368
  26.6 7.9 %copy-start.6 = (s32[1,4]{1,0:T(1,128)S(1)}, s32[1,4]{1,0:T(1,128)}, u32[]{:S(2)}) copy-start(s32[1,4]{1,0:T(1,128)} %param.14) | copy-start | bytes 52
  26.6 7.9 %copy-start.7 = (s32[1,4]{1,0:T(1,128)S(1)}, s32[1,4]{1,0:T(1,128)}, u32[]{:S(2)}) copy-start(s32[1,4]{1,0:T(1,128)} %param.15) | copy-start | bytes 52
  30.0 4.5 %collective-permute-start.9 = (bf16[2560,256]{1,0:T(8,128)(2,1)}, bf16[2560,256]{1,0:T(8,128)(2,1)S(1)}, u32[]{:S(2)}, u32[]{:S(2)}) collective-permute-start(bf16[2560,256]{1,0:T(8,128)(2,1)} %constant_dynamic-update-slice_fusion), channel_id=1, source_target_pairs={{0,1},{1,0},{2,3},{3,2},{4,5},{5,4},{6,7},{7,6},{8,9},{9,8},{10,11... | collective-permute-start | bytes 3932168 | tf_op jit(solution)/shard_map/gather_keys/ppermute | solution.py:351
  30.9 3.6 %collective-permute-start.8 = (bf16[1536,256]{1,0:T(8,128)(2,1)}, bf16[1536,256]{1,0:T(8,128)(2,1)}, u32[]{:S(2)}, u32[]{:S(2)}) collective-permute-start(bf16[1536,256]{1,0:T(8,128)(2,1)} %pad_maximum_fusion), channel_id=1, source_target_pairs={{0,1},{1,0},{2,3},{3,2},{4,5},{5,4},{6,7},{7,6},{8,9},{9,8},{10,11... | collective-permute-start | bytes 2359304 | tf_op jit(solution)/shard_map/gather_keys/ppermute | solution.py:351
  34.5 1.0 copy-start.1
  35.5 0.9 copy-start.2
  36.5 0.9 copy-start.3
  37.4 25.5 %copy-start.4 = (bf16[1,512,128]{2,1,0:T(8,128)(2,1)S(1)}, bf16[1,512,128]{2,1,0:T(8,128)(2,1)}, u32[]{:S(2)}) copy-start(bf16[1,512,128]{2,1,0:T(8,128)(2,1)} %param.8) | copy-start | bytes 393220
  37.4 25.5 %copy-start.5 = (bf16[1,512,128]{2,1,0:T(8,128)(2,1)S(1)}, bf16[1,512,128]{2,1,0:T(8,128)(2,1)}, u32[]{:S(2)}) copy-start(bf16[1,512,128]{2,1,0:T(8,128)(2,1)} %param.10) | copy-start | bytes 393220
  59.4 11.9 %collective-permute-start.10 = (bf16[4096,256]{1,0:T(8,128)(2,1)S(1)}, bf16[4096,256]{1,0:T(8,128)(2,1)S(1)}, u32[]{:S(2)}, u32[]{:S(2)}) collective-permute-start(bf16[4096,256]{1,0:T(8,128)(2,1)S(1)} %get-tuple-element.23), channel_id=1, source_target_pairs={{0,1},{1,0},{2,3},{3,2},{4,5},{5,4},{6,7},{7,6},{8,9},{9,8},{10,11... | collective-permute-start | bytes 6291464 | tf_op jit(solution)/shard_map/ppermute | solution.py:351
  59.4 11.9 %collective-permute-start.11 = (bf16[256,256]{1,0:T(8,128)(2,1)S(1)}, bf16[256,256]{1,0:T(8,128)(2,1)S(1)}, u32[]{:S(2)}, u32[]{:S(2)}) collective-permute-start(bf16[256,256]{1,0:T(8,128)(2,1)S(1)} %get-tuple-element.25), channel_id=1, source_target_pairs={{0,16},{16,32},{32,48},{48,0},{64,80},{80,96},{96,112},{112,64},{1... | collective-permute-start | bytes 393224 | tf_op jit(solution)/shard_map/prompt_cache_sum/ppermute | solution.py:355
  59.4 11.9 %collective-permute-start.12 = (bf16[256,256]{1,0:T(8,128)(2,1)S(1)}, bf16[256,256]{1,0:T(8,128)(2,1)S(1)}, u32[]{:S(2)}, u32[]{:S(2)}) collective-permute-start(bf16[256,256]{1,0:T(8,128)(2,1)S(1)} %get-tuple-element.26), channel_id=1, source_target_pairs={{0,32},{16,48},{32,0},{48,16},{64,96},{80,112},{96,64},{112,80},{1... | collective-permute-start | bytes 393224 | tf_op jit(solution)/shard_map/prompt_cache_sum/ppermute | solution.py:355
  60.6 10.7 %collective-permute-start.13 = (bf16[256,256]{1,0:T(8,128)(2,1)S(1)}, bf16[256,256]{1,0:T(8,128)(2,1)S(1)}, u32[]{:S(2)}, u32[]{:S(2)}) collective-permute-start(bf16[256,256]{1,0:T(8,128)(2,1)S(1)} %get-tuple-element.27), channel_id=1, source_target_pairs={{0,48},{16,0},{32,16},{48,32},{64,112},{80,64},{96,80},{112,96},{1... | collective-permute-start | bytes 393224 | tf_op jit(solution)/shard_map/prompt_cache_sum/ppermute | solution.py:355
  73.1 44.4 %all-to-all-start = ((bf16[64,64,256]{2,1,0:T(8,128)(2,1)}), bf16[64,64,256]{2,1,0:T(8,128)(2,1)S(1)}, u32[]{:S(2)}, u32[]{:S(2)}) async-start(bf16[64,64,256]{2,1,0:T(8,128)(2,1)} %bitcast.9), calls=%async_computation | async-start | bytes 4194304 | tf_op jit(solution)/shard_map/prompt_cache_sum/all_to_all | solution.py:397
  86.1 26.8 %collective-permute-start.15 = (bf16[256,256]{1,0:T(8,128)(2,1)S(1)}, bf16[256,256]{1,0:T(8,128)(2,1)S(1)}, u32[]{:S(2)}, u32[]{:S(2)}) collective-permute-start(bf16[256,256]{1,0:T(8,128)(2,1)S(1)} %get-tuple-element.31), channel_id=1, source_target_pairs={{0,64},{16,80},{32,96},{48,112},{64,0},{80,16},{96,32},{112,48},{1... | collective-permute-start | bytes 393224 | tf_op jit(solution)/shard_map/reply_cache_sum/ppermute | solution.py:358
  113.0 8.8 %collective-permute-start.18 = (bf16[256,256]{1,0:T(8,128)(2,1)S(1)}, bf16[256,256]{1,0:T(8,128)(2,1)S(1)}, u32[]{:S(2)}, u32[]{:S(2)}) collective-permute-start(bf16[256,256]{1,0:T(8,128)(2,1)S(1)} %add_convert_fusion.refs_0_), channel_id=1, source_target_pairs={{0,48},{16,0},{32,16},{48,32},{64,112},{80,64},{96,80},{112,96},{1... | collective-permute-start | bytes 393224 | tf_op jit(solution)/shard_map/reply_cache_sum/ppermute | solution.py:355
  116.1 7.9 %collective-permute-start.17 = (bf16[256,256]{1,0:T(8,128)(2,1)S(1)}, bf16[256,256]{1,0:T(8,128)(2,1)S(1)}, u32[]{:S(2)}, u32[]{:S(2)}) collective-permute-start(bf16[256,256]{1,0:T(8,128)(2,1)S(1)} %add_convert_fusion.refs_0_), channel_id=1, source_target_pairs={{0,32},{16,48},{32,0},{48,16},{64,96},{80,112},{96,64},{112,80},{1... | collective-permute-start | bytes 393224 | tf_op jit(solution)/shard_map/reply_cache_sum/ppermute | solution.py:355
  116.5 8.7 %collective-permute-start.16 = (bf16[256,256]{1,0:T(8,128)(2,1)S(1)}, bf16[256,256]{1,0:T(8,128)(2,1)S(1)}, u32[]{:S(2)}, u32[]{:S(2)}) collective-permute-start(bf16[256,256]{1,0:T(8,128)(2,1)S(1)} %add_convert_fusion.refs_0_), channel_id=1, source_target_pairs={{0,16},{16,32},{32,48},{48,0},{64,80},{80,96},{96,112},{112,64},{1... | collective-permute-start | bytes 393224 | tf_op jit(solution)/shard_map/reply_cache_sum/ppermute | solution.py:355
  117.9 8.1 %collective-permute-start.14 = (bf16[32,256]{1,0:T(8,128)(2,1)S(1)}, bf16[32,256]{1,0:T(8,128)(2,1)S(1)}, u32[]{:S(2)}, u32[]{:S(2)}) collective-permute-start(bf16[32,256]{1,0:T(8,128)(2,1)S(1)} %get-tuple-element.35), channel_id=1, source_target_pairs={{0,1},{1,0},{2,3},{3,2},{4,5},{5,4},{6,7},{7,6},{8,9},{9,8},{10,11... | collective-permute-start | bytes 49160 | tf_op jit(solution)/shard_map/prompt_cache_halves/ppermute | solution.py:351

commit v4 on v3

--- a/solution.py
+++ b/solution.py
@@ -149,19 +149,8 @@
     )(place, q, do, *caches, carried)
 
 
-def reply_kernel(
-    scaling, inner, other_count, other_order, scalars_ref, lengths_ref, owners_ref, q_ref, do_ref, own_ref, *refs
-):
-    caches, refs = refs[: -13 - inner], refs[-13 - inner :]
-    out_ref, dq_ref, other_sum_ref, mine_sum_ref = refs[:4]
-    own_pieces = refs[4 : 4 + inner]
-    picks_ref, q_t_ref, do_t_ref, results, grad, own_grad, score_ref, weight_ref, slope_ref = refs[4 + inner :]
-    others, mines = caches[:other_count], caches[other_count:]
-    capacity, head = q_ref.shape
-    length = grad.shape[0]
+def ranking(scalars_ref, lengths_ref, owners_ref):
     slots = lengths_ref.shape[0]
-    window = capacity // 2
-
     starts, ranks, counts = [], [], []
     total = jnp.int32(0)
     edges = [total]
@@ -187,13 +176,73 @@
             start = jnp.where(inside, starts[s], start)
         return place, start
 
-    spread = q_t_ref.shape[1]
-    place_all, _ = located(lax.broadcasted_iota(jnp.int32, (1, spread), 1))
+    return starts, ranks, counts, edges, located
+
+
+def order_kernel(scalars_ref, lengths_ref, owners_ref, q_ref, do_ref, own_ref, picks_ref, q_t_ref, do_t_ref, staged_ref):
+    _, _, _, _, located = ranking(scalars_ref, lengths_ref, owners_ref)
+    place, _ = located(lax.broadcasted_iota(jnp.int32, (1, picks_ref.shape[1]), 1))
     picks_ref[...] = jnp.where(
-        lax.broadcasted_iota(jnp.int32, (capacity, spread), 0) == place_all, 1.0, 0.0
+        lax.broadcasted_iota(jnp.int32, picks_ref.shape, 0) == place, 1.0, 0.0
     ).astype(BF16)
     q_t_ref[...] = dot(turned(q_ref[...]), picks_ref[...], 1, 0).astype(BF16)
     do_t_ref[...] = dot(turned(do_ref[...]), picks_ref[...], 1, 0).astype(BF16)
+    staged_ref[...] = own_ref[...]
+
+
+def order_rows(scalars, lengths, owners, q, do, own):
+    capacity, head = q.shape
+    spread = capacity + ROWS
+    return pl.pallas_call(
+        order_kernel,
+        out_shape=[
+            jax.ShapeDtypeStruct((capacity, spread), BF16),
+            jax.ShapeDtypeStruct((head, spread), BF16),
+            jax.ShapeDtypeStruct((head, spread), BF16),
+            jax.ShapeDtypeStruct(own.shape, BF16),
+        ],
+        in_specs=[pl.BlockSpec(memory_space=pltpu.SMEM)] * 3 + [pl.BlockSpec(memory_space=pltpu.VMEM)] * 3,
+        out_specs=[pl.BlockSpec(memory_space=pltpu.VMEM)] * 4,
+        compiler_params=pltpu.CompilerParams(vmem_limit_bytes=16 * 1024 * 1024),
+        cost_estimate=pl.CostEstimate(flops=4 * capacity * spread * head, bytes_accessed=8 * capacity * spread, transcendentals=0),
+        name="order_rows",
+    )(scalars, lengths, owners, q, do, own)
+
+
+def stack_kernel(after_ref, *refs):
+    *pieces, out_ref = refs
+    at = 0
+    for ref in pieces:
+        out_ref[at : at + ref.shape[0], :] = ref[...]
+        at += ref.shape[0]
+
+
+def stack_after(after, pieces):
+    rows = sum(x.shape[0] for x in pieces)
+    return pl.pallas_call(
+        stack_kernel,
+        out_shape=jax.ShapeDtypeStruct((rows, pieces[0].shape[1]), BF16),
+        in_specs=[pl.BlockSpec(memory_space=pl.ANY)] + [pl.BlockSpec(memory_space=pltpu.VMEM)] * len(pieces),
+        out_specs=pl.BlockSpec(memory_space=pltpu.VMEM),
+        compiler_params=pltpu.CompilerParams(vmem_limit_bytes=8 * 1024 * 1024),
+        name="stack_after",
+    )(after, *pieces)
+
+
+def reply_kernel(
+    scaling, inner, other_count, other_order, scalars_ref, lengths_ref, owners_ref, picks_ref, q_t_ref, do_t_ref, own_ref, *refs
+):
+    caches, refs = refs[: -10 - inner], refs[-10 - inner :]
+    out_ref, dq_ref, other_sum_ref, mine_sum_ref = refs[:4]
+    own_pieces = refs[4 : 4 + inner]
+    results, grad, own_grad, score_ref, weight_ref, slope_ref = refs[4 + inner :]
+    others, mines = caches[:other_count], caches[other_count:]
+    capacity, head = own_ref.shape[0], own_ref.shape[1] // 2
+    length = grad.shape[0]
+    slots = lengths_ref.shape[0]
+    window = capacity // 2
+
+    starts, ranks, counts, edges, located = ranking(scalars_ref, lengths_ref, owners_ref)
     results[...] = jnp.zeros_like(results)
     own_grad[...] = jnp.zeros_like(own_grad)
 
@@ -255,8 +304,8 @@
             ref[outer * share : (outer + 1) * share, :] = own_grad[pl.ds(at, share), :].astype(BF16)
 
 
-def reply_pass(scalars, inner, lengths, owners, q, do, own, others, other_order, mines, scaling):
-    capacity, head = q.shape
+def reply_pass(scalars, inner, lengths, owners, ordered, others, other_order, mines, scaling):
+    capacity, head = ordered[3].shape[0], ordered[3].shape[1] // 2
     length = sum(part.shape[0] for part in mines)
     spread = capacity + ROWS
     return pl.pallas_call(
@@ -268,12 +317,9 @@
             jax.ShapeDtypeStruct((length, 2 * head), BF16),
         ]
         + [jax.ShapeDtypeStruct((capacity // inner, 2 * head), BF16)] * inner,
-        in_specs=[pl.BlockSpec(memory_space=pltpu.SMEM)] * 3 + [pl.BlockSpec(memory_space=pltpu.VMEM)] * (3 + len(others) + len(mines)),
+        in_specs=[pl.BlockSpec(memory_space=pltpu.SMEM)] * 3 + [pl.BlockSpec(memory_space=pltpu.VMEM)] * (len(ordered) + len(others) + len(mines)),
         out_specs=[pl.BlockSpec(memory_space=pltpu.VMEM)] * (4 + inner),
         scratch_shapes=[
-            pltpu.VMEM((capacity, spread), BF16),
-            pltpu.VMEM((head, spread), BF16),
-            pltpu.VMEM((head, spread), BF16),
             pltpu.VMEM((spread, 2 * head), BF16),
             pltpu.VMEM((length, 2 * head), F32),
             pltpu.VMEM((capacity, 2 * head), F32),
@@ -284,7 +330,7 @@
         compiler_params=pltpu.CompilerParams(vmem_limit_bytes=36 * 1024 * 1024),
         cost_estimate=pl.CostEstimate(flops=24 * capacity * length * head, bytes_accessed=16 * length * head, transcendentals=0),
         name="reply_pass",
-    )(scalars, lengths, owners, q, do, own, *others, *mines)
+    )(scalars, lengths, owners, *ordered, *others, *mines)
 
 
 def place_kernel(inner, place_ref, *refs):
@@ -367,22 +413,26 @@
                 pairs.append((ctx * comp_count + comp, to_ctx * comp_count + to_comp))
         return lax.ppermute(x, ("ctx", "comp"), pairs)
 
+    reply_scalars = (jnp.concatenate([place, group]), reply_lengths[0], reply_owner[0])
+    with jax.named_scope("order_rows"):
+        ordered = order_rows(*reply_scalars, reply_query, reply_cotangent, reply_cache)
     with jax.named_scope("gather_keys"):
         own = prompt_cache[0]
-        next_1, next_3, next_2 = along_z(own, 1), along_z(own, inner - 1), along_z(own, 2)
+        next_1, next_3 = along_z(own, 1), along_z(own, inner - 1)
         y_0 = along_y(own, 1)
+        half = own.shape[0] // 2
+        next_2a, next_2b = along_z(next_1[:half], 1), along_z(next_3[half:], inner - 1)
         y_1, y_3 = along_y(next_1, 1), along_y(next_3, -1)
-        half = own.shape[0] // 2
-        y_2a, y_2b = along_y(next_2[:half], 1), along_y(next_2[half:], -1)
-        mines = [own, next_1, next_2, next_3, y_0, y_1, y_2a, y_2b, y_3]
-        early, late = [own, next_1, next_3], [next_2, y_0, y_1, y_2a, y_2b, y_3]
-        others = [swap(jnp.concatenate(part, axis=0)) for part in (early, late)]
+        y_2a, y_2b = along_y(next_2a, 1), along_y(next_2b, -1)
+        mines = [own, next_1, next_2a, next_2b, next_3, y_0, y_1, y_2a, y_2b, y_3]
+        early, late = [own, next_1, next_3], [next_2a, next_2b, y_0, y_1, y_2a, y_2b, y_3]
+        others = [swap(jnp.concatenate(early, axis=0)), swap(stack_after(ordered[3], late))]
         other_order = (0, 1, 3, 2, 4, 5, 6, 7)
 
     with jax.named_scope("reply_rows"):
+        scalars, lengths, owners = reply_scalars
         reply_out, reply_dq, other_sum, mine_sum, *own_pieces = reply_pass(
-            jnp.concatenate([place, group]), inner, reply_lengths[0], reply_owner[0], reply_query, reply_cotangent, reply_cache,
-            others, other_order, mines, scaling,
+            scalars, inner, lengths, owners, ordered, others, other_order, mines, scaling
         )
     arrived = swap(other_sum)
     with jax.named_scope("prompt_rows"):

time: 127 us -> 124 us (0.976); the launches traced: 127 us -> 122 us
  starting transfers between devices: 39.4 us -> 33.7 us
  Pallas kernels: 32.9 us -> 37.4 us
  local copies, waits for them, and re-layouts: 7.19 us -> 4.29 us
    all_to_all x1, starting transfers between devices: 13 us -> 6.8 us  [per_device(): lax.all_to_all(shares.reshape(count, -1, width), ('ctx', 'comp'), 0, 0, t...]
    pallas_call x1, Pallas kernels: 22 us -> 24.4 us  [reply_pass(): pl.pallas_call(functools.partial(reply_kernel, scaling, inner, len(others...]
    unnamed x21 -> x20, local copies, waits for them, and re-layouts: 6.46 us -> 4.28 us
    ppermute x9 -> x10, starting transfers between devices: 14.7 us -> 16.8 us  [along_z(): return lax.ppermute(x, 'ctx', pairs)]
    pallas_call x0 -> x2, Pallas kernels: none -> 1.87 us  [the longest x1 1.79 us: order_rows(): pl.pallas_call(order_kernel, out_shape=[jax.ShapeDtypeStruct((capacity, s...]
    ppermute x9 -> x10, waiting for transfers between devices: 14.9 us -> 13.1 us  [along_z(): return lax.ppermute(x, 'ctx', pairs)]
    ppermute x5, starting transfers between devices: 9.47 us -> 7.73 us  [along_y(): return lax.ppermute(x, ('ctx', 'comp'), pairs)]
    ppermute x5, waiting for transfers between devices: 1.35 us -> 2.98 us  [along_y(): return lax.ppermute(x, ('ctx', 'comp'), pairs)]
  transfers between devices with their start and end apart: 20 -> 21, of which waited for: 9 -> 7; matrix products, arithmetic and copies ran while one was open for 4% -> 0% of each run, Pallas kernels for 7% -> 9%
where the time goes in v4:
time: 124 us; the launch traced here: 122 us
  waiting for transfers between devices  44.8 us (36%)
  Pallas kernels  37.4 us (30%)
  starting transfers between devices  33.7 us (27%)
  local copies, waits for them, and re-layouts  4.29 us (3%)
    ppermute x1, waiting for transfers between devices, outer_swap(): lax.ppermute(x, 'ctx', [(i, (i + inner) % ctx_count) for i in range(ctx_c...  25.2 us
    pallas_call x1, Pallas kernels, reply_pass(): pl.pallas_call(functools.partial(reply_kernel, scaling, inner, len(others...  24.4 us
    ppermute x10, starting transfers between devices, along_z(): return lax.ppermute(x, 'ctx', pairs)  16.8 us
    ppermute x10, waiting for transfers between devices, along_z(): return lax.ppermute(x, 'ctx', pairs)  13.1 us
    pallas_call x1, Pallas kernels, prompt_pass(): pl.pallas_call(functools.partial(prompt_kernel, scaling, inner), out_shap...  8.45 us
    ppermute x5, starting transfers between devices, along_y(): return lax.ppermute(x, ('ctx', 'comp'), pairs)  7.73 us
    all_to_all x1, starting transfers between devices, per_device(): lax.all_to_all(shares.reshape(count, -1, width), ('ctx', 'comp'), 0, 0, t...  6.8 us
    unnamed x20, local copies, waits for them, and re-layouts  4.28 us
  transfers between devices with their start and end apart: 21, of which 7 were waited for; matrix products, arithmetic and copies ran while one was open for 0% of the time, Pallas kernels for 9%

profile of v4, /device:TPU:4, one launch (start us, length us, event | category | flops | bytes accessed | tf_op | source)
XLA Modules:
  0.0 122.1 jit_solution(14646323047571937453)
XLA Ops:
  0.6 4.1 %collective-permute-start.2 = (bf16[512,256]{1,0:T(8,128)(2,1)}, bf16[512,256]{1,0:T(8,128)(2,1)S(1)}, u32[]{:S(2)}, u32[]{:S(2)}) collective-permute-start(bf16[512,256]{1,0:T(8,128)(2,1)} %bitcast.13), channel_id=1, source_target_pairs={{0,48},{16,0},{32,16},{48,32},{64,112},{80,64},{96,80},{112,96},{1... | collective-permute-start | bytes 786440 | tf_op jit(solution)/shard_map/gather_keys/ppermute | solution.py:401
  4.7 5.9 %collective-permute-done.2.refs_6_.refs_4_ = bf16[512,256]{1,0:T(8,128)(2,1)S(1)} collective-permute-done((bf16[512,256]{1,0:T(8,128)(2,1)}, bf16[512,256]{1,0:T(8,128)(2,1)S(1)}, u32[]{:S(2)}, u32[]{:S(2)}) %collective-permute-start.2) | collective-permute-done | bytes 262176 | tf_op jit(solution)/shard_map/gather_keys/ppermute | solution.py:401
  10.6 3.7 %collective-permute-start.3 = (bf16[256,256]{1,0:T(8,128)(2,1)S(1)}, bf16[256,256]{1,0:T(8,128)(2,1)S(1)}, u32[]{:S(2)}, u32[]{:S(2)}) collective-permute-start(bf16[256,256]{1,0:T(8,128)(2,1)S(1)} %slice.17), channel_id=1, source_target_pairs={{0,48},{16,0},{32,16},{48,32},{64,112},{80,64},{96,80},{112,96},{1... | collective-permute-start | bytes 393224 | tf_op jit(solution)/shard_map/gather_keys/ppermute | solution.py:401
  14.4 1.6 %collective-permute-start.4 = (bf16[512,256]{1,0:T(8,128)(2,1)}, bf16[512,256]{1,0:T(8,128)(2,1)S(1)}, u32[]{:S(2)}, u32[]{:S(2)}) collective-permute-start(bf16[512,256]{1,0:T(8,128)(2,1)} %bitcast.15), channel_id=1, source_target_pairs={{0,64},{2,66},{4,68},{6,70},{8,72},{10,74},{12,76},{14,78},{16,80}... | collective-permute-start | bytes 786440 | tf_op jit(solution)/shard_map/gather_keys/ppermute | solution.py:414
  16.0 1.7 %collective-permute-start.8 = (bf16[512,256]{1,0:T(8,128)(2,1)S(1)}, bf16[512,256]{1,0:T(8,128)(2,1)S(1)}, u32[]{:S(2)}, u32[]{:S(2)}) collective-permute-start(bf16[512,256]{1,0:T(8,128)(2,1)S(1)} %collective-permute-done.2.refs_6_.refs_4_), channel_id=1, source_target_pairs={{0,72},{2,74},{4,76},{6,78},{8,64},{10,66},{12,68},{14,70},{16,88}... | collective-permute-start | bytes 786440 | tf_op jit(solution)/shard_map/gather_keys/ppermute | solution.py:414
  17.7 0.4 collective-permute-start.5
  18.1 2.9 %collective-permute-start.7 = (bf16[256,256]{1,0:T(8,128)(2,1)S(1)}, bf16[256,256]{1,0:T(8,128)(2,1)S(1)}, u32[]{:S(2)}, u32[]{:S(2)}) collective-permute-start(bf16[256,256]{1,0:T(8,128)(2,1)S(1)} %collective-permute-done.3.refs_1_.refs_5_.refs_3_), channel_id=1, source_target_pairs={{0,72},{2,74},{4,76},{6,78},{8,64},{10,66},{12,68},{14,70},{16,88}... | collective-permute-start | bytes 393224 | tf_op jit(solution)/shard_map/gather_keys/ppermute | solution.py:414
  20.9 1.2 collective-permute-start.6
  22.2 1.0 copy-done.1
  23.2 0.9 copy-done.2
  24.2 0.9 copy-done.3
  25.1 0.7 copy-done.6
  25.8 0.7 copy-done.8
  26.5 1.8 %order_rows.1 = (bf16[1024,1280]{1,0:T(8,128)(2,1)S(1)}, bf16[128,1280]{1,0:T(8,128)(2,1)S(1)}, bf16[128,1280]{1,0:T(8,128)(2,1)S(1)}, bf16[1024,256]{1,0:T(8,128)(2,1)S(1)}) custom-call(s32[2]{0:T(128)S(1)} %pad_add_fusion.scalars_ref, s32[4]{0:T(128)S(1)} %bitcast.21, s32[4]{0:T(128)S(1)} %bitcast.23, bf16[1024,128]{1,0:T(8,128)(2,1)S(1)} %copy-done.2, ...), custom_call_target="tpu_custom_call" | custom-call | flops 671088640 | bytes 10485760 | tf_op jit(solution)/shard_map/order_rows/order_rows/pallas_call | solution.py:196
  28.3 3.0 %collective-permute-done.6.refs_4_.refs_9_.refs_7_ = bf16[256,256]{1,0:T(8,128)(2,1)S(1)} collective-permute-done((bf16[256,256]{1,0:T(8,128)(2,1)S(1)}, bf16[256,256]{1,0:T(8,128)(2,1)S(1)}, u32[]{:S(2)}, u32[]{:S(2)}) %collective-permute-start.6) | collective-permute-done | bytes 131104 | tf_op jit(solution)/shard_map/gather_keys/ppermute | solution.py:414
  31.5 0.6 collective-permute-start.9
  32.1 3.5 %collective-permute-done.9.refs_0_ = bf16[1536,256]{1,0:T(8,128)(2,1)S(1)} collective-permute-done((bf16[1536,256]{1,0:T(8,128)(2,1)S(1)}, bf16[1536,256]{1,0:T(8,128)(2,1)S(1)}, u32[]{:S(2)}, u32[]{:S(2)}) %collective-permute-start.9) | collective-permute-done | bytes 786464 | tf_op jit(solution)/shard_map/gather_keys/ppermute | solution.py:397
  35.6 24.4 %reply_pass.1 = (bf16[1024,128]{1,0:T(8,128)(2,1)}, bf16[1024,128]{1,0:T(8,128)(2,1)}, bf16[4096,256]{1,0:T(8,128)(2,1)S(1)}, bf16[4096,256]{1,0:T(8,128)(2,1)S(...) custom-call(s32[2]{0:T(128)S(1)} %pad_add_fusion.scalars_ref, ...), custom_call_target="tpu_custom_call" | custom-call | flops 12884901888 | bytes 8388608 | tf_op jit(solution)/shard_map/reply_rows/reply_pass/pallas_call | solution.py:311
  60.1 4.3 %collective-permute-start.13 = (bf16[256,256]{1,0:T(8,128)(2,1)S(1)}, bf16[256,256]{1,0:T(8,128)(2,1)S(1)}, u32[]{:S(2)}, u32[]{:S(2)}) collective-permute-start(bf16[256,256]{1,0:T(8,128)(2,1)S(1)} %get-tuple-element.34), channel_id=1, source_target_pairs={{0,32},{16,48},{32,0},{48,16},{64,96},{80,112},{96,64},{112,80},{1... | collective-permute-start | bytes 393224 | tf_op jit(solution)/shard_map/prompt_cache_sum/ppermute | solution.py:401
  64.4 8.5 %prompt_pass.1 = (bf16[512,128]{1,0:T(8,128)(2,1)}, bf16[512,128]{1,0:T(8,128)(2,1)}, bf16[4096,256]{1,0:T(8,128)(2,1)S(1)}) custom-call(s32[1]{0:T(128)} %bitcast.place_ref, bf16[512,128]{1,0:T(8,128)(2,1)S(1)} %bitcast.19, bf16[512,128]{1,0:T(8,128)(2,1)S(1)} %bitcast.20, bf16[512,256]{1,0:T(8,128)(2,1)S(1)} %bitcast.18, ...), custom_call_target="tpu_custom_call" | custom-call | flops 6442450944 | bytes 4194304 | tf_op jit(solution)/shard_map/prompt_rows/prompt_pass/pallas_call | solution.py:132
  72.9 1.8 %join_sums.1 = (bf16[4096,256]{1,0:T(8,128)(2,1)}, bf16[256,256]{1,0:T(8,128)(2,1)S(1)}) custom-call(bf16[4096,256]{1,0:T(8,128)(2,1)S(1)} %get-tuple-element.30.total_ref, bf16[4096,256]{1,0:T(8,128)(2,1)S(1)} %collective-permute-done.11.arrived_ref, bf16[256,256]{1,0:T(8,128)(2,1)S(1)} %get-tuple-element.32.refs_0_, ...), custom_call_target="tpu_custom_call" | custom-call | tf_op jit(solution)/shard_map/prompt_cache_sum/join_sums/pallas_call | solution.py:368
  74.7 6.8 %all-to-all-start = ((bf16[64,64,256]{2,1,0:T(8,128)(2,1)}), bf16[64,64,256]{2,1,0:T(8,128)(2,1)S(1)}, u32[]{:S(2)}, u32[]{:S(2)}) async-start(bf16[64,64,256]{2,1,0:T(8,128)(2,1)} %bitcast.9), calls=%async_computation | async-start | bytes 4194304 | tf_op jit(solution)/shard_map/prompt_cache_sum/all_to_all | solution.py:447
  81.5 1.7 %collective-permute-start.16 = (bf16[256,256]{1,0:T(8,128)(2,1)S(1)}, bf16[256,256]{1,0:T(8,128)(2,1)S(1)}, u32[]{:S(2)}, u32[]{:S(2)}) collective-permute-start(bf16[256,256]{1,0:T(8,128)(2,1)S(1)} %get-tuple-element.39), channel_id=1, source_target_pairs={{0,64},{16,80},{32,96},{48,112},{64,0},{80,16},{96,32},{112,48},{1... | collective-permute-start | bytes 393224 | tf_op jit(solution)/shard_map/reply_cache_sum/ppermute | solution.py:404
  83.2 25.2 %collective-permute-done.16 = bf16[256,256]{1,0:T(8,128)(2,1)S(1)} collective-permute-done((bf16[256,256]{1,0:T(8,128)(2,1)S(1)}, bf16[256,256]{1,0:T(8,128)(2,1)S(1)}, u32[]{:S(2)}, u32[]{:S(2)}) %collective-permute-start.16) | collective-permute-done | bytes 131104 | tf_op jit(solution)/shard_map/reply_cache_sum/ppermute | solution.py:404
  108.4 3.1 %collective-permute-start.19 = (bf16[256,256]{1,0:T(8,128)(2,1)S(1)}, bf16[256,256]{1,0:T(8,128)(2,1)S(1)}, u32[]{:S(2)}, u32[]{:S(2)}) collective-permute-start(bf16[256,256]{1,0:T(8,128)(2,1)S(1)} %add_convert_fusion.refs_0_), channel_id=1, source_target_pairs={{0,48},{16,0},{32,16},{48,32},{64,112},{80,64},{96,80},{112,96},{1... | collective-permute-start | bytes 393224 | tf_op jit(solution)/shard_map/reply_cache_sum/ppermute | solution.py:401
  111.6 0.3 collective-permute-start.18
  111.9 1.1 collective-permute-start.17
  113.4 3.8 %collective-permute-done.19.refs_3_ = bf16[256,256]{1,0:T(8,128)(2,1)S(1)} collective-permute-done((bf16[256,256]{1,0:T(8,128)(2,1)S(1)}, bf16[256,256]{1,0:T(8,128)(2,1)S(1)}, u32[]{:S(2)}, u32[]{:S(2)}) %collective-permute-start.19) | collective-permute-done | bytes 131104 | tf_op jit(solution)/shard_map/reply_cache_sum/ppermute | solution.py:401
  117.2 2.3 %collective-permute-done.18.refs_2_ = bf16[256,256]{1,0:T(8,128)(2,1)S(1)} collective-permute-done((bf16[256,256]{1,0:T(8,128)(2,1)S(1)}, bf16[256,256]{1,0:T(8,128)(2,1)S(1)}, u32[]{:S(2)}, u32[]{:S(2)}) %collective-permute-start.18) | collective-permute-done | bytes 131104 | tf_op jit(solution)/shard_map/reply_cache_sum/ppermute | solution.py:401
  119.5 1.2 collective-permute-done.17.refs_1_
  120.6 0.8 placed_in_order.1
  121.5 0.6 maximum_select_fusion
  (44 shorter events, 0.9 us)
Async XLA Ops:
  0.6 10.0 %collective-permute-start.2 = (bf16[512,256]{1,0:T(8,128)(2,1)}, bf16[512,256]{1,0:T(8,128)(2,1)S(1)}, u32[]{:S(2)}, u32[]{:S(2)}) collective-permute-start(bf16[512,256]{1,0:T(8,128)(2,1)} %bitcast.13), channel_id=1, source_target_pairs={{0,48},{16,0},{32,16},{48,32},{64,112},{80,64},{96,80},{112,96},{1... | collective-permute-start | bytes 786440 | tf_op jit(solution)/shard_map/gather_keys/ppermute | solution.py:401
  4.7 9.6 %collective-permute-start = (bf16[512,256]{1,0:T(8,128)(2,1)}, bf16[512,256]{1,0:T(8,128)(2,1)S(1)}, u32[]{:S(2)}, u32[]{:S(2)}) collective-permute-start(bf16[512,256]{1,0:T(8,128)(2,1)} %bitcast.14), channel_id=1, source_target_pairs={{0,16},{16,32},{32,48},{48,0},{64,80},{80,96},{96,112},{112,64},{1... | collective-permute-start | bytes 786440 | tf_op jit(solution)/shard_map/gather_keys/ppermute | solution.py:401
  10.6 7.4 %collective-permute-start.3 = (bf16[256,256]{1,0:T(8,128)(2,1)S(1)}, bf16[256,256]{1,0:T(8,128)(2,1)S(1)}, u32[]{:S(2)}, u32[]{:S(2)}) collective-permute-start(bf16[256,256]{1,0:T(8,128)(2,1)S(1)} %slice.17), channel_id=1, source_target_pairs={{0,48},{16,0},{32,16},{48,32},{64,112},{80,64},{96,80},{112,96},{1... | collective-permute-start | bytes 393224 | tf_op jit(solution)/shard_map/gather_keys/ppermute | solution.py:401
  14.3 6.6 %collective-permute-start.1 = (bf16[256,256]{1,0:T(8,128)(2,1)S(1)}, bf16[256,256]{1,0:T(8,128)(2,1)S(1)}, u32[]{:S(2)}, u32[]{:S(2)}) collective-permute-start(bf16[256,256]{1,0:T(8,128)(2,1)S(1)} %slice.16), channel_id=1, source_target_pairs={{0,16},{16,32},{32,48},{48,0},{64,80},{80,96},{96,112},{112,64},{1... | collective-permute-start | bytes 393224 | tf_op jit(solution)/shard_map/gather_keys/ppermute | solution.py:401
  14.4 13.9 %collective-permute-start.4 = (bf16[512,256]{1,0:T(8,128)(2,1)}, bf16[512,256]{1,0:T(8,128)(2,1)S(1)}, u32[]{:S(2)}, u32[]{:S(2)}) collective-permute-start(bf16[512,256]{1,0:T(8,128)(2,1)} %bitcast.15), channel_id=1, source_target_pairs={{0,64},{2,66},{4,68},{6,70},{8,72},{10,74},{12,76},{14,78},{16,80}... | collective-permute-start | bytes 786440 | tf_op jit(solution)/shard_map/gather_keys/ppermute | solution.py:414
  16.0 12.3 %collective-permute-start.8 = (bf16[512,256]{1,0:T(8,128)(2,1)S(1)}, bf16[512,256]{1,0:T(8,128)(2,1)S(1)}, u32[]{:S(2)}, u32[]{:S(2)}) collective-permute-start(bf16[512,256]{1,0:T(8,128)(2,1)S(1)} %collective-permute-done.2.refs_6_.refs_4_), channel_id=1, source_target_pairs={{0,72},{2,74},{4,76},{6,78},{8,64},{10,66},{12,68},{14,70},{16,88}... | collective-permute-start | bytes 786440 | tf_op jit(solution)/shard_map/gather_keys/ppermute | solution.py:414
  17.7 13.6 %collective-permute-start.5 = (bf16[512,256]{1,0:T(8,128)(2,1)S(1)}, bf16[512,256]{1,0:T(8,128)(2,1)S(1)}, u32[]{:S(2)}, u32[]{:S(2)}) collective-permute-start(bf16[512,256]{1,0:T(8,128)(2,1)S(1)} %collective-permute-done.refs_3_.refs_1_), channel_id=1, source_target_pairs={{0,64},{2,66},{4,68},{6,70},{8,72},{10,74},{12,76},{14,78},{16,80}... | collective-permute-start | bytes 786440 | tf_op jit(solution)/shard_map/gather_keys/ppermute | solution.py:414
  18.1 10.2 %collective-permute-start.7 = (bf16[256,256]{1,0:T(8,128)(2,1)S(1)}, bf16[256,256]{1,0:T(8,128)(2,1)S(1)}, u32[]{:S(2)}, u32[]{:S(2)}) collective-permute-start(bf16[256,256]{1,0:T(8,128)(2,1)S(1)} %collective-permute-done.3.refs_1_.refs_5_.refs_3_), channel_id=1, source_target_pairs={{0,72},{2,74},{4,76},{6,78},{8,64},{10,66},{12,68},{14,70},{16,88}... | collective-permute-start | bytes 393224 | tf_op jit(solution)/shard_map/gather_keys/ppermute | solution.py:414
  20.9 10.3 %collective-permute-start.6 = (bf16[256,256]{1,0:T(8,128)(2,1)S(1)}, bf16[256,256]{1,0:T(8,128)(2,1)S(1)}, u32[]{:S(2)}, u32[]{:S(2)}) collective-permute-start(bf16[256,256]{1,0:T(8,128)(2,1)S(1)} %collective-permute-done.1.refs_0_.refs_4_.refs_2_), channel_id=1, source_target_pairs={{0,64},{2,66},{4,68},{6,70},{8,72},{10,74},{12,76},{14,78},{16,80}... | collective-permute-start | bytes 393224 | tf_op jit(solution)/shard_map/gather_keys/ppermute | solution.py:414
  22.2 1.0 copy-start.1
  23.2 0.9 copy-start.2
  24.2 0.9 copy-start.3
  25.1 0.7 copy-start.6
  25.8 0.7 copy-start.8
  28.3 3.2 %copy-start = (bf16[1,512,256]{2,1,0:T(8,128)(2,1)S(1)}, bf16[1,512,256]{2,1,0:T(8,128)(2,1)}, u32[]{:S(2)}) copy-start(bf16[1,512,256]{2,1,0:T(8,128)(2,1)} %param.9) | copy-start | bytes 786436
  31.3 4.3 %copy-start.7 = (s32[1,4]{1,0:T(1,128)S(1)}, s32[1,4]{1,0:T(1,128)}, u32[]{:S(2)}) copy-start(s32[1,4]{1,0:T(1,128)} %param.14) | copy-start | bytes 52
  31.3 4.3 %copy-start.9 = (s32[1,4]{1,0:T(1,128)S(1)}, s32[1,4]{1,0:T(1,128)}, u32[]{:S(2)}) copy-start(s32[1,4]{1,0:T(1,128)} %param.15) | copy-start | bytes 52
  31.4 4.2 %collective-permute-start.10 = (bf16[2560,256]{1,0:T(8,128)(2,1)S(1)}, bf16[2560,256]{1,0:T(8,128)(2,1)S(1)}, u32[]{:S(2)}, u32[]{:S(2)}) collective-permute-start(bf16[2560,256]{1,0:T(8,128)(2,1)S(1)} %stack_after.1), channel_id=1, source_target_pairs={{0,1},{1,0},{2,3},{3,2},{4,5},{5,4},{6,7},{7,6},{8,9},{9,8},{10,11... | collective-permute-start | bytes 3932168 | tf_op jit(solution)/shard_map/gather_keys/ppermute | solution.py:397
  31.5 4.1 %collective-permute-start.9 = (bf16[1536,256]{1,0:T(8,128)(2,1)S(1)}, bf16[1536,256]{1,0:T(8,128)(2,1)S(1)}, u32[]{:S(2)}, u32[]{:S(2)}) collective-permute-start(bf16[1536,256]{1,0:T(8,128)(2,1)S(1)} %pad_maximum_fusion), channel_id=1, source_target_pairs={{0,1},{1,0},{2,3},{3,2},{4,5},{5,4},{6,7},{7,6},{8,9},{9,8},{10,11... | collective-permute-start | bytes 2359304 | tf_op jit(solution)/shard_map/gather_keys/ppermute | solution.py:397
  35.6 28.8 %copy-start.4 = (bf16[1,512,128]{2,1,0:T(8,128)(2,1)S(1)}, bf16[1,512,128]{2,1,0:T(8,128)(2,1)}, u32[]{:S(2)}) copy-start(bf16[1,512,128]{2,1,0:T(8,128)(2,1)} %param.8) | copy-start | bytes 393220
  35.6 28.8 %copy-start.5 = (bf16[1,512,128]{2,1,0:T(8,128)(2,1)S(1)}, bf16[1,512,128]{2,1,0:T(8,128)(2,1)}, u32[]{:S(2)}) copy-start(bf16[1,512,128]{2,1,0:T(8,128)(2,1)} %param.10) | copy-start | bytes 393220
  60.1 12.8 %collective-permute-start.11 = (bf16[4096,256]{1,0:T(8,128)(2,1)S(1)}, bf16[4096,256]{1,0:T(8,128)(2,1)S(1)}, u32[]{:S(2)}, u32[]{:S(2)}) collective-permute-start(bf16[4096,256]{1,0:T(8,128)(2,1)S(1)} %get-tuple-element.31), channel_id=1, source_target_pairs={{0,1},{1,0},{2,3},{3,2},{4,5},{5,4},{6,7},{7,6},{8,9},{9,8},{10,11... | collective-permute-start | bytes 6291464 | tf_op jit(solution)/shard_map/ppermute | solution.py:397
  60.1 12.8 %collective-permute-start.12 = (bf16[256,256]{1,0:T(8,128)(2,1)S(1)}, bf16[256,256]{1,0:T(8,128)(2,1)S(1)}, u32[]{:S(2)}, u32[]{:S(2)}) collective-permute-start(bf16[256,256]{1,0:T(8,128)(2,1)S(1)} %get-tuple-element.33), channel_id=1, source_target_pairs={{0,16},{16,32},{32,48},{48,0},{64,80},{80,96},{96,112},{112,64},{1... | collective-permute-start | bytes 393224 | tf_op jit(solution)/shard_map/prompt_cache_sum/ppermute | solution.py:401
  60.1 12.8 %collective-permute-start.13 = (bf16[256,256]{1,0:T(8,128)(2,1)S(1)}, bf16[256,256]{1,0:T(8,128)(2,1)S(1)}, u32[]{:S(2)}, u32[]{:S(2)}) collective-permute-start(bf16[256,256]{1,0:T(8,128)(2,1)S(1)} %get-tuple-element.34), channel_id=1, source_target_pairs={{0,32},{16,48},{32,0},{48,16},{64,96},{80,112},{96,64},{112,80},{1... | collective-permute-start | bytes 393224 | tf_op jit(solution)/shard_map/prompt_cache_sum/ppermute | solution.py:401
  64.4 8.5 %collective-permute-start.14 = (bf16[256,256]{1,0:T(8,128)(2,1)S(1)}, bf16[256,256]{1,0:T(8,128)(2,1)S(1)}, u32[]{:S(2)}, u32[]{:S(2)}) collective-permute-start(bf16[256,256]{1,0:T(8,128)(2,1)S(1)} %get-tuple-element.35), channel_id=1, source_target_pairs={{0,48},{16,0},{32,16},{48,32},{64,112},{80,64},{96,80},{112,96},{1... | collective-permute-start | bytes 393224 | tf_op jit(solution)/shard_map/prompt_cache_sum/ppermute | solution.py:401
  74.7 38.3 %all-to-all-start = ((bf16[64,64,256]{2,1,0:T(8,128)(2,1)}), bf16[64,64,256]{2,1,0:T(8,128)(2,1)S(1)}, u32[]{:S(2)}, u32[]{:S(2)}) async-start(bf16[64,64,256]{2,1,0:T(8,128)(2,1)} %bitcast.9), calls=%async_computation | async-start | bytes 4194304 | tf_op jit(solution)/shard_map/prompt_cache_sum/all_to_all | solution.py:447
  81.5 26.8 %collective-permute-start.16 = (bf16[256,256]{1,0:T(8,128)(2,1)S(1)}, bf16[256,256]{1,0:T(8,128)(2,1)S(1)}, u32[]{:S(2)}, u32[]{:S(2)}) collective-permute-start(bf16[256,256]{1,0:T(8,128)(2,1)S(1)} %get-tuple-element.39), channel_id=1, source_target_pairs={{0,64},{16,80},{32,96},{48,112},{64,0},{80,16},{96,32},{112,48},{1... | collective-permute-start | bytes 393224 | tf_op jit(solution)/shard_map/reply_cache_sum/ppermute | solution.py:404
  108.4 8.8 %collective-permute-start.19 = (bf16[256,256]{1,0:T(8,128)(2,1)S(1)}, bf16[256,256]{1,0:T(8,128)(2,1)S(1)}, u32[]{:S(2)}, u32[]{:S(2)}) collective-permute-start(bf16[256,256]{1,0:T(8,128)(2,1)S(1)} %add_convert_fusion.refs_0_), channel_id=1, source_target_pairs={{0,48},{16,0},{32,16},{48,32},{64,112},{80,64},{96,80},{112,96},{1... | collective-permute-start | bytes 393224 | tf_op jit(solution)/shard_map/reply_cache_sum/ppermute | solution.py:401
  111.6 7.9 %collective-permute-start.18 = (bf16[256,256]{1,0:T(8,128)(2,1)S(1)}, bf16[256,256]{1,0:T(8,128)(2,1)S(1)}, u32[]{:S(2)}, u32[]{:S(2)}) collective-permute-start(bf16[256,256]{1,0:T(8,128)(2,1)S(1)} %add_convert_fusion.refs_0_), channel_id=1, source_target_pairs={{0,32},{16,48},{32,0},{48,16},{64,96},{80,112},{96,64},{112,80},{1... | collective-permute-start | bytes 393224 | tf_op jit(solution)/shard_map/reply_cache_sum/ppermute | solution.py:401
  111.9 8.7 %collective-permute-start.17 = (bf16[256,256]{1,0:T(8,128)(2,1)S(1)}, bf16[256,256]{1,0:T(8,128)(2,1)S(1)}, u32[]{:S(2)}, u32[]{:S(2)}) collective-permute-start(bf16[256,256]{1,0:T(8,128)(2,1)S(1)} %add_convert_fusion.refs_0_), channel_id=1, source_target_pairs={{0,16},{16,32},{32,48},{48,0},{64,80},{80,96},{96,112},{112,64},{1... | collective-permute-start | bytes 393224 | tf_op jit(solution)/shard_map/reply_cache_sum/ppermute | solution.py:401
  113.3 8.1 %collective-permute-start.15 = (bf16[32,256]{1,0:T(8,128)(2,1)S(1)}, bf16[32,256]{1,0:T(8,128)(2,1)S(1)}, u32[]{:S(2)}, u32[]{:S(2)}) collective-permute-start(bf16[32,256]{1,0:T(8,128)(2,1)S(1)} %get-tuple-element.41), channel_id=1, source_target_pairs={{0,1},{1,0},{2,3},{3,2},{4,5},{5,4},{6,7},{7,6},{8,9},{9,8},{10,11... | collective-permute-start | bytes 49160 | tf_op jit(solution)/shard_map/prompt_cache_halves/ppermute | solution.py:397

commit v5 on v4

--- a/solution.py
+++ b/solution.py
@@ -421,7 +421,8 @@
         next_1, next_3 = along_z(own, 1), along_z(own, inner - 1)
         y_0 = along_y(own, 1)
         half = own.shape[0] // 2
-        next_2a, next_2b = along_z(next_1[:half], 1), along_z(next_3[half:], inner - 1)
+        next_2a = along_z(stack_after(y_0, [next_1[:half]]), 1)
+        next_2b = along_z(stack_after(y_0, [next_3[half:]]), inner - 1)
         y_1, y_3 = along_y(next_1, 1), along_y(next_3, -1)
         y_2a, y_2b = along_y(next_2a, 1), along_y(next_2b, -1)
         mines = [own, next_1, next_2a, next_2b, next_3, y_0, y_1, y_2a, y_2b, y_3]

time: 124 us -> 119 us (0.960); the launches traced: 122 us -> 121 us
  starting transfers between devices: 33.7 us -> 31 us
    ppermute x10, starting transfers between devices: 16.8 us -> 13.4 us  [along_z(): return lax.ppermute(x, 'ctx', pairs)]
    all_to_all x1, starting transfers between devices: 6.8 us -> 8.44 us  [per_device(): lax.all_to_all(shares.reshape(count, -1, width), ('ctx', 'comp'), 0, 0, t...]
  transfers between devices with their start and end apart: 21 -> 21, of which waited for: 7 -> 10; matrix products, arithmetic and copies ran while one was open for 0% -> 0% of each run, Pallas kernels for 9% -> 9%
where the time goes in v5:
time: 119 us; the launch traced here: 121 us
  waiting for transfers between devices  45.3 us (38%)
  Pallas kernels  37.4 us (31%)
  starting transfers between devices  31 us (26%)
  local copies, waits for them, and re-layouts  4.98 us (4%)
    ppermute x1, waiting for transfers between devices, outer_swap(): lax.ppermute(x, 'ctx', [(i, (i + inner) % ctx_count) for i in range(ctx_c...  25.2 us
    pallas_call x1, Pallas kernels, reply_pass(): pl.pallas_call(functools.partial(reply_kernel, scaling, inner, len(others...  24.4 us
    ppermute x10, starting transfers between devices, along_z(): return lax.ppermute(x, 'ctx', pairs)  13.4 us
    ppermute x10, waiting for transfers between devices, along_z(): return lax.ppermute(x, 'ctx', pairs)  13.4 us
    pallas_call x1, Pallas kernels, prompt_pass(): pl.pallas_call(functools.partial(prompt_kernel, scaling, inner), out_shap...  8.45 us
    all_to_all x1, starting transfers between devices, per_device(): lax.all_to_all(shares.reshape(count, -1, width), ('ctx', 'comp'), 0, 0, t...  8.44 us
    ppermute x5, starting transfers between devices, along_y(): return lax.ppermute(x, ('ctx', 'comp'), pairs)  7.29 us
    unnamed x20, local copies, waits for them, and re-layouts  4.96 us
  transfers between devices with their start and end apart: 21, of which 10 were waited for; matrix products, arithmetic and copies ran while one was open for 0% of the time, Pallas kernels for 9%

profile of v5, /device:TPU:4, one launch (start us, length us, event | category | flops | bytes accessed | tf_op | source)
XLA Modules:
  0.0 120.6 jit_solution(4435431009845240186)
XLA Ops:
  0.6 4.1 %collective-permute-start.3 = (bf16[512,256]{1,0:T(8,128)(2,1)}, bf16[512,256]{1,0:T(8,128)(2,1)S(1)}, u32[]{:S(2)}, u32[]{:S(2)}) collective-permute-start(bf16[512,256]{1,0:T(8,128)(2,1)} %bitcast.13), channel_id=1, source_target_pairs={{0,48},{16,0},{32,16},{48,32},{64,112},{80,64},{96,80},{112,96},{1... | collective-permute-start | bytes 786440 | tf_op jit(solution)/shard_map/gather_keys/ppermute | solution.py:401
  4.7 1.6 %collective-permute-start.1 = (bf16[512,256]{1,0:T(8,128)(2,1)}, bf16[512,256]{1,0:T(8,128)(2,1)S(1)}, u32[]{:S(2)}, u32[]{:S(2)}) collective-permute-start(bf16[512,256]{1,0:T(8,128)(2,1)} %bitcast.14), channel_id=1, source_target_pairs={{0,64},{2,66},{4,68},{6,70},{8,72},{10,74},{12,76},{14,78},{16,80}... | collective-permute-start | bytes 786440 | tf_op jit(solution)/shard_map/gather_keys/ppermute | solution.py:414
  6.3 4.3 %collective-permute-done.3.refs_6_.refs_4_ = bf16[512,256]{1,0:T(8,128)(2,1)S(1)} collective-permute-done((bf16[512,256]{1,0:T(8,128)(2,1)}, bf16[512,256]{1,0:T(8,128)(2,1)S(1)}, u32[]{:S(2)}, u32[]{:S(2)}) %collective-permute-start.3) | collective-permute-done | bytes 262176 | tf_op jit(solution)/shard_map/gather_keys/ppermute | solution.py:401
  10.6 3.4 %collective-permute-done.1.after_ref.refs_2_.refs_7_.refs_5_ = bf16[512,256]{1,0:T(8,128)(2,1)S(1)} collective-permute-done((bf16[512,256]{1,0:T(8,128)(2,1)}, bf16[512,256]{1,0:T(8,128)(2,1)S(1)}, u32[]{:S(2)}, u32[]{:S(2)}) %collective-permute-start.1) | collective-permute-done | bytes 262176 | tf_op jit(solution)/shard_map/gather_keys/ppermute | solution.py:414
  14.5 0.7 collective-permute-done.refs_3_.refs_1_
  15.3 1.0 collective-permute-start.2
  16.2 1.7 %collective-permute-start.8 = (bf16[512,256]{1,0:T(8,128)(2,1)S(1)}, bf16[512,256]{1,0:T(8,128)(2,1)S(1)}, u32[]{:S(2)}, u32[]{:S(2)}) collective-permute-start(bf16[512,256]{1,0:T(8,128)(2,1)S(1)} %collective-permute-done.3.refs_6_.refs_4_), channel_id=1, source_target_pairs={{0,72},{2,74},{4,76},{6,78},{8,64},{10,66},{12,68},{14,70},{16,88}... | collective-permute-start | bytes 786440 | tf_op jit(solution)/shard_map/gather_keys/ppermute | solution.py:414
  18.3 0.8 collective-permute-done.4.refs_1_.refs_5_.refs_3_
  19.1 2.1 %collective-permute-start.7 = (bf16[256,256]{1,0:T(8,128)(2,1)S(1)}, bf16[256,256]{1,0:T(8,128)(2,1)S(1)}, u32[]{:S(2)}, u32[]{:S(2)}) collective-permute-start(bf16[256,256]{1,0:T(8,128)(2,1)S(1)} %collective-permute-done.4.refs_1_.refs_5_.refs_3_), channel_id=1, source_target_pairs={{0,72},{2,74},{4,76},{6,78},{8,64},{10,66},{12,68},{14,70},{16,88}... | collective-permute-start | bytes 393224 | tf_op jit(solution)/shard_map/gather_keys/ppermute | solution.py:414
  21.5 1.6 %collective-permute-start.6 = (bf16[256,256]{1,0:T(8,128)(2,1)S(1)}, bf16[256,256]{1,0:T(8,128)(2,1)S(1)}, u32[]{:S(2)}, u32[]{:S(2)}) collective-permute-start(bf16[256,256]{1,0:T(8,128)(2,1)S(1)} %collective-permute-done.2.refs_0_.refs_4_.refs_2_), channel_id=1, source_target_pairs={{0,64},{2,66},{4,68},{6,70},{8,72},{10,74},{12,76},{14,78},{16,80}... | collective-permute-start | bytes 393224 | tf_op jit(solution)/shard_map/gather_keys/ppermute | solution.py:414
  23.2 1.0 copy-done.1
  24.2 0.9 copy-done.2
  25.1 0.9 copy-done.3
  26.1 0.7 copy-done.6
  26.8 0.7 copy-done.8
  27.4 1.8 %order_rows.1 = (bf16[1024,1280]{1,0:T(8,128)(2,1)S(1)}, bf16[128,1280]{1,0:T(8,128)(2,1)S(1)}, bf16[128,1280]{1,0:T(8,128)(2,1)S(1)}, bf16[1024,256]{1,0:T(8,128)(2,1)S(1)}) custom-call(s32[2]{0:T(128)S(1)} %pad_add_fusion.scalars_ref, s32[4]{0:T(128)S(1)} %bitcast.21, s32[4]{0:T(128)S(1)} %bitcast.23, bf16[1024,128]{1,0:T(8,128)(2,1)S(1)} %copy-done.2, ...), custom_call_target="tpu_custom_call" | custom-call | flops 671088640 | bytes 10485760 | tf_op jit(solution)/shard_map/order_rows/order_rows/pallas_call | solution.py:196
  29.5 0.7 copy-done
  30.3 3.3 %collective-permute-done.9.refs_0_ = bf16[1536,256]{1,0:T(8,128)(2,1)S(1)} collective-permute-done((bf16[1536,256]{1,0:T(8,128)(2,1)S(1)}, bf16[1536,256]{1,0:T(8,128)(2,1)S(1)}, u32[]{:S(2)}, u32[]{:S(2)}) %collective-permute-start.9) | collective-permute-done | bytes 786464 | tf_op jit(solution)/shard_map/gather_keys/ppermute | solution.py:397
  33.6 24.4 %reply_pass.1 = (bf16[1024,128]{1,0:T(8,128)(2,1)}, bf16[1024,128]{1,0:T(8,128)(2,1)}, bf16[4096,256]{1,0:T(8,128)(2,1)S(1)}, bf16[4096,256]{1,0:T(8,128)(2,1)S(...) custom-call(s32[2]{0:T(128)S(1)} %pad_add_fusion.scalars_ref, ...), custom_call_target="tpu_custom_call" | custom-call | flops 12884901888 | bytes 8388608 | tf_op jit(solution)/shard_map/reply_rows/reply_pass/pallas_call | solution.py:311
  58.1 3.2 %collective-permute-start.13 = (bf16[256,256]{1,0:T(8,128)(2,1)S(1)}, bf16[256,256]{1,0:T(8,128)(2,1)S(1)}, u32[]{:S(2)}, u32[]{:S(2)}) collective-permute-start(bf16[256,256]{1,0:T(8,128)(2,1)S(1)} %get-tuple-element.34), channel_id=1, source_target_pairs={{0,32},{16,48},{32,0},{48,16},{64,96},{80,112},{96,64},{112,80},{1... | collective-permute-start | bytes 393224 | tf_op jit(solution)/shard_map/prompt_cache_sum/ppermute | solution.py:401
  61.3 8.4 %prompt_pass.1 = (bf16[512,128]{1,0:T(8,128)(2,1)}, bf16[512,128]{1,0:T(8,128)(2,1)}, bf16[4096,256]{1,0:T(8,128)(2,1)S(1)}) custom-call(s32[1]{0:T(128)} %bitcast.place_ref, bf16[512,128]{1,0:T(8,128)(2,1)S(1)} %bitcast.19, bf16[512,128]{1,0:T(8,128)(2,1)S(1)} %bitcast.20, bf16[512,256]{1,0:T(8,128)(2,1)S(1)} %bitcast.18, ...), custom_call_target="tpu_custom_call" | custom-call | flops 6442450944 | bytes 4194304 | tf_op jit(solution)/shard_map/prompt_rows/prompt_pass/pallas_call | solution.py:132
  69.8 1.8 %join_sums.1 = (bf16[4096,256]{1,0:T(8,128)(2,1)}, bf16[256,256]{1,0:T(8,128)(2,1)S(1)}) custom-call(bf16[4096,256]{1,0:T(8,128)(2,1)S(1)} %get-tuple-element.30.total_ref, bf16[4096,256]{1,0:T(8,128)(2,1)S(1)} %collective-permute-done.11.arrived_ref, bf16[256,256]{1,0:T(8,128)(2,1)S(1)} %get-tuple-element.32.refs_0_, ...), custom_call_target="tpu_custom_call" | custom-call | tf_op jit(solution)/shard_map/prompt_cache_sum/join_sums/pallas_call | solution.py:368
  71.6 8.4 %all-to-all-start = ((bf16[64,64,256]{2,1,0:T(8,128)(2,1)}), bf16[64,64,256]{2,1,0:T(8,128)(2,1)S(1)}, u32[]{:S(2)}, u32[]{:S(2)}) async-start(bf16[64,64,256]{2,1,0:T(8,128)(2,1)} %bitcast.9), calls=%async_computation | async-start | bytes 4194304 | tf_op jit(solution)/shard_map/prompt_cache_sum/all_to_all | solution.py:448
  80.1 1.7 %collective-permute-start.16 = (bf16[256,256]{1,0:T(8,128)(2,1)S(1)}, bf16[256,256]{1,0:T(8,128)(2,1)S(1)}, u32[]{:S(2)}, u32[]{:S(2)}) collective-permute-start(bf16[256,256]{1,0:T(8,128)(2,1)S(1)} %get-tuple-element.39), channel_id=1, source_target_pairs={{0,64},{16,80},{32,96},{48,112},{64,0},{80,16},{96,32},{112,48},{1... | collective-permute-start | bytes 393224 | tf_op jit(solution)/shard_map/reply_cache_sum/ppermute | solution.py:404
  81.7 25.2 %collective-permute-done.16 = bf16[256,256]{1,0:T(8,128)(2,1)S(1)} collective-permute-done((bf16[256,256]{1,0:T(8,128)(2,1)S(1)}, bf16[256,256]{1,0:T(8,128)(2,1)S(1)}, u32[]{:S(2)}, u32[]{:S(2)}) %collective-permute-start.16) | collective-permute-done | bytes 131104 | tf_op jit(solution)/shard_map/reply_cache_sum/ppermute | solution.py:404
  107.0 3.1 %collective-permute-start.19 = (bf16[256,256]{1,0:T(8,128)(2,1)S(1)}, bf16[256,256]{1,0:T(8,128)(2,1)S(1)}, u32[]{:S(2)}, u32[]{:S(2)}) collective-permute-start(bf16[256,256]{1,0:T(8,128)(2,1)S(1)} %add_convert_fusion.refs_0_), channel_id=1, source_target_pairs={{0,48},{16,0},{32,16},{48,32},{64,112},{80,64},{96,80},{112,96},{1... | collective-permute-start | bytes 393224 | tf_op jit(solution)/shard_map/reply_cache_sum/ppermute | solution.py:401
  110.4 1.1 collective-permute-start.17
  112.0 3.8 %collective-permute-done.19.refs_3_ = bf16[256,256]{1,0:T(8,128)(2,1)S(1)} collective-permute-done((bf16[256,256]{1,0:T(8,128)(2,1)S(1)}, bf16[256,256]{1,0:T(8,128)(2,1)S(1)}, u32[]{:S(2)}, u32[]{:S(2)}) %collective-permute-start.19) | collective-permute-done | bytes 131104 | tf_op jit(solution)/shard_map/reply_cache_sum/ppermute | solution.py:401
  115.8 2.3 %collective-permute-done.18.refs_2_ = bf16[256,256]{1,0:T(8,128)(2,1)S(1)} collective-permute-done((bf16[256,256]{1,0:T(8,128)(2,1)S(1)}, bf16[256,256]{1,0:T(8,128)(2,1)S(1)}, u32[]{:S(2)}, u32[]{:S(2)}) %collective-permute-start.18) | collective-permute-done | bytes 131104 | tf_op jit(solution)/shard_map/reply_cache_sum/ppermute | solution.py:401
  118.0 1.2 collective-permute-done.17.refs_1_
  119.2 0.8 placed_in_order.1
  120.0 0.6 maximum_select_fusion
  (46 shorter events, 2.4 us)
Async XLA Ops:
  0.6 10.0 %collective-permute-start.3 = (bf16[512,256]{1,0:T(8,128)(2,1)}, bf16[512,256]{1,0:T(8,128)(2,1)S(1)}, u32[]{:S(2)}, u32[]{:S(2)}) collective-permute-start(bf16[512,256]{1,0:T(8,128)(2,1)} %bitcast.13), channel_id=1, source_target_pairs={{0,48},{16,0},{32,16},{48,32},{64,112},{80,64},{96,80},{112,96},{1... | collective-permute-start | bytes 786440 | tf_op jit(solution)/shard_map/gather_keys/ppermute | solution.py:401
  4.7 9.3 %collective-permute-start.1 = (bf16[512,256]{1,0:T(8,128)(2,1)}, bf16[512,256]{1,0:T(8,128)(2,1)S(1)}, u32[]{:S(2)}, u32[]{:S(2)}) collective-permute-start(bf16[512,256]{1,0:T(8,128)(2,1)} %bitcast.14), channel_id=1, source_target_pairs={{0,64},{2,66},{4,68},{6,70},{8,72},{10,74},{12,76},{14,78},{16,80}... | collective-permute-start | bytes 786440 | tf_op jit(solution)/shard_map/gather_keys/ppermute | solution.py:414
  6.3 8.9 %collective-permute-start = (bf16[512,256]{1,0:T(8,128)(2,1)}, bf16[512,256]{1,0:T(8,128)(2,1)S(1)}, u32[]{:S(2)}, u32[]{:S(2)}) collective-permute-start(bf16[512,256]{1,0:T(8,128)(2,1)} %bitcast.15), channel_id=1, source_target_pairs={{0,16},{16,32},{32,48},{48,0},{64,80},{80,96},{96,112},{112,64},{1... | collective-permute-start | bytes 786440 | tf_op jit(solution)/shard_map/gather_keys/ppermute | solution.py:401
  14.0 5.0 %collective-permute-start.4 = (bf16[256,256]{1,0:T(8,128)(2,1)S(1)}, bf16[256,256]{1,0:T(8,128)(2,1)S(1)}, u32[]{:S(2)}, u32[]{:S(2)}) collective-permute-start(bf16[256,256]{1,0:T(8,128)(2,1)S(1)} %stack_after.4), channel_id=1, source_target_pairs={{0,48},{16,0},{32,16},{48,32},{64,112},{80,64},{96,80},{112,96},{1... | collective-permute-start | bytes 393224 | tf_op jit(solution)/shard_map/gather_keys/ppermute | solution.py:401
  15.3 6.2 %collective-permute-start.2 = (bf16[256,256]{1,0:T(8,128)(2,1)S(1)}, bf16[256,256]{1,0:T(8,128)(2,1)S(1)}, u32[]{:S(2)}, u32[]{:S(2)}) collective-permute-start(bf16[256,256]{1,0:T(8,128)(2,1)S(1)} %stack_after.3), channel_id=1, source_target_pairs={{0,16},{16,32},{32,48},{48,0},{64,80},{80,96},{96,112},{112,64},{1... | collective-permute-start | bytes 393224 | tf_op jit(solution)/shard_map/gather_keys/ppermute | solution.py:401
  16.2 13.0 %collective-permute-start.8 = (bf16[512,256]{1,0:T(8,128)(2,1)S(1)}, bf16[512,256]{1,0:T(8,128)(2,1)S(1)}, u32[]{:S(2)}, u32[]{:S(2)}) collective-permute-start(bf16[512,256]{1,0:T(8,128)(2,1)S(1)} %collective-permute-done.3.refs_6_.refs_4_), channel_id=1, source_target_pairs={{0,72},{2,74},{4,76},{6,78},{8,64},{10,66},{12,68},{14,70},{16,88}... | collective-permute-start | bytes 786440 | tf_op jit(solution)/shard_map/gather_keys/ppermute | solution.py:414
  17.9 11.3 %collective-permute-start.5 = (bf16[512,256]{1,0:T(8,128)(2,1)S(1)}, bf16[512,256]{1,0:T(8,128)(2,1)S(1)}, u32[]{:S(2)}, u32[]{:S(2)}) collective-permute-start(bf16[512,256]{1,0:T(8,128)(2,1)S(1)} %collective-permute-done.refs_3_.refs_1_), channel_id=1, source_target_pairs={{0,64},{2,66},{4,68},{6,70},{8,72},{10,74},{12,76},{14,78},{16,80}... | collective-permute-start | bytes 786440 | tf_op jit(solution)/shard_map/gather_keys/ppermute | solution.py:414
  19.1 10.2 %collective-permute-start.7 = (bf16[256,256]{1,0:T(8,128)(2,1)S(1)}, bf16[256,256]{1,0:T(8,128)(2,1)S(1)}, u32[]{:S(2)}, u32[]{:S(2)}) collective-permute-start(bf16[256,256]{1,0:T(8,128)(2,1)S(1)} %collective-permute-done.4.refs_1_.refs_5_.refs_3_), channel_id=1, source_target_pairs={{0,72},{2,74},{4,76},{6,78},{8,64},{10,66},{12,68},{14,70},{16,88}... | collective-permute-start | bytes 393224 | tf_op jit(solution)/shard_map/gather_keys/ppermute | solution.py:414
  21.5 7.7 %collective-permute-start.6 = (bf16[256,256]{1,0:T(8,128)(2,1)S(1)}, bf16[256,256]{1,0:T(8,128)(2,1)S(1)}, u32[]{:S(2)}, u32[]{:S(2)}) collective-permute-start(bf16[256,256]{1,0:T(8,128)(2,1)S(1)} %collective-permute-done.2.refs_0_.refs_4_.refs_2_), channel_id=1, source_target_pairs={{0,64},{2,66},{4,68},{6,70},{8,72},{10,74},{12,76},{14,78},{16,80}... | collective-permute-start | bytes 393224 | tf_op jit(solution)/shard_map/gather_keys/ppermute | solution.py:414
  23.2 1.0 copy-start.1
  24.2 0.9 copy-start.2
  25.1 0.9 copy-start.3
  26.1 0.7 copy-start.6
  26.8 0.7 copy-start.8
  29.2 1.0 copy-start
  29.3 4.4 %copy-start.7 = (s32[1,4]{1,0:T(1,128)S(1)}, s32[1,4]{1,0:T(1,128)}, u32[]{:S(2)}) copy-start(s32[1,4]{1,0:T(1,128)} %param.14) | copy-start | bytes 52
  29.3 4.4 %copy-start.9 = (s32[1,4]{1,0:T(1,128)S(1)}, s32[1,4]{1,0:T(1,128)}, u32[]{:S(2)}) copy-start(s32[1,4]{1,0:T(1,128)} %param.15) | copy-start | bytes 52
  29.4 4.2 %collective-permute-start.10 = (bf16[2560,256]{1,0:T(8,128)(2,1)S(1)}, bf16[2560,256]{1,0:T(8,128)(2,1)S(1)}, u32[]{:S(2)}, u32[]{:S(2)}) collective-permute-start(bf16[2560,256]{1,0:T(8,128)(2,1)S(1)} %stack_after.5), channel_id=1, source_target_pairs={{0,1},{1,0},{2,3},{3,2},{4,5},{5,4},{6,7},{7,6},{8,9},{9,8},{10,11... | collective-permute-start | bytes 3932168 | tf_op jit(solution)/shard_map/gather_keys/ppermute | solution.py:397
  30.2 3.4 %collective-permute-start.9 = (bf16[1536,256]{1,0:T(8,128)(2,1)S(1)}, bf16[1536,256]{1,0:T(8,128)(2,1)S(1)}, u32[]{:S(2)}, u32[]{:S(2)}) collective-permute-start(bf16[1536,256]{1,0:T(8,128)(2,1)S(1)} %pad_maximum_fusion), channel_id=1, source_target_pairs={{0,1},{1,0},{2,3},{3,2},{4,5},{5,4},{6,7},{7,6},{8,9},{9,8},{10,11... | collective-permute-start | bytes 2359304 | tf_op jit(solution)/shard_map/gather_keys/ppermute | solution.py:397
  33.6 27.7 %copy-start.4 = (bf16[1,512,128]{2,1,0:T(8,128)(2,1)S(1)}, bf16[1,512,128]{2,1,0:T(8,128)(2,1)}, u32[]{:S(2)}) copy-start(bf16[1,512,128]{2,1,0:T(8,128)(2,1)} %param.8) | copy-start | bytes 393220
  33.6 27.7 %copy-start.5 = (bf16[1,512,128]{2,1,0:T(8,128)(2,1)S(1)}, bf16[1,512,128]{2,1,0:T(8,128)(2,1)}, u32[]{:S(2)}) copy-start(bf16[1,512,128]{2,1,0:T(8,128)(2,1)} %param.10) | copy-start | bytes 393220
  58.1 11.7 %collective-permute-start.11 = (bf16[4096,256]{1,0:T(8,128)(2,1)S(1)}, bf16[4096,256]{1,0:T(8,128)(2,1)S(1)}, u32[]{:S(2)}, u32[]{:S(2)}) collective-permute-start(bf16[4096,256]{1,0:T(8,128)(2,1)S(1)} %get-tuple-element.31), channel_id=1, source_target_pairs={{0,1},{1,0},{2,3},{3,2},{4,5},{5,4},{6,7},{7,6},{8,9},{9,8},{10,11... | collective-permute-start | bytes 6291464 | tf_op jit(solution)/shard_map/ppermute | solution.py:397
  58.1 11.7 %collective-permute-start.12 = (bf16[256,256]{1,0:T(8,128)(2,1)S(1)}, bf16[256,256]{1,0:T(8,128)(2,1)S(1)}, u32[]{:S(2)}, u32[]{:S(2)}) collective-permute-start(bf16[256,256]{1,0:T(8,128)(2,1)S(1)} %get-tuple-element.33), channel_id=1, source_target_pairs={{0,16},{16,32},{32,48},{48,0},{64,80},{80,96},{96,112},{112,64},{1... | collective-permute-start | bytes 393224 | tf_op jit(solution)/shard_map/prompt_cache_sum/ppermute | solution.py:401
  58.1 11.7 %collective-permute-start.13 = (bf16[256,256]{1,0:T(8,128)(2,1)S(1)}, bf16[256,256]{1,0:T(8,128)(2,1)S(1)}, u32[]{:S(2)}, u32[]{:S(2)}) collective-permute-start(bf16[256,256]{1,0:T(8,128)(2,1)S(1)} %get-tuple-element.34), channel_id=1, source_target_pairs={{0,32},{16,48},{32,0},{48,16},{64,96},{80,112},{96,64},{112,80},{1... | collective-permute-start | bytes 393224 | tf_op jit(solution)/shard_map/prompt_cache_sum/ppermute | solution.py:401
  61.3 8.5 %collective-permute-start.14 = (bf16[256,256]{1,0:T(8,128)(2,1)S(1)}, bf16[256,256]{1,0:T(8,128)(2,1)S(1)}, u32[]{:S(2)}, u32[]{:S(2)}) collective-permute-start(bf16[256,256]{1,0:T(8,128)(2,1)S(1)} %get-tuple-element.35), channel_id=1, source_target_pairs={{0,48},{16,0},{32,16},{48,32},{64,112},{80,64},{96,80},{112,96},{1... | collective-permute-start | bytes 393224 | tf_op jit(solution)/shard_map/prompt_cache_sum/ppermute | solution.py:401
  71.6 39.9 %all-to-all-start = ((bf16[64,64,256]{2,1,0:T(8,128)(2,1)}), bf16[64,64,256]{2,1,0:T(8,128)(2,1)S(1)}, u32[]{:S(2)}, u32[]{:S(2)}) async-start(bf16[64,64,256]{2,1,0:T(8,128)(2,1)} %bitcast.9), calls=%async_computation | async-start | bytes 4194304 | tf_op jit(solution)/shard_map/prompt_cache_sum/all_to_all | solution.py:448
  80.1 26.8 %collective-permute-start.16 = (bf16[256,256]{1,0:T(8,128)(2,1)S(1)}, bf16[256,256]{1,0:T(8,128)(2,1)S(1)}, u32[]{:S(2)}, u32[]{:S(2)}) collective-permute-start(bf16[256,256]{1,0:T(8,128)(2,1)S(1)} %get-tuple-element.39), channel_id=1, source_target_pairs={{0,64},{16,80},{32,96},{48,112},{64,0},{80,16},{96,32},{112,48},{1... | collective-permute-start | bytes 393224 | tf_op jit(solution)/shard_map/reply_cache_sum/ppermute | solution.py:404
  107.0 8.8 %collective-permute-start.19 = (bf16[256,256]{1,0:T(8,128)(2,1)S(1)}, bf16[256,256]{1,0:T(8,128)(2,1)S(1)}, u32[]{:S(2)}, u32[]{:S(2)}) collective-permute-start(bf16[256,256]{1,0:T(8,128)(2,1)S(1)} %add_convert_fusion.refs_0_), channel_id=1, source_target_pairs={{0,48},{16,0},{32,16},{48,32},{64,112},{80,64},{96,80},{112,96},{1... | collective-permute-start | bytes 393224 | tf_op jit(solution)/shard_map/reply_cache_sum/ppermute | solution.py:401
  110.1 7.9 %collective-permute-start.18 = (bf16[256,256]{1,0:T(8,128)(2,1)S(1)}, bf16[256,256]{1,0:T(8,128)(2,1)S(1)}, u32[]{:S(2)}, u32[]{:S(2)}) collective-permute-start(bf16[256,256]{1,0:T(8,128)(2,1)S(1)} %add_convert_fusion.refs_0_), channel_id=1, source_target_pairs={{0,32},{16,48},{32,0},{48,16},{64,96},{80,112},{96,64},{112,80},{1... | collective-permute-start | bytes 393224 | tf_op jit(solution)/shard_map/reply_cache_sum/ppermute | solution.py:401
  110.4 8.7 %collective-permute-start.17 = (bf16[256,256]{1,0:T(8,128)(2,1)S(1)}, bf16[256,256]{1,0:T(8,128)(2,1)S(1)}, u32[]{:S(2)}, u32[]{:S(2)}) collective-permute-start(bf16[256,256]{1,0:T(8,128)(2,1)S(1)} %add_convert_fusion.refs_0_), channel_id=1, source_target_pairs={{0,16},{16,32},{32,48},{48,0},{64,80},{80,96},{96,112},{112,64},{1... | collective-permute-start | bytes 393224 | tf_op jit(solution)/shard_map/reply_cache_sum/ppermute | solution.py:401
  111.9 8.1 %collective-permute-start.15 = (bf16[32,256]{1,0:T(8,128)(2,1)S(1)}, bf16[32,256]{1,0:T(8,128)(2,1)S(1)}, u32[]{:S(2)}, u32[]{:S(2)}) collective-permute-start(bf16[32,256]{1,0:T(8,128)(2,1)S(1)} %get-tuple-element.41), channel_id=1, source_target_pairs={{0,1},{1,0},{2,3},{3,2},{4,5},{5,4},{6,7},{7,6},{8,9},{9,8},{10,11... | collective-permute-start | bytes 49160 | tf_op jit(solution)/shard_map/prompt_cache_halves/ppermute | solution.py:397
